TPU v7x, 768 devices: a whole 4x8x12 slice. The times are simulated.
768 devices in a mesh: dp: 48 (over z, x_hi, core), aug: 16 (over x_lo, y).
Axes of the slice: x: 4 (x_hi: 2, x_lo: 2; x = x_hi * 2 + x_lo), y: 8, z: 12, core: 2. Of those that a mesh axis runs over, the one named last changes fastest.
Arguments:
- acts: bfloat16 [48, 16, 1664, 128], P('dp', 'aug'), may hold values from -6 to 6
- out_grads: bfloat16 [48, 16, 16, 312, 128], P('dp', 'aug'), may hold values from -60 to 60
- aug_count: int32 [48], P('dp'), may hold values from 4 to 16
- noise: float32 [4992, 1664], P('dp', 'aug'), may hold values from -6 to 6
- first_moment: float32 [4992, 1664], P('dp', 'aug'), may hold values from -6 to 6
- second_moment: float32 [4992, 1664], P('dp', 'aug'), may hold values from 0.1 to 4
Outputs:
- noisy_grad: float32 [4992, 1664], P('dp', 'aug')
- new_first: float32 [4992, 1664], P('dp', 'aug')
- new_second: float32 [4992, 1664], P('dp', 'aug')
All inputs are finite; a program needn't handle non-finite values.
Results may differ from a plain program's by a relative error of at most 0.0003.
Values may be sent and summed in bfloat16 or wider, within the bound.
No kernel may reach another device: no remote copies, remote signals or barrier semaphores. Data moves between devices by JAX's collectives and lax.ppermute only.
A program may use at most 32 MiB of HBM per device.

v0:
```python
import math

import jax
import jax.numpy as jnp
from jax import lax
from jax.sharding import PartitionSpec as P


def body(acts, out_grads, aug_count, noise, first_moment, second_moment):
    augs = lax.axis_size("aug")
    images = lax.axis_size("dp")
    width = acts.shape[2]
    tokens = acts.shape[3]
    heads_dev = out_grads.shape[2] // augs
    head_size = out_grads.shape[3] // 3
    clip = jnp.float32(0.5 * width * math.sqrt(3.0 * tokens / augs))
    sigma = jnp.float32(0.2 * math.sqrt(images) / width)
    count = aug_count[0]
    received = lax.all_to_all(out_grads, "aug", split_axis=2, concat_axis=1, tiled=True)
    live = (jnp.arange(augs) < count).astype(jnp.bfloat16)
    masked = received[0] * live[:, None, None, None]
    masked = masked.reshape(augs, heads_dev, 3, head_size, tokens)
    gathered = lax.all_gather(acts, "aug", axis=1, tiled=True)
    summed = jnp.einsum("aft,ahjet->jfhe", gathered[0], masked, preferred_element_type=jnp.float32)
    summed = summed / count.astype(jnp.float32)
    squares = lax.psum(jnp.sum(summed * summed), "aug")
    norm = jnp.sqrt(squares + 1e-06)
    factor = jnp.minimum(jnp.float32(1.0), clip / norm)
    scaled = (factor * summed).reshape(3 * width, heads_dev * head_size)
    total = lax.psum_scatter(scaled, "dp", scatter_dimension=0, tiled=True)
    noisy_grad = (total + sigma * clip * noise) / jnp.float32(images)
    new_first = 0.9 * first_moment + 0.1 * noisy_grad
    new_second = 0.999 * second_moment + 0.001 * noisy_grad * noisy_grad
    return (noisy_grad, new_first, new_second)


def solution(mesh):
    return jax.shard_map(
        body,
        mesh=mesh,
        in_specs=(
            P("dp", "aug", None, None),
            P("dp", "aug", None, None, None),
            P("dp"),
            P("dp", "aug"),
            P("dp", "aug"),
            P("dp", "aug"),
        ),
        out_specs=(P("dp", "aug"), P("dp", "aug"), P("dp", "aug")),
        check_vma=False,
    )
```

profile of v0, /device:TPU:16, one launch (start us, length us, event | category | flops | bytes accessed | tf_op | source)
XLA Modules:
  0.0 349.5 jit_solution(15825676788356823008)
XLA Ops:
  7.2 0.0 all-gather.2.cloned.1.call-start
  7.2 0.7 all-gather.2.cloned.1.call-update
  7.9 12.9 %all-to-all-start = ((bf16[1,1,16,312,128]{4,3,1,0,2:T(8,128)(2,1)}), bf16[1,1,16,312,128]{4,3,1,0,2:T(8,128)(2,1)S(1)}, u32[]{:S(2)}, u32[]{:S(2)}) async-start(bf16[1,1,16,312,128]{4,3,1,0,2:T(8,128)(2,1)} %bitcast.30), calls=%async_computation | async-start | bytes 2555904 | tf_op jit(solution)/shard_map/all_to_all | solution.py:19
  20.8 0.0 reduce-scatter.4.cloned.1.call-start
  21.5 32.2 %all-to-all-done = bf16[1,1,16,312,128]{4,3,1,0,2:T(8,128)(2,1)S(1)} async-done(((bf16[1,1,16,312,128]{4,3,1,0,2:T(8,128)(2,1)}), bf16[1,1,16,312,128]{4,3,1,0,2:T(8,128)(2,1)S(1)}, u32[]{:S(2)}, u32[]{:S(2)}) %all-to-all-start) | async-done | bytes 1277984 | tf_op jit(solution)/shard_map/all_to_all | solution.py:19
  53.6 0.1 broadcast_multiply_fusion
  53.8 61.7 %all-gather.2.cloned.1.call-done = bf16[1,16,1664,128]{3,2,0,1:T(8,128)(2,1)} async-done(((bf16[1,1,1664,128]{3,2,0,1:T(8,128)(2,1)}), bf16[1,16,1664,128]{3,2,0,1:T(8,128)(2,1)}) %all-gather.2.cloned.1.call-update) | async-done | bytes 6815760 | tf_op jit(solution)/shard_map/all_gather | solution.py:23
  115.4 7.4 %multiply_reduce_fusion = (f32[]{:T(128)}, f32[3,104,1664]{2,1,0:T(8,128)}) fusion(f32[]{:T(128)S(6)} %convert_element_type.11, bf16[16,3,104,128]{3,2,1,0:T(8,128)(2,1)S(1)} %bitcast.31, bf16[1,16,1664,128]{3,2,0,1:T(8,128)(2,1)} %all-gather.2.cloned.1.call-done), kind=kOutput, calls=%fused_computation.5 | convolution fusion | flops 2128069632 | bytes 10170376 | tf_op jit(solution)/shard_map/aft,ahjet->jfhe/dot_general | solution.py:24
  122.9 31.8 %psum.7 = f32[]{:T(128)} all-reduce(f32[]{:T(128)} %get-tuple-element.6), channel_id=1, replica_groups=mesh['dp'=48,'aug'=16] {'aug'}, use_global_device_ids=true, to_apply=%region_1.0 | all-reduce | flops 1 | bytes 8 | tf_op jit(solution)/shard_map/psum | solution.py:26
  155.4 1.7 multiply_bitcast_fusion
  157.1 2.1 copy.14
  159.3 0.0 copy-start
  159.3 0.0 copy-start.1
  159.3 0.0 copy-start.2
  159.3 0.0 reduce-scatter.4.cloned.1.call-update
  159.3 181.9 %reduce-scatter.4.cloned.1.call-done = f32[104,104]{1,0:T(8,128)} async-done(((f32[4992,104]{1,0:T(8,128)}), f32[104,104]{1,0:T(8,128)}) %reduce-scatter.4.cloned.1.call-update) | async-done | bytes 43280
  341.2 0.0 copy-done
  341.2 0.0 copy-done.1
  341.2 0.0 copy-done.2
  341.2 1.5 multiply_add_fusion
  (1 shorter events, 0.0 us)
Async XLA Ops:
  7.2 108.3 %all-gather.2.cloned.1.call-start = ((), (), s32[]{:S(2)}) async-start(), calls=%async_computation.2 | async-start | bytes 7241728 | tf_op jit(solution)/shard_map/all_gather | solution.py:23
  7.9 45.7 %all-to-all-start = ((bf16[1,1,16,312,128]{4,3,1,0,2:T(8,128)(2,1)}), bf16[1,1,16,312,128]{4,3,1,0,2:T(8,128)(2,1)S(1)}, u32[]{:S(2)}, u32[]{:S(2)}) async-start(bf16[1,1,16,312,128]{4,3,1,0,2:T(8,128)(2,1)} %bitcast.30), calls=%async_computation | async-start | bytes 2555904 | tf_op jit(solution)/shard_map/all_to_all | solution.py:19
  20.8 320.5 %reduce-scatter.4.cloned.1.call-start = ((), (), s32[]{:S(2)}) async-start(), calls=%async_computation.3 | async-start | bytes 2609152
  159.3 182.0 %copy-start = (f32[104,104]{1,0:T(8,128)S(1)}, f32[104,104]{1,0:T(8,128)}, u32[]{:S(2)}) copy-start(f32[104,104]{1,0:T(8,128)} %param.11) | copy-start | bytes 129796
  159.3 182.0 %copy-start.1 = (f32[104,104]{1,0:T(8,128)S(1)}, f32[104,104]{1,0:T(8,128)}, u32[]{:S(2)}) copy-start(f32[104,104]{1,0:T(8,128)} %param.9) | copy-start | bytes 129796
  159.3 182.0 %copy-start.2 = (f32[104,104]{1,0:T(8,128)S(1)}, f32[104,104]{1,0:T(8,128)}, u32[]{:S(2)}) copy-start(f32[104,104]{1,0:T(8,128)} %param.10) | copy-start | bytes 129796
Sparse Core Ops, SparseCore 0:
  10.4 105.0 all-gather.1
  159.4 181.7 reduce-scatter.3
where the time goes:
time: 350 us
  waiting for transfers between devices  276 us (79%)
  blocking collectives  31.8 us (9%)
  between operations  15.4 us (4%)
  starting transfers between devices  12.9 us (4%)
  matrix products  7.42 us (2%)
    unnamed x3, waiting for transfers between devices  183 us
    all_gather x1, waiting for transfers between devices, body(): gathered = lax.all_gather(acts, 'aug', axis=1, tiled=True)  61.7 us
    all_to_all x1, waiting for transfers between devices, body(): lax.all_to_all(out_grads, 'aug', split_axis=2, concat_axis=1, tiled=True)  32.2 us
    psum x1, blocking collectives, body(): squares = lax.psum(jnp.sum(summed * summed), 'aug')  31.8 us
    all_to_all x1, starting transfers between devices, body(): lax.all_to_all(out_grads, 'aug', split_axis=2, concat_axis=1, tiled=True)  12.9 us
    dot_general x1, matrix products, body(): jnp.einsum('aft,ahjet->jfhe', gathered[0], masked, preferred_element_type...  7.42 us
  transfers between devices with their start and end apart: 3, of which 3 were waited for; matrix products, arithmetic and copies ran while one was open for 0% of the time, Pallas kernels for 0%

commit v1 on v0

v1 whole, which is shorter than its diff:
```python
import functools
import math

import jax
import jax.numpy as jnp
from jax import lax
from jax.experimental import pallas as pl
from jax.experimental.pallas import tpu as pltpu
from jax.sharding import Mesh
from jax.sharding import PartitionSpec as P

LANES = 128
TOP = 32767.0
VMEM = 48 * 1024 * 1024


def multiply_kernel(place, x_ref, own_ref, other_ref, keep_ref, send_ref, sum_ref, padded, squares, *, groups, span):
    step = pl.program_id(0)
    part, count = place[0], place[1]
    rings = x_ref.shape[0]
    size = own_ref.shape[2]
    tokens = x_ref.shape[3]

    @pl.when(step == 0)
    def _():
        padded[...] = jnp.zeros_like(padded)
        squares[...] = jnp.zeros_like(squares)
        for y in range(rings):
            for s in range(2):
                aug = jnp.bitwise_xor(part, s) * rings + y
                live = (aug < count).astype(jnp.float32).astype(jnp.bfloat16)
                for j in range(3):
                    for h, ref in enumerate((own_ref, other_ref)):
                        padded[y, j, h * LANES : h * LANES + size, s * tokens : (s + 1) * tokens] = ref[aug, j] * live

    scale = 1.0 / count.astype(jnp.float32)
    rows = x_ref.shape[2]
    blocks = rows // span
    both = jnp.where(part == 0, 1.0, 0.0)
    for j in range(3):
        acc = jnp.zeros((rows, 2 * LANES), jnp.float32)
        for y in range(rings):
            x = jnp.concatenate([x_ref[y, 0], x_ref[y, 1]], axis=1)
            acc += lax.dot_general(x, padded[y, j], (((1,), (1,)), ((), ())), preferred_element_type=jnp.float32)
        acc = (acc * scale).reshape(blocks, span, 2 * LANES)
        whole = acc[:, 8:] * acc[:, 8:]
        first = acc[:, :8] * acc[:, :8] * both
        total = jnp.sum(whole.reshape(blocks * (span // 8 - 1), 8, 2 * LANES), axis=0) + jnp.sum(first, axis=0)
        squares[...] += total[:, :LANES] + total[:, LANES:]

        @pl.when(step < groups)
        def _():
            for h in range(2):
                keep_ref[:, j, h] = acc[:, :, h * LANES : (h + 1) * LANES]

        @pl.when(step >= groups)
        def _():
            for h in range(2):
                send_ref[:, j, h] = acc[:, :, h * LANES : (h + 1) * LANES]

    sum_ref[...] = jnp.broadcast_to(jnp.sum(squares[...], keepdims=True), sum_ref.shape)


def clip_kernel(place, norms_ref, keep_ref, got_ref, out_ref, *, clip):
    part, core = place[0], place[1]
    half = norms_ref.shape[0] // 2
    factors = []
    for c in range(2):
        total = jnp.sum(norms_ref[c * half : (c + 1) * half], axis=0, keepdims=True)
        factors.append(jnp.minimum(1.0, clip / jnp.sqrt(total + 1e-06)))
    mine = jnp.where(core == 0, factors[0], factors[1])
    theirs = jnp.where(core == 0, factors[1], factors[0])
    lane = lax.broadcasted_iota(jnp.int32, keep_ref.shape[3:], 1)
    for j in range(3):
        for h in range(2):
            value = keep_ref[0, j, h] * mine + got_ref[0, j, h] * theirs
            top = jnp.maximum(jnp.max(jnp.abs(value), axis=1, keepdims=True), 1e-30)
            code = jnp.ceil(jnp.log2(top) * 8.0 + 0.05)
            value = jnp.round(value * (jnp.exp2(code * -0.125) * TOP))
            value = jnp.where(lane < 104, value, code)
            out_ref[j, 0, jnp.bitwise_xor(part, h)] = value.astype(jnp.int32).astype(jnp.int16)


def update_kernel(got_ref, noise_ref, first_ref, second_ref, grad_ref, new_first_ref, new_second_ref, *, weight, images):
    sums = []
    for part in range(2):
        total = jnp.zeros(got_ref.shape[2:], jnp.float32)
        for k in range(got_ref.shape[0]):
            value = got_ref[k, part].astype(jnp.int32).astype(jnp.float32)
            scale = jnp.exp2(value[:, 104:105] * 0.125) * (1.0 / TOP)
            total += value * scale
        sums.append(total)
    total = jnp.concatenate([sums[0], sums[1][8:]], axis=0)[:, :104]
    grad = (total + weight * noise_ref[...]) / images
    grad_ref[...] = grad
    new_first_ref[...] = 0.9 * first_ref[...] + 0.1 * grad
    new_second_ref[...] = 0.999 * second_ref[...] + 0.001 * grad * grad


def body(acts, out_grads, aug_count, noise, first_moment, second_moment):
    part, core = lax.axis_index("xl"), lax.axis_index("core")
    rings = lax.axis_size("y")
    augs = 2 * rings
    chips = lax.axis_size("z") * lax.axis_size("xh")
    images = 2 * chips
    width, tokens = acts.shape[2:]
    size = out_grads.shape[3] // 3
    clip = 0.5 * width * math.sqrt(3.0 * tokens / augs)
    sigma = 0.2 * math.sqrt(images) / width
    span = 56
    pairs = width // size // 2
    rows = pairs * 2 * span

    blocks = acts[0, 0].reshape(pairs, 2, size, tokens)

    def half_of(which):
        got = lax.dynamic_slice(blocks, (0, 0, which * (size - span), 0), (pairs, 2, span, tokens))
        mine = jnp.where(core == 0, got[:, 0], got[:, 1])
        sent = jnp.where(core == 0, got[:, 1], got[:, 0])
        return jnp.stack([mine, sent]).reshape(rows, tokens)

    swap = [(0, 1), (1, 0)]
    passed = lax.ppermute(half_of(1 - part), "xl", swap)
    x = lax.all_gather(jnp.stack([half_of(part), passed]), "y")

    own = lax.all_to_all(out_grads[0, 0], ("xl", "y"), 0, 0, tiled=True)
    other = lax.ppermute(own, "xl", swap)
    own = own.reshape(augs, 3, size, tokens)
    other = other.reshape(augs, 3, size, tokens)

    groups = 2
    tile = rows // (2 * groups)
    in_tile = tile // span
    whole = lambda *shape: pl.BlockSpec(shape, lambda i, place: (0,) * len(shape))
    keep, send, square = pl.pallas_call(
        functools.partial(multiply_kernel, groups=groups, span=span),
        grid_spec=pltpu.PrefetchScalarGridSpec(
            num_scalar_prefetch=1,
            grid=(2 * groups,),
            in_specs=[
                pl.BlockSpec((rings, 2, tile, tokens), lambda i, place: (0, 0, i, 0)),
                whole(augs, 3, size, tokens),
                whole(augs, 3, size, tokens),
            ],
            out_specs=[
                pl.BlockSpec((in_tile, 3, 2, span, LANES), lambda i, place: (jnp.minimum(i, groups - 1), 0, 0, 0, 0)),
                pl.BlockSpec((in_tile, 3, 2, span, LANES), lambda i, place: (jnp.maximum(i - groups, 0), 0, 0, 0, 0)),
                whole(8, LANES),
            ],
            scratch_shapes=[
                pltpu.VMEM((rings, 3, 2 * LANES, 2 * tokens), jnp.bfloat16),
                pltpu.VMEM((8, LANES), jnp.float32),
            ],
        ),
        out_shape=[
            jax.ShapeDtypeStruct((pairs, 3, 2, span, LANES), jnp.float32),
            jax.ShapeDtypeStruct((pairs, 3, 2, span, LANES), jnp.float32),
            jax.ShapeDtypeStruct((8, LANES), jnp.float32),
        ],
        compiler_params=pltpu.CompilerParams(vmem_limit_bytes=VMEM),
        name="multiply",
    )(jnp.stack([part, aug_count[0]]).astype(jnp.int32), x, own, other)

    got = lax.ppermute(send, "core", swap)
    group = 2 * augs
    norms = lax.all_to_all(jnp.broadcast_to(square[:1], (group, LANES)), ("core", "xl", "y"), 0, 0, tiled=True)

    pieces = pl.pallas_call(
        functools.partial(clip_kernel, clip=clip),
        grid_spec=pltpu.PrefetchScalarGridSpec(
            num_scalar_prefetch=1,
            grid=(pairs,),
            in_specs=[
                whole(group, LANES),
                pl.BlockSpec((1, 3, 2, span, LANES), lambda i, place: (i, 0, 0, 0, 0)),
                pl.BlockSpec((1, 3, 2, span, LANES), lambda i, place: (i, 0, 0, 0, 0)),
            ],
            out_specs=pl.BlockSpec((3, 1, 2, span, LANES), lambda i, place: (0, i, 0, 0, 0)),
        ),
        out_shape=jax.ShapeDtypeStruct((3, pairs, 2, span, LANES), jnp.int16),
        compiler_params=pltpu.CompilerParams(vmem_limit_bytes=VMEM),
        name="clip",
    )(jnp.stack([part, core]).astype(jnp.int32), norms, keep, got)

    pieces = pieces.reshape(2 * chips, span, LANES)
    pieces = lax.all_to_all(pieces, ("z", "xh", "xl"), 0, 0, tiled=True)
    state = jax.ShapeDtypeStruct(noise.shape, jnp.float32)
    return pl.pallas_call(
        functools.partial(update_kernel, weight=sigma * clip, images=float(images)),
        out_shape=[state, state, state],
        compiler_params=pltpu.CompilerParams(vmem_limit_bytes=VMEM),
        name="update",
    )(pieces.reshape(chips, 2, span, LANES), noise, first_moment, second_moment)


def solution(mesh):
    images, augs = mesh.devices.shape
    split = Mesh(mesh.devices.reshape(images // 4, 2, 2, 2, augs // 2), ("z", "xh", "core", "xl", "y"))
    dp, aug = ("z", "xh", "core"), ("xl", "y")
    state = P(dp, aug)
    run = jax.shard_map(
        body,
        mesh=split,
        in_specs=(P(dp, aug, None, None), P(dp, aug, None, None, None), P(dp), state, state, state),
        out_specs=(state, state, state),
        check_vma=False,
    )
    return lambda *args: tuple(run(*args))
```

time: 350 us -> 187 us (0.53)
  the two profiles are of different devices: /device:TPU:16 before, /device:TPU:8 now
where the time goes in v1:
time: 187 us
  blocking collectives  99.1 us (53%)
  waiting for transfers between devices  33.4 us (18%)
  Pallas kernels  18 us (10%)
  starting transfers between devices  16.2 us (9%)
  between operations  14.8 us (8%)
  local copies, waits for them, and re-layouts  3.01 us (2%)
  other arithmetic  2.2 us (1%)
    all_to_all x1, blocking collectives, body(): pieces = lax.all_to_all(pieces, ('z', 'xh', 'xl'), 0, 0, tiled=True)  53.1 us
    all_to_all x1, blocking collectives, body(): own = lax.all_to_all(out_grads[0, 0], ('xl', 'y'), 0, 0, tiled=True)  46 us
    ppermute x1, waiting for transfers between devices, body(): other = lax.ppermute(own, 'xl', swap)  20 us
    pallas_call x1, Pallas kernels, body(): pl.pallas_call(functools.partial(multiply_kernel, groups=groups, span=spa...  11.5 us
    all_to_all x1, starting transfers between devices, body(): lax.all_to_all(jnp.broadcast_to(square[:1], (group, LANES)), ('core', 'xl...  7.42 us
    all_to_all x1, waiting for transfers between devices, body(): lax.all_to_all(jnp.broadcast_to(square[:1], (group, LANES)), ('core', 'xl...  6.97 us
    ppermute x1, waiting for transfers between devices, body(): passed = lax.ppermute(half_of(1 - part), 'xl', swap)  5.8 us
    pallas_call x1, Pallas kernels, body(): pl.pallas_call(functools.partial(clip_kernel, clip=clip), grid_spec=pltpu...  5.38 us
  transfers between devices with their start and end apart: 5, of which 4 were waited for; matrix products, arithmetic and copies ran while one was open for 0% of the time, Pallas kernels for 0%

profile of v1, /device:TPU:8, one launch (start us, length us, event | category | flops | bytes accessed | tf_op | source)
XLA Modules:
  0.0 186.7 jit_solution(5711920321869482087)
XLA Ops:
  7.2 0.0 all-gather.3.cloned.1.call-start
  7.2 1.2 select_bitcast_fusion.3
  8.4 0.0 copy-start.5
  8.4 3.5 %collective-permute-start = (bf16[896,128]{1,0:T(8,128)(2,1)S(1)}, bf16[896,128]{1,0:T(8,128)(2,1)S(1)}, u32[]{:S(2)}, u32[]{:S(2)}) collective-permute-start(bf16[896,128]{1,0:T(8,128)(2,1)S(1)} %bitcast.57), channel_id=1, source_target_pairs={{0,8},{8,0},{1,9},{9,1},{2,10},{10,2},{3,11},{11,3},{4,12},{12,4},... | collective-permute-start | bytes 688136 | tf_op jit(solution)/shard_map/ppermute | solution.py:123
  12.0 5.8 %collective-permute-done = bf16[896,128]{1,0:T(8,128)(2,1)S(1)} collective-permute-done((bf16[896,128]{1,0:T(8,128)(2,1)S(1)}, bf16[896,128]{1,0:T(8,128)(2,1)S(1)}, u32[]{:S(2)}, u32[]{:S(2)}) %collective-permute-start) | collective-permute-done | bytes 229408 | tf_op jit(solution)/shard_map/ppermute | solution.py:123
  17.8 0.8 pad_maximum_fusion
  18.6 0.0 all-gather.3.cloned.1.call-update
  18.7 46.0 %all_to_all.18 = bf16[16,312,128]{2,1,0:T(8,128)(2,1)S(1)} all-to-all(bf16[16,312,128]{2,1,0:T(8,128)(2,1)S(1)} %bitcast.53), channel_id=1, replica_groups=mesh['z'=12,'xh'=2,'core'=2,'xl'=2,'y'=8] {'xl','y'}, dimensions={0} | all-to-all | bytes 2555904 | tf_op jit(solution)/shard_map/all_to_all | solution.py:126
  64.7 3.2 %collective-permute-start.1 = (bf16[16,312,128]{2,1,0:T(8,128)(2,1)S(1)}, bf16[16,312,128]{2,1,0:T(8,128)(2,1)S(1)}, u32[]{:S(2)}, u32[]{:S(2)}) collective-permute-start(bf16[16,312,128]{2,1,0:T(8,128)(2,1)S(1)} %all_to_all.18), channel_id=1, source_target_pairs={{0,8},{8,0},{1,9},{9,1},{2,10},{10,2},{3,11},{11,3},{4,12},{12,4},... | collective-permute-start | bytes 3833864 | tf_op jit(solution)/shard_map/ppermute | solution.py:127
  68.6 0.1 pad_add_fusion.1.place
  68.6 20.0 %collective-permute-done.1 = bf16[16,312,128]{2,1,0:T(8,128)(2,1)S(1)} collective-permute-done((bf16[16,312,128]{2,1,0:T(8,128)(2,1)S(1)}, bf16[16,312,128]{2,1,0:T(8,128)(2,1)S(1)}, u32[]{:S(2)}, u32[]{:S(2)}) %collective-permute-start.1) | collective-permute-done | bytes 1277984 | tf_op jit(solution)/shard_map/ppermute | solution.py:127
  88.6 1.1 copy-done
  89.7 0.6 all-gather.3.cloned.1.call-done
  90.3 1.3 copy-done.1
  91.6 11.5 %multiply.1 = (f32[8,3,2,56,128]{4,3,2,1,0:T(8,128)S(1)}, f32[8,3,2,56,128]{4,3,2,1,0:T(8,128)}, f32[8,128]{1,0:T(8,128)S(1)}) custom-call(s32[2]{0:T(128)S(1)} %pad_add_fusion.1.place, bf16[8,2,896,128]{3,2,1,0:T(8,128)(2,1)} %bitcast.52, bf16[16,3,104,128]{3,2,1,0:T(8,128)(2,1)S(1)} %bitcast.47, bf16[16,3,104,128]{3,2,1,0:T(8,128)(2,1)S(1)} %bitcast.50), custom_call_target="tpu_custom_call" | custom-call | tf_op jit(solution)/shard_map/multiply/pallas_call | solution.py:135
  103.2 2.0 %collective-permute-start.2 = (f32[8,3,2,56,128]{4,3,2,1,0:T(8,128)}, f32[8,3,2,56,128]{4,3,2,1,0:T(8,128)}, u32[]{:S(2)}, u32[]{:S(2)}) collective-permute-start(f32[8,3,2,56,128]{4,3,2,1,0:T(8,128)} %get-tuple-element.8), channel_id=1, source_target_pairs={{0,16},{16,0},{1,17},{17,1},{2,18},{18,2},{3,19},{19,3},{4,20},{20... | collective-permute-start | bytes 4128776 | tf_op jit(solution)/shard_map/ppermute | solution.py:164
  105.1 0.6 broadcast_in_dim.2
  105.7 7.4 %all-to-all-start.1 = ((f32[32,1,128]{2,1,0:T(1,128)}), f32[32,1,128]{2,1,0:T(1,128)S(1)}, u32[]{:S(2)}, u32[]{:S(2)}) async-start(f32[32,1,128]{2,1,0:T(1,128)} %broadcast_in_dim.2), calls=%async_computation.1 | async-start | bytes 32768 | tf_op jit(solution)/shard_map/all_to_all | solution.py:166
  113.2 0.1 pad_add_fusion.place
  113.3 7.0 %all-to-all-done.1 = f32[32,1,128]{2,1,0:T(1,128)S(1)} async-done(((f32[32,1,128]{2,1,0:T(1,128)}), f32[32,1,128]{2,1,0:T(1,128)S(1)}, u32[]{:S(2)}, u32[]{:S(2)}) %all-to-all-start.1) | async-done | bytes 16416 | tf_op jit(solution)/shard_map/all_to_all | solution.py:166
  120.2 5.4 %clip.1 = s16[3,8,2,56,128]{4,3,2,1,0:T(8,128)(2,1)S(1)} custom-call(s32[2]{0:T(128)S(1)} %pad_add_fusion.place, f32[32,128]{1,0:T(8,128)S(1)} %bitcast.51, f32[8,3,2,56,128]{4,3,2,1,0:T(8,128)S(1)} %get-tuple-element.7.keep_ref, f32[8,3,2,56,128]{4,3,2,1,0:T(8,128)} %collective-permute-done.2.got_ref), custom_call_target="tpu_custom_call" | custom-call | tf_op jit(solution)/shard_map/clip/pallas_call | solution.py:168
  125.6 0.0 copy-start.2
  125.7 53.1 %all_to_all.19 = s16[48,56,128]{2,1,0:T(8,128)(2,1)S(1)} all-to-all(s16[48,56,128]{2,1,0:T(8,128)(2,1)S(1)} %bitcast.48), channel_id=1, replica_groups=mesh['z'=12,'xh'=2,'core'=2,'xl'=2,'y'=8] {'z','xh','xl'}, dimensions={0} | all-to-all | bytes 1376256 | tf_op jit(solution)/shard_map/all_to_all | solution.py:186
  178.7 1.1 update.1
  (12 shorter events, 0.1 us)
Async XLA Ops:
  7.2 83.1 %all-gather.3.cloned.1.call-start = ((), (), s32[]{:S(2)}) async-start(), calls=%async_computation.3 | async-start | bytes 4128768 | tf_op jit(solution)/shard_map/all_gather | solution.py:124
  8.4 10.3 %copy-start.5 = (bf16[1,1,16,312,128]{4,3,2,1,0:T(8,128)(2,1)S(1)}, bf16[1,1,16,312,128]{4,3,2,1,0:T(8,128)(2,1)}, u32[]{:S(2)}) copy-start(bf16[1,1,16,312,128]{4,3,2,1,0:T(8,128)(2,1)} %param.7) | copy-start | bytes 3833860
  8.4 9.4 %collective-permute-start = (bf16[896,128]{1,0:T(8,128)(2,1)S(1)}, bf16[896,128]{1,0:T(8,128)(2,1)S(1)}, u32[]{:S(2)}, u32[]{:S(2)}) collective-permute-start(bf16[896,128]{1,0:T(8,128)(2,1)S(1)} %bitcast.57), channel_id=1, source_target_pairs={{0,8},{8,0},{1,9},{9,1},{2,10},{10,2},{3,11},{11,3},{4,12},{12,4},... | collective-permute-start | bytes 688136 | tf_op jit(solution)/shard_map/ppermute | solution.py:123
  64.7 24.0 %collective-permute-start.1 = (bf16[16,312,128]{2,1,0:T(8,128)(2,1)S(1)}, bf16[16,312,128]{2,1,0:T(8,128)(2,1)S(1)}, u32[]{:S(2)}, u32[]{:S(2)}) collective-permute-start(bf16[16,312,128]{2,1,0:T(8,128)(2,1)S(1)} %all_to_all.18), channel_id=1, source_target_pairs={{0,8},{8,0},{1,9},{9,1},{2,10},{10,2},{3,11},{11,3},{4,12},{12,4},... | collective-permute-start | bytes 3833864 | tf_op jit(solution)/shard_map/ppermute | solution.py:127
  88.6 1.1 copy-start
  90.3 1.3 copy-start.1
  103.2 17.1 %collective-permute-start.2 = (f32[8,3,2,56,128]{4,3,2,1,0:T(8,128)}, f32[8,3,2,56,128]{4,3,2,1,0:T(8,128)}, u32[]{:S(2)}, u32[]{:S(2)}) collective-permute-start(f32[8,3,2,56,128]{4,3,2,1,0:T(8,128)} %get-tuple-element.8), channel_id=1, source_target_pairs={{0,16},{16,0},{1,17},{17,1},{2,18},{18,2},{3,19},{19,3},{4,20},{20... | collective-permute-start | bytes 4128776 | tf_op jit(solution)/shard_map/ppermute | solution.py:164
  105.7 14.5 %all-to-all-start.1 = ((f32[32,1,128]{2,1,0:T(1,128)}), f32[32,1,128]{2,1,0:T(1,128)S(1)}, u32[]{:S(2)}, u32[]{:S(2)}) async-start(f32[32,1,128]{2,1,0:T(1,128)} %broadcast_in_dim.2), calls=%async_computation.1 | async-start | bytes 32768 | tf_op jit(solution)/shard_map/all_to_all | solution.py:166
  125.6 53.1 %copy-start.2 = (f32[104,104]{1,0:T(8,128)S(1)}, f32[104,104]{1,0:T(8,128)}, u32[]{:S(2)}) copy-start(f32[104,104]{1,0:T(8,128)} %noise_ref.1) | copy-start | bytes 129796
  125.6 53.1 %copy-start.3 = (f32[104,104]{1,0:T(8,128)S(1)}, f32[104,104]{1,0:T(8,128)}, u32[]{:S(2)}) copy-start(f32[104,104]{1,0:T(8,128)} %first_ref.1) | copy-start | bytes 129796
  125.6 53.1 %copy-start.4 = (f32[104,104]{1,0:T(8,128)S(1)}, f32[104,104]{1,0:T(8,128)}, u32[]{:S(2)}) copy-start(f32[104,104]{1,0:T(8,128)} %second_ref.1) | copy-start | bytes 129796
Sparse Core Ops, SparseCore 0:
  18.8 71.4 all-gather.2

commit v2 on v0

v2 whole, which is shorter than its diff:
```python
import functools
import math

import jax
import jax.numpy as jnp
from jax import lax
from jax.experimental import pallas as pl
from jax.experimental.pallas import tpu as pltpu
from jax.sharding import Mesh
from jax.sharding import PartitionSpec as P

LANES = 128
TOP = 32767.0
VMEM = 48 * 1024 * 1024
BIG, SMALL = 56, 48
SPARE = 24


def prepare_kernel(place, *refs):
    *ins, out_ref = refs
    part, count = place[0], place[1]
    half = len(ins) // 2
    rings = ins[0].shape[0] // 2
    size = ins[0].shape[2]
    out_ref[...] = jnp.zeros_like(out_ref)
    for y in range(rings):
        for s in range(2):
            aug = jnp.bitwise_xor(part, s) * rings + y
            live = (aug < count).astype(jnp.float32).astype(jnp.bfloat16)
            at = (2 * y + s) * LANES
            for h in range(2):
                j = 0
                for ref in ins[h * half : (h + 1) * half]:
                    for k in range(ref.shape[1]):
                        out_ref[j, at : at + LANES, h * LANES : h * LANES + size] = (ref[aug, k] * live).T
                        j += 1


def multiply_kernel(place, x_hbm, y_ref, out_ref, sum_ref, x_vmem, sems):
    part, core, count = place[0], place[1], place[2]
    slabs = x_hbm.shape[0]
    blocks = out_ref.shape[1] // 2
    tiles = []
    at = 0
    for span in (BIG, SMALL):
        for i in range(2):
            tiles.append((at, span, i * blocks))
            at += blocks * span
    copies = []
    for t, (row, span, _) in enumerate(tiles):
        rows = pl.ds(row, blocks * span)
        copies.append(pltpu.make_async_copy(x_hbm.at[:, rows], x_vmem.at[:, rows], sems.at[t]))
        copies[-1].start()
    scale = 1.0 / count.astype(jnp.float32)
    big_slot = (part != core).astype(jnp.int32)
    squares = jnp.zeros((8, LANES), jnp.float32)
    for t, (row, span, first) in enumerate(tiles):
        rows = blocks * span
        copies[t].wait()
        x = jnp.concatenate([x_vmem[k, row : row + rows] for k in range(slabs)], axis=1)
        slot = big_slot if span == BIG else 1 - big_slot
        for j in range(3):
            acc = jnp.dot(x, y_ref[j], preferred_element_type=jnp.float32) * scale
            square = jnp.sum((acc * acc).reshape(rows // 8, 8, 2 * LANES), axis=0)
            squares += square[:, :LANES] + square[:, LANES:]
            for b in range(blocks):
                for h in range(2):
                    out_ref[slot, first + b, j, h, :span] = acc[b * span : (b + 1) * span, h * LANES : (h + 1) * LANES]
                    if span < BIG:
                        out_ref[slot, first + b, j, h, span:] = jnp.zeros((BIG - span, LANES), jnp.float32)
    sum_ref[...] = jnp.broadcast_to(jnp.sum(squares, keepdims=True), sum_ref.shape)


def clip_kernel(place, norms_ref, keep_ref, got_ref, out_ref, *, clip, size):
    part, core = place[0], place[1]
    half = norms_ref.shape[0] // 2
    factors = []
    for c in range(2):
        total = jnp.sum(norms_ref[c * half : (c + 1) * half], axis=0, keepdims=True)
        factors.append(jnp.minimum(1.0, clip / jnp.sqrt(total + 1e-06)))
    mine = jnp.where(core == 0, factors[0], factors[1])
    theirs = jnp.where(core == 0, factors[1], factors[0])
    lane = lax.broadcasted_iota(jnp.int32, (8, LANES), 1)

    def block(k, carry):
        for j in range(3):
            for h in range(2):
                value = keep_ref[0, k, j, h] * mine + got_ref[0, k, j, h] * theirs
                top = jnp.maximum(jnp.max(jnp.abs(value), axis=1, keepdims=True), 1e-30)
                code = jnp.ceil(jnp.log2(top) * 8.0 + 0.05)
                value = jnp.round(value * (jnp.exp2(code * -0.125) * TOP))
                pieces = []
                for g in range(SMALL // 8):
                    if g < 5:
                        spare = pltpu.roll(value[SMALL:], (size - SPARE * g) % LANES, 1)
                    else:
                        spare = jnp.zeros((8, LANES), jnp.float32)
                        for q in range(BIG // 8):
                            spare = jnp.where(lane == size + q, code[8 * q : 8 * q + 8], spare)
                    pieces.append(jnp.where(lane < size, value[8 * g : 8 * g + 8], spare))
                piece = jnp.concatenate(pieces, axis=0)
                out_ref[j, k, jnp.bitwise_xor(part, h)] = piece.astype(jnp.int32).astype(jnp.int16)
        return carry

    lax.fori_loop(0, keep_ref.shape[1], block, 0)


def update_kernel(place, got_ref, noise_ref, first_ref, second_ref, grad_ref, new_first_ref, new_second_ref, *, weight, images):
    size = noise_ref.shape[1]
    lane = lax.broadcasted_iota(jnp.int32, (8, LANES), 1)
    zero = jnp.zeros((8, LANES), jnp.float32)
    halves = []
    for part in range(2):
        total = [zero] * (SMALL // 8)
        tails = [zero] * 5
        for k in range(got_ref.shape[0]):
            value = got_ref[k, part].astype(jnp.int32).astype(jnp.float32)
            scale = jnp.exp2(value[SMALL - 8 :] * 0.125) * (1.0 / TOP)
            for g in range(SMALL // 8):
                total[g] += value[8 * g : 8 * g + 8] * scale[:, size + g : size + g + 1]
            for g in range(5):
                tails[g] += value[8 * g : 8 * g + 8] * scale[:, size + 6 : size + 7]
        tail = zero
        for g in range(5):
            back = pltpu.roll(tails[g], (SPARE * g - size) % LANES, 1)
            tail = jnp.where((lane >= SPARE * g) & (lane < SPARE * (g + 1)), back, tail)
        halves.append(total + [tail])
    even = halves[0] + halves[1][:-1]
    odd = halves[0][:-1] + halves[1]
    total = jnp.concatenate([jnp.where(place[0] == 0, a, b) for a, b in zip(even, odd)], axis=0)[:, :size]
    grad = (total + weight * noise_ref[...]) / images
    grad_ref[...] = grad
    new_first_ref[...] = 0.9 * first_ref[...] + 0.1 * grad
    new_second_ref[...] = 0.999 * second_ref[...] + 0.001 * grad * grad


def call(kernel, out_shape, in_specs, **kw):
    return pl.pallas_call(
        kernel,
        in_specs=in_specs,
        out_shape=out_shape,
        compiler_params=pltpu.CompilerParams(vmem_limit_bytes=VMEM),
        **kw,
    )


def body(acts, out_grads, aug_count, noise, first_moment, second_moment):
    part, core = lax.axis_index("xl"), lax.axis_index("core")
    augs = 2 * lax.axis_size("y")
    chips = lax.axis_size("z") * lax.axis_size("xh")
    images = 2 * chips
    width, tokens = acts.shape[2:]
    size = out_grads.shape[3] // 3
    pairs = width // size // 2
    clip = 0.5 * width * math.sqrt(3.0 * tokens / augs)
    sigma = 0.2 * math.sqrt(images) / width
    smem = pl.BlockSpec(memory_space=pltpu.SMEM)
    vmem = pl.BlockSpec(memory_space=pltpu.VMEM)
    swap = [(0, 1), (1, 0)]

    blocks = acts[0, 0].reshape(pairs, 2, size, tokens)

    def half_of(which):
        big = lax.dynamic_slice(blocks, (0, which, (size - BIG) * which, 0), (pairs, 1, BIG, tokens))
        small = lax.dynamic_slice(blocks, (0, 1 - which, BIG * which, 0), (pairs, 1, SMALL, tokens))
        return jnp.concatenate([big.reshape(pairs * BIG, tokens), small.reshape(pairs * SMALL, tokens)])

    passed = lax.ppermute(half_of(1 - part), "xl", swap)
    x = lax.all_gather(jnp.stack([half_of(part), passed]), "y")
    x = x.reshape(augs, pairs * (BIG + SMALL), tokens)

    grads = out_grads[0, 0].reshape(augs, 3, size, tokens)
    own = [lax.all_to_all(g, ("xl", "y"), 0, 0, tiled=True) for g in (grads[:, :2], grads[:, 2:])]
    other = [lax.ppermute(g, "xl", swap) for g in own]
    y = call(
        prepare_kernel,
        jax.ShapeDtypeStruct((3, augs * tokens, 2 * LANES), jnp.bfloat16),
        [smem] + [vmem] * 4,
        name="prepare",
    )(jnp.stack([part, aug_count[0]]), *own, *other)

    group = 2 * augs
    share, square = call(
        multiply_kernel,
        [
            jax.ShapeDtypeStruct((2, pairs, 3, 2, BIG, LANES), jnp.float32),
            jax.ShapeDtypeStruct((group, LANES), jnp.float32),
        ],
        [smem, pl.BlockSpec(memory_space=pl.ANY), vmem],
        out_specs=[vmem, vmem],
        scratch_shapes=[pltpu.VMEM(x.shape, x.dtype), pltpu.SemaphoreType.DMA((4,))],
        name="multiply",
    )(jnp.stack([part, core, aug_count[0]]), x, y)

    norms = lax.all_to_all(square, ("core", "xl", "y"), 0, 0, tiled=True)
    got = lax.ppermute(share, "core", swap)
    half = (1, pairs, 3, 2, BIG, LANES)
    pieces = call(
        functools.partial(clip_kernel, clip=clip, size=size),
        jax.ShapeDtypeStruct((3, pairs, 2, SMALL, LANES), jnp.int16),
        [
            smem,
            pl.BlockSpec((group, LANES), lambda i: (0, 0)),
            pl.BlockSpec(half, lambda i: (0, 0, 0, 0, 0, 0)),
            pl.BlockSpec(half, lambda i: (1, 0, 0, 0, 0, 0)),
        ],
        grid=(1,),
        out_specs=pl.BlockSpec((3, pairs, 2, SMALL, LANES), lambda i: (0, 0, 0, 0, 0)),
        name="clip",
    )(jnp.stack([part, core]), norms, share, got)

    pieces = pieces.reshape(2 * chips, SMALL, LANES)
    pieces = lax.all_to_all(pieces, ("z", "xh", "xl"), 0, 0, tiled=True)
    state = jax.ShapeDtypeStruct(noise.shape, jnp.float32)
    return call(
        functools.partial(update_kernel, weight=sigma * clip, images=float(images)),
        [state, state, state],
        [smem] + [vmem] * 4,
        out_specs=[vmem] * 3,
        name="update",
    )(core.reshape(1), pieces.reshape(chips, 2, SMALL, LANES), noise, first_moment, second_moment)


def solution(mesh):
    images, augs = mesh.devices.shape
    split = Mesh(mesh.devices.reshape(images // 4, 2, 2, 2, augs // 2), ("z", "xh", "core", "xl", "y"))
    dp, aug = ("z", "xh", "core"), ("xl", "y")
    state = P(dp, aug)
    run = jax.shard_map(
        body,
        mesh=split,
        in_specs=(P(dp, aug, None, None), P(dp, aug, None, None, None), P(dp), state, state, state),
        out_specs=(state, state, state),
        check_vma=False,
    )
    return lambda *args: tuple(run(*args))
```

time: 350 us -> 183 us (0.52)
  the two profiles are of different devices: /device:TPU:16 before, /device:TPU:8 now
where the time goes in v2:
time: 183 us; the launch traced here: 182 us
  waiting for transfers between devices  53.5 us (29%)
  blocking collectives  49.8 us (27%)
  starting transfers between devices  38.5 us (21%)
  between operations  14.8 us (8%)
  Pallas kernels  14.1 us (8%)
  local copies, waits for them, and re-layouts  10.6 us (6%)
    all_to_all x1, blocking collectives, body(): pieces = lax.all_to_all(pieces, ('z', 'xh', 'xl'), 0, 0, tiled=True)  49.8 us
    all_to_all x2, waiting for transfers between devices, body(): lax.all_to_all(g, ('xl', 'y'), 0, 0, tiled=True)  30.4 us
    all_to_all x2, starting transfers between devices, body(): lax.all_to_all(g, ('xl', 'y'), 0, 0, tiled=True)  18.9 us
    ppermute x2, waiting for transfers between devices, body(): other = [lax.ppermute(g, 'xl', swap) for g in own]  10.6 us
    all_to_all x1, starting transfers between devices, body(): norms = lax.all_to_all(square, ('core', 'xl', 'y'), 0, 0, tiled=True)  7.53 us
    pallas_call x1, Pallas kernels, body(): call(multiply_kernel, [jax.ShapeDtypeStruct((2, pairs, 3, 2, BIG, LANES),...  7.52 us
    all_to_all x1, waiting for transfers between devices, body(): norms = lax.all_to_all(square, ('core', 'xl', 'y'), 0, 0, tiled=True)  6.97 us
    unnamed x24, local copies, waits for them, and re-layouts  6.76 us
  transfers between devices with their start and end apart: 8, of which 5 were waited for; matrix products, arithmetic and copies ran while one was open for 1% of the time, Pallas kernels for 1%

profile of v2, /device:TPU:8, one launch (start us, length us, event | category | flops | bytes accessed | tf_op | source)
XLA Modules:
  0.0 182.4 jit_solution(16528881482078686814)
XLA Ops:
  7.2 1.1 constant_dynamic-slice_fusion.2
  8.3 1.0 constant_dynamic-slice_fusion.3
  9.3 3.4 %collective-permute-start = (bf16[832,128]{1,0:T(8,128)(2,1)S(1)}, bf16[832,128]{1,0:T(8,128)(2,1)S(1)}, u32[]{:S(2)}, u32[]{:S(2)}) collective-permute-start(bf16[832,128]{1,0:T(8,128)(2,1)S(1)} %pad_maximum_fusion.1), channel_id=1, source_target_pairs={{0,8},{8,0},{1,9},{9,1},{2,10},{10,2},{3,11},{11,3},{4,12},{12,4},... | collective-permute-start | bytes 638984 | tf_op jit(solution)/shard_map/ppermute | solution.py:168
  12.7 5.5 %collective-permute-done = bf16[832,128]{1,0:T(8,128)(2,1)S(1)} collective-permute-done((bf16[832,128]{1,0:T(8,128)(2,1)S(1)}, bf16[832,128]{1,0:T(8,128)(2,1)S(1)}, u32[]{:S(2)}, u32[]{:S(2)}) %collective-permute-start) | collective-permute-done | bytes 213024 | tf_op jit(solution)/shard_map/ppermute | solution.py:168
  19.1 1.0 slice.8
  20.0 11.7 %all-to-all-start = ((bf16[16,2,104,128]{3,2,1,0:T(8,128)(2,1)}), bf16[16,2,104,128]{3,2,1,0:T(8,128)(2,1)S(1)}, u32[]{:S(2)}, u32[]{:S(2)}) async-start(bf16[16,2,104,128]{3,2,1,0:T(8,128)(2,1)} %slice.8), calls=%async_computation | async-start | bytes 1703936 | tf_op jit(solution)/shard_map/all_to_all | solution.py:173
  32.5 19.2 %all-to-all-done.refs_0_ = bf16[16,2,104,128]{3,2,1,0:T(8,128)(2,1)S(1)} async-done(((bf16[16,2,104,128]{3,2,1,0:T(8,128)(2,1)}), bf16[16,2,104,128]{3,2,1,0:T(8,128)(2,1)S(1)}, u32[]{:S(2)}, u32[]{:S(2)}) %all-to-all-start) | async-done | bytes 852000 | tf_op jit(solution)/shard_map/all_to_all | solution.py:173
  51.7 7.2 %all-to-all-start.1 = ((bf16[16,1,104,128]{3,2,1,0:T(8,128)(2,1)}), bf16[16,1,104,128]{3,2,1,0:T(8,128)(2,1)S(1)}, u32[]{:S(2)}, u32[]{:S(2)}) async-start(bf16[16,1,104,128]{3,2,1,0:T(8,128)(2,1)} %slice.9), calls=%async_computation.1 | async-start | bytes 851968 | tf_op jit(solution)/shard_map/all_to_all | solution.py:173
  58.9 3.4 %collective-permute-start.1 = (bf16[16,2,104,128]{3,2,1,0:T(8,128)(2,1)S(1)}, bf16[16,2,104,128]{3,2,1,0:T(8,128)(2,1)S(1)}, u32[]{:S(2)}, u32[]{:S(2)}) collective-permute-start(bf16[16,2,104,128]{3,2,1,0:T(8,128)(2,1)S(1)} %all-to-all-done.refs_0_), channel_id=1, source_target_pairs={{0,8},{8,0},{1,9},{9,1},{2,10},{10,2},{3,11},{11,3},{4,12},{12,4},... | collective-permute-start | bytes 2555912 | tf_op jit(solution)/shard_map/ppermute | solution.py:174
  62.3 11.3 %all-to-all-done.1.refs_1_ = bf16[16,1,104,128]{3,2,1,0:T(8,128)(2,1)S(1)} async-done(((bf16[16,1,104,128]{3,2,1,0:T(8,128)(2,1)}), bf16[16,1,104,128]{3,2,1,0:T(8,128)(2,1)S(1)}, u32[]{:S(2)}, u32[]{:S(2)}) %all-to-all-start.1) | async-done | bytes 426016 | tf_op jit(solution)/shard_map/all_to_all | solution.py:173
  73.5 3.4 %collective-permute-start.2 = (bf16[16,1,104,128]{3,2,1,0:T(8,128)(2,1)S(1)}, bf16[16,1,104,128]{3,2,1,0:T(8,128)(2,1)S(1)}, u32[]{:S(2)}, u32[]{:S(2)}) collective-permute-start(bf16[16,1,104,128]{3,2,1,0:T(8,128)(2,1)S(1)} %all-to-all-done.1.refs_1_), channel_id=1, source_target_pairs={{0,8},{8,0},{1,9},{9,1},{2,10},{10,2},{3,11},{11,3},{4,12},{12,4},... | collective-permute-start | bytes 1277960 | tf_op jit(solution)/shard_map/ppermute | solution.py:174
  78.5 10.6 %collective-permute-done.2.refs_3_ = bf16[16,1,104,128]{3,2,1,0:T(8,128)(2,1)S(1)} collective-permute-done((bf16[16,1,104,128]{3,2,1,0:T(8,128)(2,1)S(1)}, bf16[16,1,104,128]{3,2,1,0:T(8,128)(2,1)S(1)}, u32[]{:S(2)}, u32[]{:S(2)}) %collective-permute-start.2) | collective-permute-done | bytes 426016 | tf_op jit(solution)/shard_map/ppermute | solution.py:174
  90.7 1.2 copy-done.1
  91.9 1.0 copy-done.3
  92.9 1.2 copy-done.5
  94.0 1.0 copy-done.7
  95.0 1.7 prepare.1.y_ref
  96.7 7.5 %multiply.1 = (f32[2,8,3,2,56,128]{5,4,3,2,1,0:T(8,128)}, f32[32,128]{1,0:T(8,128)}) custom-call(s32[3]{0:T(128)S(1)} %pad_add_fusion.1.place, bf16[16,832,128]{2,1,0:T(8,128)(2,1)} %all-gather.3.cloned.1.call-done.x_hbm, bf16[3,2048,256]{2,1,0:T(8,128)(2,1)S(1)} %prepare.1.y_ref), custom_call_target="tpu_custom_call" | custom-call | tf_op jit(solution)/shard_map/multiply/pallas_call | solution.py:183
  104.3 1.9 %collective-permute-start.3 = (f32[2,8,3,2,56,128]{5,4,3,2,1,0:T(8,128)}, f32[2,8,3,2,56,128]{5,4,3,2,1,0:T(8,128)S(1)}, u32[]{:S(2)}, u32[]{:S(2)}) collective-permute-start(f32[2,8,3,2,56,128]{5,4,3,2,1,0:T(8,128)} %get-tuple-element.6.keep_ref), channel_id=1, source_target_pairs={{0,16},{16,0},{1,17},{17,1},{2,18},{18,2},{3,19},{19,3},{4,20},{20... | collective-permute-start | bytes 8257544 | tf_op jit(solution)/shard_map/ppermute | solution.py:196
  106.2 7.5 %all-to-all-start.2 = ((f32[32,1,128]{2,1,0:T(1,128)}), f32[32,1,128]{2,1,0:T(1,128)S(1)}, u32[]{:S(2)}, u32[]{:S(2)}) async-start(f32[32,1,128]{2,1,0:T(1,128)} %bitcast.11), calls=%async_computation.2 | async-start | bytes 32768 | tf_op jit(solution)/shard_map/all_to_all | solution.py:195
  113.8 7.0 %all-to-all-done.2 = f32[32,1,128]{2,1,0:T(1,128)S(1)} async-done(((f32[32,1,128]{2,1,0:T(1,128)}), f32[32,1,128]{2,1,0:T(1,128)S(1)}, u32[]{:S(2)}, u32[]{:S(2)}) %all-to-all-start.2) | async-done | bytes 16416 | tf_op jit(solution)/shard_map/all_to_all | solution.py:195
  120.8 3.5 %clip.1 = s16[3,8,2,48,128]{4,3,2,1,0:T(8,128)(2,1)S(1)} custom-call(s32[2]{0:T(128)S(1)} %pad_add_fusion.place, f32[32,128]{1,0:T(8,128)S(1)} %bitcast.27, f32[2,8,3,2,56,128]{5,4,3,2,1,0:T(8,128)} %get-tuple-element.6.keep_ref, f32[2,8,3,2,56,128]{5,4,3,2,1,0:T(8,128)S(1)} %collective-permute-done.3.got_ref), custom_call_target="tpu_custom_call" | custom-call | tf_op jit(solution)/shard_map/clip/pallas_call | solution.py:198
  124.3 49.8 %all_to_all.26 = s16[48,48,128]{2,1,0:T(8,128)(2,1)S(1)} all-to-all(s16[48,48,128]{2,1,0:T(8,128)(2,1)S(1)} %bitcast.25), channel_id=1, replica_groups=mesh['z'=12,'xh'=2,'core'=2,'xl'=2,'y'=8] {'z','xh','xl'}, dimensions={0} | all-to-all | bytes 1179648 | tf_op jit(solution)/shard_map/all_to_all | solution.py:213
  174.2 1.4 update.1
  (32 shorter events, 4.4 us)
Async XLA Ops:
  7.2 11.9 %copy-start.11 = (bf16[1,1,16,312,128]{4,3,2,1,0:T(8,128)(2,1)S(1)}, bf16[1,1,16,312,128]{4,3,2,1,0:T(8,128)(2,1)}, u32[]{:S(2)}) copy-start(bf16[1,1,16,312,128]{4,3,2,1,0:T(8,128)(2,1)} %param.7) | copy-start | bytes 3833860
  7.2 89.6 %all-gather.3.cloned.1.call-start = ((), (), s32[]{:S(2)}) async-start(), calls=%async_computation.4 | async-start | bytes 3833856 | tf_op jit(solution)/shard_map/all_gather | solution.py:169
  9.3 8.9 %collective-permute-start = (bf16[832,128]{1,0:T(8,128)(2,1)S(1)}, bf16[832,128]{1,0:T(8,128)(2,1)S(1)}, u32[]{:S(2)}, u32[]{:S(2)}) collective-permute-start(bf16[832,128]{1,0:T(8,128)(2,1)S(1)} %pad_maximum_fusion.1), channel_id=1, source_target_pairs={{0,8},{8,0},{1,9},{9,1},{2,10},{10,2},{3,11},{11,3},{4,12},{12,4},... | collective-permute-start | bytes 638984 | tf_op jit(solution)/shard_map/ppermute | solution.py:168
  20.0 31.7 %all-to-all-start = ((bf16[16,2,104,128]{3,2,1,0:T(8,128)(2,1)}), bf16[16,2,104,128]{3,2,1,0:T(8,128)(2,1)S(1)}, u32[]{:S(2)}, u32[]{:S(2)}) async-start(bf16[16,2,104,128]{3,2,1,0:T(8,128)(2,1)} %slice.8), calls=%async_computation | async-start | bytes 1703936 | tf_op jit(solution)/shard_map/all_to_all | solution.py:173
  51.7 37.3 %copy-start = (bf16[16,2,104,128]{3,2,1,0:T(8,128)(2,1)}, bf16[16,2,104,128]{3,2,1,0:T(8,128)(2,1)S(1)}, u32[]{:S(2)}) copy-start(bf16[16,2,104,128]{3,2,1,0:T(8,128)(2,1)S(1)} %all-to-all-done.refs_0_) | copy-start | bytes 2555908
  51.7 21.8 %all-to-all-start.1 = ((bf16[16,1,104,128]{3,2,1,0:T(8,128)(2,1)}), bf16[16,1,104,128]{3,2,1,0:T(8,128)(2,1)S(1)}, u32[]{:S(2)}, u32[]{:S(2)}) async-start(bf16[16,1,104,128]{3,2,1,0:T(8,128)(2,1)} %slice.9), calls=%async_computation.1 | async-start | bytes 851968 | tf_op jit(solution)/shard_map/all_to_all | solution.py:173
  58.9 30.9 %collective-permute-start.1 = (bf16[16,2,104,128]{3,2,1,0:T(8,128)(2,1)S(1)}, bf16[16,2,104,128]{3,2,1,0:T(8,128)(2,1)S(1)}, u32[]{:S(2)}, u32[]{:S(2)}) collective-permute-start(bf16[16,2,104,128]{3,2,1,0:T(8,128)(2,1)S(1)} %all-to-all-done.refs_0_), channel_id=1, source_target_pairs={{0,8},{8,0},{1,9},{9,1},{2,10},{10,2},{3,11},{11,3},{4,12},{12,4},... | collective-permute-start | bytes 2555912 | tf_op jit(solution)/shard_map/ppermute | solution.py:174
  73.5 15.5 %collective-permute-start.2 = (bf16[16,1,104,128]{3,2,1,0:T(8,128)(2,1)S(1)}, bf16[16,1,104,128]{3,2,1,0:T(8,128)(2,1)S(1)}, u32[]{:S(2)}, u32[]{:S(2)}) collective-permute-start(bf16[16,1,104,128]{3,2,1,0:T(8,128)(2,1)S(1)} %all-to-all-done.1.refs_1_), channel_id=1, source_target_pairs={{0,8},{8,0},{1,9},{9,1},{2,10},{10,2},{3,11},{11,3},{4,12},{12,4},... | collective-permute-start | bytes 1277960 | tf_op jit(solution)/shard_map/ppermute | solution.py:174
  76.9 0.8 copy-start.2
  89.0 0.8 copy-start.6
  89.8 0.9 copy-start.4
  90.7 1.2 copy-start.1
  91.9 1.0 copy-start.3
  92.9 1.2 copy-start.5
  94.0 1.0 copy-start.7
  104.3 16.5 %collective-permute-start.3 = (f32[2,8,3,2,56,128]{5,4,3,2,1,0:T(8,128)}, f32[2,8,3,2,56,128]{5,4,3,2,1,0:T(8,128)S(1)}, u32[]{:S(2)}, u32[]{:S(2)}) collective-permute-start(f32[2,8,3,2,56,128]{5,4,3,2,1,0:T(8,128)} %get-tuple-element.6.keep_ref), channel_id=1, source_target_pairs={{0,16},{16,0},{1,17},{17,1},{2,18},{18,2},{3,19},{19,3},{4,20},{20... | collective-permute-start | bytes 8257544 | tf_op jit(solution)/shard_map/ppermute | solution.py:196
  106.2 14.6 %all-to-all-start.2 = ((f32[32,1,128]{2,1,0:T(1,128)}), f32[32,1,128]{2,1,0:T(1,128)S(1)}, u32[]{:S(2)}, u32[]{:S(2)}) async-start(f32[32,1,128]{2,1,0:T(1,128)} %bitcast.11), calls=%async_computation.2 | async-start | bytes 32768 | tf_op jit(solution)/shard_map/all_to_all | solution.py:195
  120.8 53.4 %copy-start.8 = (f32[104,104]{1,0:T(8,128)S(1)}, f32[104,104]{1,0:T(8,128)}, u32[]{:S(2)}) copy-start(f32[104,104]{1,0:T(8,128)} %noise_ref.1) | copy-start | bytes 129796
  120.8 53.4 %copy-start.9 = (f32[104,104]{1,0:T(8,128)S(1)}, f32[104,104]{1,0:T(8,128)}, u32[]{:S(2)}) copy-start(f32[104,104]{1,0:T(8,128)} %first_ref.1) | copy-start | bytes 129796
  120.8 53.4 %copy-start.10 = (f32[104,104]{1,0:T(8,128)S(1)}, f32[104,104]{1,0:T(8,128)}, u32[]{:S(2)}) copy-start(f32[104,104]{1,0:T(8,128)} %second_ref.1) | copy-start | bytes 129796
Sparse Core Ops, SparseCore 0:
  19.2 70.2 all-gather.2

commit v3 on v2

--- a/solution.py
+++ b/solution.py
@@ -16,27 +16,36 @@
 SPARE = 24
 
 
-def prepare_kernel(place, *refs):
-    *ins, out_ref = refs
-    part, count = place[0], place[1]
-    half = len(ins) // 2
-    rings = ins[0].shape[0] // 2
-    size = ins[0].shape[2]
-    out_ref[...] = jnp.zeros_like(out_ref)
-    for y in range(rings):
-        for s in range(2):
-            aug = jnp.bitwise_xor(part, s) * rings + y
-            live = (aug < count).astype(jnp.float32).astype(jnp.bfloat16)
-            at = (2 * y + s) * LANES
-            for h in range(2):
-                j = 0
-                for ref in ins[h * half : (h + 1) * half]:
-                    for k in range(ref.shape[1]):
-                        out_ref[j, at : at + LANES, h * LANES : h * LANES + size] = (ref[aug, k] * live).T
-                        j += 1
-
-
-def multiply_kernel(place, x_hbm, y_ref, out_ref, sum_ref, x_vmem, sems):
+def stack_kernel(mine_ref, passed_ref, first_ref, out_ref):
+    out_ref[0] = mine_ref[...]
+    out_ref[1] = passed_ref[...]
+
+
+def prepare_kernel(place, grads_hbm, *refs, shifts):
+    *pieces, out_ref, held, sems = refs
+    part, ring, count = place[0], place[1], place[2]
+    rings = grads_hbm.shape[1]
+    size = grads_hbm.shape[3]
+    copies = [pltpu.make_async_copy(grads_hbm.at[:, ring], held.at[0], sems.at[0])]
+    for i, piece in enumerate(pieces):
+        copies.append(pltpu.make_async_copy(piece, held.at[i + 1], sems.at[i + 1]))
+    for copy in copies:
+        copy.start()
+    for j in range(3):
+        for h in range(2):
+            out_ref[j, :, h * LANES + size : (h + 1) * LANES] = jnp.zeros((out_ref.shape[1], LANES - size), out_ref.dtype)
+    for i, copy in enumerate(copies):
+        copy.wait()
+        y = lax.rem(ring - shifts[i % rings] + rings, rings)
+        row = i // rings
+        live = (jnp.bitwise_xor(part, row) * rings + y < count).astype(jnp.float32).astype(jnp.bfloat16)
+        at = pl.multiple_of((2 * y + row) * LANES, LANES)
+        for h in range(2):
+            for j in range(3):
+                out_ref[j, pl.ds(at, LANES), h * LANES : h * LANES + size] = (held[i, h, j] * live).T
+
+
+def multiply_kernel(place, x_hbm, y_ref, out_hbm, sum_ref, x_vmem, out_ref, sems, out_sems):
     part, core, count = place[0], place[1], place[2]
     slabs = x_hbm.shape[0]
     blocks = out_ref.shape[1] // 2
@@ -68,11 +77,16 @@
                     out_ref[slot, first + b, j, h, :span] = acc[b * span : (b + 1) * span, h * LANES : (h + 1) * LANES]
                     if span < BIG:
                         out_ref[slot, first + b, j, h, span:] = jnp.zeros((BIG - span, LANES), jnp.float32)
+        some = pl.ds(first, blocks)
+        copies.append(pltpu.make_async_copy(out_ref.at[slot, some], out_hbm.at[slot, some], out_sems.at[t]))
+        copies[-1].start()
     sum_ref[...] = jnp.broadcast_to(jnp.sum(squares, keepdims=True), sum_ref.shape)
+    for copy in copies[len(tiles) :]:
+        copy.wait()
 
 
 def clip_kernel(place, norms_ref, keep_ref, got_ref, out_ref, *, clip, size):
-    part, core = place[0], place[1]
+    core = place[0]
     half = norms_ref.shape[0] // 2
     factors = []
     for c in range(2):
@@ -99,7 +113,7 @@
                             spare = jnp.where(lane == size + q, code[8 * q : 8 * q + 8], spare)
                     pieces.append(jnp.where(lane < size, value[8 * g : 8 * g + 8], spare))
                 piece = jnp.concatenate(pieces, axis=0)
-                out_ref[j, k, jnp.bitwise_xor(part, h)] = piece.astype(jnp.int32).astype(jnp.int16)
+                out_ref[j, k, h] = piece.astype(jnp.int32).astype(jnp.int16)
         return carry
 
     lax.fori_loop(0, keep_ref.shape[1], block, 0)
@@ -145,8 +159,9 @@
 
 
 def body(acts, out_grads, aug_count, noise, first_moment, second_moment):
-    part, core = lax.axis_index("xl"), lax.axis_index("core")
-    augs = 2 * lax.axis_size("y")
+    part, core, ring = lax.axis_index("xl"), lax.axis_index("core"), lax.axis_index("y")
+    rings = lax.axis_size("y")
+    augs = 2 * rings
     chips = lax.axis_size("z") * lax.axis_size("xh")
     images = 2 * chips
     width, tokens = acts.shape[2:]
@@ -166,18 +181,32 @@
         return jnp.concatenate([big.reshape(pairs * BIG, tokens), small.reshape(pairs * SMALL, tokens)])
 
     passed = lax.ppermute(half_of(1 - part), "xl", swap)
-    x = lax.all_gather(jnp.stack([half_of(part), passed]), "y")
+    mine = half_of(part)
+
+    grads = out_grads[0, 0].reshape(2, rings, 3, size, tokens)
+
+    def shifted(shift):
+        heads = lax.dynamic_index_in_dim(grads, lax.rem(ring + shift, rings), 1, keepdims=False)
+        return lax.ppermute(heads, "y", [(i, (i + shift) % rings) for i in range(rings)]) if shift else heads
+
+    shifts = (0, 4, 3, 5, 2, 6, 1, 7)
+    pieces = [shifted(shift) for shift in shifts]
+    stacked = call(
+        stack_kernel,
+        jax.ShapeDtypeStruct((2,) + mine.shape, mine.dtype),
+        [vmem, vmem, pl.BlockSpec(memory_space=pl.ANY)],
+        name="stack",
+    )(mine, passed, pieces[1])
+    x = lax.all_gather(stacked, "y")
     x = x.reshape(augs, pairs * (BIG + SMALL), tokens)
-
-    grads = out_grads[0, 0].reshape(augs, 3, size, tokens)
-    own = [lax.all_to_all(g, ("xl", "y"), 0, 0, tiled=True) for g in (grads[:, :2], grads[:, 2:])]
-    other = [lax.ppermute(g, "xl", swap) for g in own]
+    pieces = pieces[1:] + [lax.ppermute(piece, "xl", swap) for piece in pieces]
     y = call(
-        prepare_kernel,
+        functools.partial(prepare_kernel, shifts=shifts),
         jax.ShapeDtypeStruct((3, augs * tokens, 2 * LANES), jnp.bfloat16),
-        [smem] + [vmem] * 4,
+        [smem] + [pl.BlockSpec(memory_space=pl.ANY)] * augs,
+        scratch_shapes=[pltpu.VMEM((augs, 2, 3, size, tokens), jnp.bfloat16), pltpu.SemaphoreType.DMA((augs,))],
         name="prepare",
-    )(jnp.stack([part, aug_count[0]]), *own, *other)
+    )(jnp.stack([part, ring, aug_count[0]]), grads, *pieces)
 
     group = 2 * augs
     share, square = call(
@@ -187,8 +216,13 @@
             jax.ShapeDtypeStruct((group, LANES), jnp.float32),
         ],
         [smem, pl.BlockSpec(memory_space=pl.ANY), vmem],
-        out_specs=[vmem, vmem],
-        scratch_shapes=[pltpu.VMEM(x.shape, x.dtype), pltpu.SemaphoreType.DMA((4,))],
+        out_specs=[pl.BlockSpec(memory_space=pl.ANY), vmem],
+        scratch_shapes=[
+            pltpu.VMEM(x.shape, x.dtype),
+            pltpu.VMEM((2, pairs, 3, 2, BIG, LANES), jnp.float32),
+            pltpu.SemaphoreType.DMA((4,)),
+            pltpu.SemaphoreType.DMA((4,)),
+        ],
         name="multiply",
     )(jnp.stack([part, core, aug_count[0]]), x, y)
 
@@ -207,7 +241,7 @@
         grid=(1,),
         out_specs=pl.BlockSpec((3, pairs, 2, SMALL, LANES), lambda i: (0, 0, 0, 0, 0)),
         name="clip",
-    )(jnp.stack([part, core]), norms, share, got)
+    )(core.reshape(1), norms, share, got)
 
     pieces = pieces.reshape(2 * chips, SMALL, LANES)
     pieces = lax.all_to_all(pieces, ("z", "xh", "xl"), 0, 0, tiled=True)

time: 183 us -> 178 us (0.973)
  waiting for transfers between devices: 53.5 us -> 20.4 us
  starting transfers between devices: 38.5 us -> 59.9 us
  blocking collectives: 49.8 us -> 57.5 us
  local copies, waits for them, and re-layouts: 10.6 us -> 5.46 us
  Pallas kernels: 14.1 us -> 19.1 us
    ppermute x2 -> x15, starting transfers between devices: 6.72 us -> 54.6 us  [the longest x7 32.7 us: shifted(): lax.ppermute(heads, 'y', [(i, (i + shift) % rings) for i in range(rings)])]
    all_to_all x3 -> x0, waiting for transfers between devices: 37.4 us -> none  [the longest x2 30.4 us: body(): lax.all_to_all(g, ('xl', 'y'), 0, 0, tiled=True)]
    all_to_all x3 -> x0, starting transfers between devices: 26.5 us -> none  [the longest x2 18.9 us: body(): lax.all_to_all(g, ('xl', 'y'), 0, 0, tiled=True)]
    all_to_all x0 -> x1, blocking collectives: none -> 13.7 us  [body(): norms = lax.all_to_all(square, ('core', 'xl', 'y'), 0, 0, tiled=True)]
    pallas_call x1 -> x2, Pallas kernels: 1.65 us -> 8.37 us  [the longest x1 7.58 us: body(): call(functools.partial(prepare_kernel, shifts=shifts), jax.ShapeDtypeStru...]
    all_to_all x1, blocking collectives: 49.8 us -> 43.8 us  [body(): pieces = lax.all_to_all(pieces, ('z', 'xh', 'xl'), 0, 0, tiled=True)]
    ppermute x1, waiting for transfers between devices: 5.45 us -> 0.01 us  [body(): passed = lax.ppermute(half_of(1 - part), 'xl', swap)]
    all_gather x1, waiting for transfers between devices: 0.02 us -> 4.95 us  [body(): x = lax.all_gather(stacked, 'y')]
  transfers between devices with their start and end apart: 8 -> 18, of which waited for: 5 -> 6; matrix products, arithmetic and copies ran while one was open for 1% -> 1% of each run, Pallas kernels for 1% -> 4%
where the time goes in v3:
time: 178 us; the launch traced here: 177 us
  starting transfers between devices  59.9 us (34%)
  blocking collectives  57.5 us (32%)
  waiting for transfers between devices  20.4 us (11%)
  Pallas kernels  19.1 us (11%)
  between operations  15 us (8%)
  local copies, waits for them, and re-layouts  5.46 us (3%)
    all_to_all x1, blocking collectives, body(): pieces = lax.all_to_all(pieces, ('z', 'xh', 'xl'), 0, 0, tiled=True)  43.8 us
    ppermute x7, starting transfers between devices, shifted(): lax.ppermute(heads, 'y', [(i, (i + shift) % rings) for i in range(rings)])  32.7 us
    ppermute x8, starting transfers between devices, body(): pieces = pieces[1:] + [lax.ppermute(piece, 'xl', swap) for piece in pieces]  21.9 us
    all_to_all x1, blocking collectives, body(): norms = lax.all_to_all(square, ('core', 'xl', 'y'), 0, 0, tiled=True)  13.7 us
    ppermute x7, waiting for transfers between devices, shifted(): lax.ppermute(heads, 'y', [(i, (i + shift) % rings) for i in range(rings)])  10.5 us
    pallas_call x1, Pallas kernels, body(): call(functools.partial(prepare_kernel, shifts=shifts), jax.ShapeDtypeStru...  7.58 us
    pallas_call x1, Pallas kernels, body(): call(multiply_kernel, [jax.ShapeDtypeStruct((2, pairs, 3, 2, BIG, LANES),...  7.09 us
    all_gather x1, waiting for transfers between devices, body(): x = lax.all_gather(stacked, 'y')  4.95 us
  transfers between devices with their start and end apart: 18, of which 6 were waited for; matrix products, arithmetic and copies ran while one was open for 1% of the time, Pallas kernels for 4%

profile of v3, /device:TPU:8, one launch (start us, length us, event | category | flops | bytes accessed | tf_op | source)
XLA Modules:
  0.0 177.4 jit_solution(6577148422976031117)
XLA Ops:
  9.3 3.4 %collective-permute-start = (bf16[832,128]{1,0:T(8,128)(2,1)S(1)}, bf16[832,128]{1,0:T(8,128)(2,1)S(1)}, u32[]{:S(2)}, u32[]{:S(2)}) collective-permute-start(bf16[832,128]{1,0:T(8,128)(2,1)S(1)} %pad_maximum_fusion.1), channel_id=1, source_target_pairs={{0,8},{8,0},{1,9},{9,1},{2,10},{10,2},{3,11},{11,3},{4,12},{12,4},... | collective-permute-start | bytes 638984 | tf_op jit(solution)/shard_map/ppermute | solution.py:183
  14.3 6.8 %collective-permute-start.1 = (bf16[2,3,104,128]{3,2,1,0:T(8,128)(2,1)S(1)}, bf16[2,3,104,128]{3,2,1,0:T(8,128)(2,1)S(1)}, u32[]{:S(2)}, u32[]{:S(2)}) collective-permute-start(bf16[2,3,104,128]{3,2,1,0:T(8,128)(2,1)S(1)} %get-tuple-element.14), channel_id=1, source_target_pairs={{0,4},{1,5},{2,6},{3,7},{4,0},{5,1},{6,2},{7,3},{8,12},{9,13},{10,... | collective-permute-start | bytes 479240 | tf_op jit(solution)/shard_map/ppermute | solution.py:190
  21.1 7.2 %collective-permute-done.1.first_ref.refs_0_ = bf16[2,3,104,128]{3,2,1,0:T(8,128)(2,1)S(1)} collective-permute-done((bf16[2,3,104,128]{3,2,1,0:T(8,128)(2,1)S(1)}, bf16[2,3,104,128]{3,2,1,0:T(8,128)(2,1)S(1)}, u32[]{:S(2)}, u32[]{:S(2)}) %collective-permute-start.1) | collective-permute-done | bytes 159776 | tf_op jit(solution)/shard_map/ppermute | solution.py:190
  29.2 2.4 %collective-permute-start.8 = (bf16[2,3,104,128]{3,2,1,0:T(8,128)(2,1)S(1)}, bf16[2,3,104,128]{3,2,1,0:T(8,128)(2,1)S(1)}, u32[]{:S(2)}, u32[]{:S(2)}) collective-permute-start(bf16[2,3,104,128]{3,2,1,0:T(8,128)(2,1)S(1)} %get-tuple-element.7), channel_id=1, source_target_pairs={{0,8},{8,0},{1,9},{9,1},{2,10},{10,2},{3,11},{11,3},{4,12},{12,4},... | collective-permute-start | bytes 479240 | tf_op jit(solution)/shard_map/ppermute | solution.py:202
  31.6 8.4 %collective-permute-start.7 = (bf16[2,3,104,128]{3,2,1,0:T(8,128)(2,1)S(1)}, bf16[2,3,104,128]{3,2,1,0:T(8,128)(2,1)S(1)}, u32[]{:S(2)}, u32[]{:S(2)}) collective-permute-start(bf16[2,3,104,128]{3,2,1,0:T(8,128)(2,1)S(1)} %get-tuple-element.8), channel_id=1, source_target_pairs={{0,7},{1,0},{2,1},{3,2},{4,3},{5,4},{6,5},{7,6},{8,15},{9,8},{10,9... | collective-permute-start | bytes 479240 | tf_op jit(solution)/shard_map/ppermute | solution.py:190
  40.0 1.9 %collective-permute-start.6 = (bf16[2,3,104,128]{3,2,1,0:T(8,128)(2,1)S(1)}, bf16[2,3,104,128]{3,2,1,0:T(8,128)(2,1)S(1)}, u32[]{:S(2)}, u32[]{:S(2)}) collective-permute-start(bf16[2,3,104,128]{3,2,1,0:T(8,128)(2,1)S(1)} %get-tuple-element.9), channel_id=1, source_target_pairs={{0,1},{1,2},{2,3},{3,4},{4,5},{5,6},{6,7},{7,0},{8,9},{9,10},{10,1... | collective-permute-start | bytes 479240 | tf_op jit(solution)/shard_map/ppermute | solution.py:190
  41.9 4.6 %collective-permute-start.5 = (bf16[2,3,104,128]{3,2,1,0:T(8,128)(2,1)S(1)}, bf16[2,3,104,128]{3,2,1,0:T(8,128)(2,1)S(1)}, u32[]{:S(2)}, u32[]{:S(2)}) collective-permute-start(bf16[2,3,104,128]{3,2,1,0:T(8,128)(2,1)S(1)} %get-tuple-element.10), channel_id=1, source_target_pairs={{0,6},{1,7},{2,0},{3,1},{4,2},{5,3},{6,4},{7,5},{8,14},{9,15},{10,... | collective-permute-start | bytes 479240 | tf_op jit(solution)/shard_map/ppermute | solution.py:190
  46.5 2.2 %collective-permute-start.4 = (bf16[2,3,104,128]{3,2,1,0:T(8,128)(2,1)S(1)}, bf16[2,3,104,128]{3,2,1,0:T(8,128)(2,1)S(1)}, u32[]{:S(2)}, u32[]{:S(2)}) collective-permute-start(bf16[2,3,104,128]{3,2,1,0:T(8,128)(2,1)S(1)} %get-tuple-element.11), channel_id=1, source_target_pairs={{0,2},{1,3},{2,4},{3,5},{4,6},{5,7},{6,0},{7,1},{8,10},{9,11},{10,... | collective-permute-start | bytes 479240 | tf_op jit(solution)/shard_map/ppermute | solution.py:190
  48.7 4.6 %collective-permute-start.3 = (bf16[2,3,104,128]{3,2,1,0:T(8,128)(2,1)S(1)}, bf16[2,3,104,128]{3,2,1,0:T(8,128)(2,1)S(1)}, u32[]{:S(2)}, u32[]{:S(2)}) collective-permute-start(bf16[2,3,104,128]{3,2,1,0:T(8,128)(2,1)S(1)} %get-tuple-element.12), channel_id=1, source_target_pairs={{0,5},{1,6},{2,7},{3,0},{4,1},{5,2},{6,3},{7,4},{8,13},{9,14},{10,... | collective-permute-start | bytes 479240 | tf_op jit(solution)/shard_map/ppermute | solution.py:190
  53.3 4.3 %collective-permute-start.2 = (bf16[2,3,104,128]{3,2,1,0:T(8,128)(2,1)S(1)}, bf16[2,3,104,128]{3,2,1,0:T(8,128)(2,1)S(1)}, u32[]{:S(2)}, u32[]{:S(2)}) collective-permute-start(bf16[2,3,104,128]{3,2,1,0:T(8,128)(2,1)S(1)} %get-tuple-element.13), channel_id=1, source_target_pairs={{0,3},{1,4},{2,5},{3,6},{4,7},{5,0},{6,1},{7,2},{8,11},{9,12},{10,... | collective-permute-start | bytes 479240 | tf_op jit(solution)/shard_map/ppermute | solution.py:190
  59.5 3.9 %collective-permute-start.14 = (bf16[2,3,104,128]{3,2,1,0:T(8,128)(2,1)S(1)}, bf16[2,3,104,128]{3,2,1,0:T(8,128)(2,1)S(1)}, u32[]{:S(2)}, u32[]{:S(2)}) collective-permute-start(bf16[2,3,104,128]{3,2,1,0:T(8,128)(2,1)S(1)} %collective-permute-done.6.refs_5_), channel_id=1, source_target_pairs={{0,8},{8,0},{1,9},{9,1},{2,10},{10,2},{3,11},{11,3},{4,12},{12,4},... | collective-permute-start | bytes 479240 | tf_op jit(solution)/shard_map/ppermute | solution.py:202
  66.1 3.2 %collective-permute-start.12 = (bf16[2,3,104,128]{3,2,1,0:T(8,128)(2,1)S(1)}, bf16[2,3,104,128]{3,2,1,0:T(8,128)(2,1)S(1)}, u32[]{:S(2)}, u32[]{:S(2)}) collective-permute-start(bf16[2,3,104,128]{3,2,1,0:T(8,128)(2,1)S(1)} %collective-permute-done.4.refs_3_), channel_id=1, source_target_pairs={{0,8},{8,0},{1,9},{9,1},{2,10},{10,2},{3,11},{11,3},{4,12},{12,4},... | collective-permute-start | bytes 479240 | tf_op jit(solution)/shard_map/ppermute | solution.py:202
  69.3 2.6 %collective-permute-done.2.refs_1_ = bf16[2,3,104,128]{3,2,1,0:T(8,128)(2,1)S(1)} collective-permute-done((bf16[2,3,104,128]{3,2,1,0:T(8,128)(2,1)S(1)}, bf16[2,3,104,128]{3,2,1,0:T(8,128)(2,1)S(1)}, u32[]{:S(2)}, u32[]{:S(2)}) %collective-permute-start.2) | collective-permute-done | bytes 159776 | tf_op jit(solution)/shard_map/ppermute | solution.py:190
  71.9 2.6 %collective-permute-start.11 = (bf16[2,3,104,128]{3,2,1,0:T(8,128)(2,1)S(1)}, bf16[2,3,104,128]{3,2,1,0:T(8,128)(2,1)S(1)}, u32[]{:S(2)}, u32[]{:S(2)}) collective-permute-start(bf16[2,3,104,128]{3,2,1,0:T(8,128)(2,1)S(1)} %collective-permute-done.3.refs_2_), channel_id=1, source_target_pairs={{0,8},{8,0},{1,9},{9,1},{2,10},{10,2},{3,11},{11,3},{4,12},{12,4},... | collective-permute-start | bytes 479240 | tf_op jit(solution)/shard_map/ppermute | solution.py:202
  74.5 3.2 %collective-permute-start.10 = (bf16[2,3,104,128]{3,2,1,0:T(8,128)(2,1)S(1)}, bf16[2,3,104,128]{3,2,1,0:T(8,128)(2,1)S(1)}, u32[]{:S(2)}, u32[]{:S(2)}) collective-permute-start(bf16[2,3,104,128]{3,2,1,0:T(8,128)(2,1)S(1)} %collective-permute-done.2.refs_1_), channel_id=1, source_target_pairs={{0,8},{8,0},{1,9},{9,1},{2,10},{10,2},{3,11},{11,3},{4,12},{12,4},... | collective-permute-start | bytes 479240 | tf_op jit(solution)/shard_map/ppermute | solution.py:202
  77.8 2.6 %collective-permute-start.9 = (bf16[2,3,104,128]{3,2,1,0:T(8,128)(2,1)S(1)}, bf16[2,3,104,128]{3,2,1,0:T(8,128)(2,1)}, u32[]{:S(2)}, u32[]{:S(2)}) collective-permute-start(bf16[2,3,104,128]{3,2,1,0:T(8,128)(2,1)S(1)} %collective-permute-done.1.first_ref.refs_0_), channel_id=1, source_target_pairs={{0,8},{8,0},{1,9},{9,1},{2,10},{10,2},{3,11},{11,3},{4,12},{12,4},... | collective-permute-start | bytes 479240 | tf_op jit(solution)/shard_map/ppermute | solution.py:202
  81.1 2.6 %collective-permute-done.10.refs_9_ = bf16[2,3,104,128]{3,2,1,0:T(8,128)(2,1)S(1)} collective-permute-done((bf16[2,3,104,128]{3,2,1,0:T(8,128)(2,1)S(1)}, bf16[2,3,104,128]{3,2,1,0:T(8,128)(2,1)S(1)}, u32[]{:S(2)}, u32[]{:S(2)}) %collective-permute-start.10) | collective-permute-done | bytes 159776 | tf_op jit(solution)/shard_map/ppermute | solution.py:202
  83.8 2.2 %collective-permute-done.9.refs_8_ = bf16[2,3,104,128]{3,2,1,0:T(8,128)(2,1)} collective-permute-done((bf16[2,3,104,128]{3,2,1,0:T(8,128)(2,1)S(1)}, bf16[2,3,104,128]{3,2,1,0:T(8,128)(2,1)}, u32[]{:S(2)}, u32[]{:S(2)}) %collective-permute-start.9) | collective-permute-done | bytes 159776 | tf_op jit(solution)/shard_map/ppermute | solution.py:202
  86.0 7.6 %prepare.1.y_ref = bf16[3,2048,256]{2,1,0:T(8,128)(2,1)} custom-call(s32[3]{0:T(128)S(1)} %get-tuple-element.20.place, bf16[2,8,3,104,128]{4,3,2,1,0:T(8,128)(2,1)S(1)} %bitcast.40, bf16[2,3,104,128]{3,2,1,0:T(8,128)(2,1)S(1)} %collective-permute-done.1.first_ref.refs_0_, bf16[2,3,104,128]{3,2,1,0:T(8,128)(2,1)S(1)} %collective-permute-done.2.refs_1_, ...), custom_call_target="tpu_custom_call" | custom-call | tf_op jit(solution)/shard_map/prepare/pallas_call | solution.py:203
  93.6 5.0 %all-gather.3.cloned.1.call-done.x_hbm = bf16[16,832,128]{2,1,0:T(8,128)(2,1)} async-done(((bf16[2,832,128]{2,1,0:T(8,128)(2,1)}), bf16[16,832,128]{2,1,0:T(8,128)(2,1)}) %all-gather.3.cloned.1.call-update) | async-done | bytes 3407888 | tf_op jit(solution)/shard_map/all_gather | solution.py:200
  100.4 7.1 %multiply.1 = (f32[2,8,3,2,56,128]{5,4,3,2,1,0:T(8,128)S(1)}, f32[32,128]{1,0:T(8,128)S(1)}) custom-call(s32[3]{0:T(128)S(1)} %get-tuple-element.19.place, bf16[16,832,128]{2,1,0:T(8,128)(2,1)} %all-gather.3.cloned.1.call-done.x_hbm, bf16[3,2048,256]{2,1,0:T(8,128)(2,1)S(1)} %copy-done), custom_call_target="tpu_custom_call" | custom-call | tf_op jit(solution)/shard_map/multiply/pallas_call | solution.py:212
  109.4 13.7 %all_to_all.16 = f32[32,1,128]{2,1,0:T(1,128)S(1)} all-to-all(f32[32,1,128]{2,1,0:T(1,128)S(1)} %bitcast.44), channel_id=1, replica_groups=mesh['z'=12,'xh'=2,'core'=2,'xl'=2,'y'=8] {'core','xl','y'}, dimensions={0} | all-to-all | bytes 32768 | tf_op jit(solution)/shard_map/all_to_all | solution.py:229
  123.2 2.2 %clip.1 = s16[3,8,2,48,128]{4,3,2,1,0:T(8,128)(2,1)S(1)} custom-call(s32[1]{0:T(128)} %bitcast.place, f32[32,128]{1,0:T(8,128)S(1)} %bitcast.43, f32[2,8,3,2,56,128]{5,4,3,2,1,0:T(8,128)S(1)} %get-tuple-element.6.keep_ref, f32[2,8,3,2,56,128]{5,4,3,2,1,0:T(8,128)S(1)} %collective-permute-done.16.got_ref), custom_call_target="tpu_custom_call" | custom-call | tf_op jit(solution)/shard_map/clip/pallas_call | solution.py:232
  125.3 43.8 %all_to_all.17 = s16[48,48,128]{2,1,0:T(8,128)(2,1)S(1)} all-to-all(s16[48,48,128]{2,1,0:T(8,128)(2,1)S(1)} %bitcast.41), channel_id=1, replica_groups=mesh['z'=12,'xh'=2,'core'=2,'xl'=2,'y'=8] {'z','xh','xl'}, dimensions={0} | all-to-all | bytes 1179648 | tf_op jit(solution)/shard_map/all_to_all | solution.py:247
  (36 shorter events, 14.4 us)
Async XLA Ops:
  7.2 91.4 %all-gather.3.cloned.1.call-start = ((), (), s32[]{:S(2)}) async-start(), calls=%async_computation.2 | async-start | bytes 3833856 | tf_op jit(solution)/shard_map/all_gather | solution.py:200
  8.2 77.8 %copy-start.1 = (bf16[1,1,16,312,128]{4,3,2,1,0:T(8,128)(2,1)S(1)}, bf16[1,1,16,312,128]{4,3,2,1,0:T(8,128)(2,1)}, u32[]{:S(2)}) copy-start(bf16[1,1,16,312,128]{4,3,2,1,0:T(8,128)(2,1)} %param.7) | copy-start | bytes 3833860
  9.3 19.0 %collective-permute-start = (bf16[832,128]{1,0:T(8,128)(2,1)S(1)}, bf16[832,128]{1,0:T(8,128)(2,1)S(1)}, u32[]{:S(2)}, u32[]{:S(2)}) collective-permute-start(bf16[832,128]{1,0:T(8,128)(2,1)S(1)} %pad_maximum_fusion.1), channel_id=1, source_target_pairs={{0,8},{8,0},{1,9},{9,1},{2,10},{10,2},{3,11},{11,3},{4,12},{12,4},... | collective-permute-start | bytes 638984 | tf_op jit(solution)/shard_map/ppermute | solution.py:183
  14.3 14.1 %collective-permute-start.1 = (bf16[2,3,104,128]{3,2,1,0:T(8,128)(2,1)S(1)}, bf16[2,3,104,128]{3,2,1,0:T(8,128)(2,1)S(1)}, u32[]{:S(2)}, u32[]{:S(2)}) collective-permute-start(bf16[2,3,104,128]{3,2,1,0:T(8,128)(2,1)S(1)} %get-tuple-element.14), channel_id=1, source_target_pairs={{0,4},{1,5},{2,6},{3,7},{4,0},{5,1},{6,2},{7,3},{8,12},{9,13},{10,... | collective-permute-start | bytes 479240 | tf_op jit(solution)/shard_map/ppermute | solution.py:190
  29.2 19.5 %collective-permute-start.8 = (bf16[2,3,104,128]{3,2,1,0:T(8,128)(2,1)S(1)}, bf16[2,3,104,128]{3,2,1,0:T(8,128)(2,1)S(1)}, u32[]{:S(2)}, u32[]{:S(2)}) collective-permute-start(bf16[2,3,104,128]{3,2,1,0:T(8,128)(2,1)S(1)} %get-tuple-element.7), channel_id=1, source_target_pairs={{0,8},{8,0},{1,9},{9,1},{2,10},{10,2},{3,11},{11,3},{4,12},{12,4},... | collective-permute-start | bytes 479240 | tf_op jit(solution)/shard_map/ppermute | solution.py:202
  31.6 21.7 %collective-permute-start.7 = (bf16[2,3,104,128]{3,2,1,0:T(8,128)(2,1)S(1)}, bf16[2,3,104,128]{3,2,1,0:T(8,128)(2,1)S(1)}, u32[]{:S(2)}, u32[]{:S(2)}) collective-permute-start(bf16[2,3,104,128]{3,2,1,0:T(8,128)(2,1)S(1)} %get-tuple-element.8), channel_id=1, source_target_pairs={{0,7},{1,0},{2,1},{3,2},{4,3},{5,4},{6,5},{7,6},{8,15},{9,8},{10,9... | collective-permute-start | bytes 479240 | tf_op jit(solution)/shard_map/ppermute | solution.py:190
  40.0 17.6 %collective-permute-start.6 = (bf16[2,3,104,128]{3,2,1,0:T(8,128)(2,1)S(1)}, bf16[2,3,104,128]{3,2,1,0:T(8,128)(2,1)S(1)}, u32[]{:S(2)}, u32[]{:S(2)}) collective-permute-start(bf16[2,3,104,128]{3,2,1,0:T(8,128)(2,1)S(1)} %get-tuple-element.9), channel_id=1, source_target_pairs={{0,1},{1,2},{2,3},{3,4},{4,5},{5,6},{6,7},{7,0},{8,9},{9,10},{10,1... | collective-permute-start | bytes 479240 | tf_op jit(solution)/shard_map/ppermute | solution.py:190
  41.9 17.6 %collective-permute-start.5 = (bf16[2,3,104,128]{3,2,1,0:T(8,128)(2,1)S(1)}, bf16[2,3,104,128]{3,2,1,0:T(8,128)(2,1)S(1)}, u32[]{:S(2)}, u32[]{:S(2)}) collective-permute-start(bf16[2,3,104,128]{3,2,1,0:T(8,128)(2,1)S(1)} %get-tuple-element.10), channel_id=1, source_target_pairs={{0,6},{1,7},{2,0},{3,1},{4,2},{5,3},{6,4},{7,5},{8,14},{9,15},{10,... | collective-permute-start | bytes 479240 | tf_op jit(solution)/shard_map/ppermute | solution.py:190
  46.5 16.9 %collective-permute-start.4 = (bf16[2,3,104,128]{3,2,1,0:T(8,128)(2,1)S(1)}, bf16[2,3,104,128]{3,2,1,0:T(8,128)(2,1)S(1)}, u32[]{:S(2)}, u32[]{:S(2)}) collective-permute-start(bf16[2,3,104,128]{3,2,1,0:T(8,128)(2,1)S(1)} %get-tuple-element.11), channel_id=1, source_target_pairs={{0,2},{1,3},{2,4},{3,5},{4,6},{5,7},{6,0},{7,1},{8,10},{9,11},{10,... | collective-permute-start | bytes 479240 | tf_op jit(solution)/shard_map/ppermute | solution.py:190
  48.7 17.4 %collective-permute-start.3 = (bf16[2,3,104,128]{3,2,1,0:T(8,128)(2,1)S(1)}, bf16[2,3,104,128]{3,2,1,0:T(8,128)(2,1)S(1)}, u32[]{:S(2)}, u32[]{:S(2)}) collective-permute-start(bf16[2,3,104,128]{3,2,1,0:T(8,128)(2,1)S(1)} %get-tuple-element.12), channel_id=1, source_target_pairs={{0,5},{1,6},{2,7},{3,0},{4,1},{5,2},{6,3},{7,4},{8,13},{9,14},{10,... | collective-permute-start | bytes 479240 | tf_op jit(solution)/shard_map/ppermute | solution.py:190
  53.3 18.6 %collective-permute-start.2 = (bf16[2,3,104,128]{3,2,1,0:T(8,128)(2,1)S(1)}, bf16[2,3,104,128]{3,2,1,0:T(8,128)(2,1)S(1)}, u32[]{:S(2)}, u32[]{:S(2)}) collective-permute-start(bf16[2,3,104,128]{3,2,1,0:T(8,128)(2,1)S(1)} %get-tuple-element.13), channel_id=1, source_target_pairs={{0,3},{1,4},{2,5},{3,6},{4,7},{5,0},{6,1},{7,2},{8,11},{9,12},{10,... | collective-permute-start | bytes 479240 | tf_op jit(solution)/shard_map/ppermute | solution.py:190
  57.6 16.9 %collective-permute-start.15 = (bf16[2,3,104,128]{3,2,1,0:T(8,128)(2,1)S(1)}, bf16[2,3,104,128]{3,2,1,0:T(8,128)(2,1)S(1)}, u32[]{:S(2)}, u32[]{:S(2)}) collective-permute-start(bf16[2,3,104,128]{3,2,1,0:T(8,128)(2,1)S(1)} %collective-permute-done.7.refs_6_), channel_id=1, source_target_pairs={{0,8},{8,0},{1,9},{9,1},{2,10},{10,2},{3,11},{11,3},{4,12},{12,4},... | collective-permute-start | bytes 479240 | tf_op jit(solution)/shard_map/ppermute | solution.py:202
  59.5 18.2 %collective-permute-start.14 = (bf16[2,3,104,128]{3,2,1,0:T(8,128)(2,1)S(1)}, bf16[2,3,104,128]{3,2,1,0:T(8,128)(2,1)S(1)}, u32[]{:S(2)}, u32[]{:S(2)}) collective-permute-start(bf16[2,3,104,128]{3,2,1,0:T(8,128)(2,1)S(1)} %collective-permute-done.6.refs_5_), channel_id=1, source_target_pairs={{0,8},{8,0},{1,9},{9,1},{2,10},{10,2},{3,11},{11,3},{4,12},{12,4},... | collective-permute-start | bytes 479240 | tf_op jit(solution)/shard_map/ppermute | solution.py:202
  63.5 17.7 %collective-permute-start.13 = (bf16[2,3,104,128]{3,2,1,0:T(8,128)(2,1)S(1)}, bf16[2,3,104,128]{3,2,1,0:T(8,128)(2,1)S(1)}, u32[]{:S(2)}, u32[]{:S(2)}) collective-permute-start(bf16[2,3,104,128]{3,2,1,0:T(8,128)(2,1)S(1)} %collective-permute-done.5.refs_4_), channel_id=1, source_target_pairs={{0,8},{8,0},{1,9},{9,1},{2,10},{10,2},{3,11},{11,3},{4,12},{12,4},... | collective-permute-start | bytes 479240 | tf_op jit(solution)/shard_map/ppermute | solution.py:202
  66.1 15.0 %collective-permute-start.12 = (bf16[2,3,104,128]{3,2,1,0:T(8,128)(2,1)S(1)}, bf16[2,3,104,128]{3,2,1,0:T(8,128)(2,1)S(1)}, u32[]{:S(2)}, u32[]{:S(2)}) collective-permute-start(bf16[2,3,104,128]{3,2,1,0:T(8,128)(2,1)S(1)} %collective-permute-done.4.refs_3_), channel_id=1, source_target_pairs={{0,8},{8,0},{1,9},{9,1},{2,10},{10,2},{3,11},{11,3},{4,12},{12,4},... | collective-permute-start | bytes 479240 | tf_op jit(solution)/shard_map/ppermute | solution.py:202
  71.9 9.3 %collective-permute-start.11 = (bf16[2,3,104,128]{3,2,1,0:T(8,128)(2,1)S(1)}, bf16[2,3,104,128]{3,2,1,0:T(8,128)(2,1)S(1)}, u32[]{:S(2)}, u32[]{:S(2)}) collective-permute-start(bf16[2,3,104,128]{3,2,1,0:T(8,128)(2,1)S(1)} %collective-permute-done.3.refs_2_), channel_id=1, source_target_pairs={{0,8},{8,0},{1,9},{9,1},{2,10},{10,2},{3,11},{11,3},{4,12},{12,4},... | collective-permute-start | bytes 479240 | tf_op jit(solution)/shard_map/ppermute | solution.py:202
  74.5 9.3 %collective-permute-start.10 = (bf16[2,3,104,128]{3,2,1,0:T(8,128)(2,1)S(1)}, bf16[2,3,104,128]{3,2,1,0:T(8,128)(2,1)S(1)}, u32[]{:S(2)}, u32[]{:S(2)}) collective-permute-start(bf16[2,3,104,128]{3,2,1,0:T(8,128)(2,1)S(1)} %collective-permute-done.2.refs_1_), channel_id=1, source_target_pairs={{0,8},{8,0},{1,9},{9,1},{2,10},{10,2},{3,11},{11,3},{4,12},{12,4},... | collective-permute-start | bytes 479240 | tf_op jit(solution)/shard_map/ppermute | solution.py:202
  77.8 8.2 %collective-permute-start.9 = (bf16[2,3,104,128]{3,2,1,0:T(8,128)(2,1)S(1)}, bf16[2,3,104,128]{3,2,1,0:T(8,128)(2,1)}, u32[]{:S(2)}, u32[]{:S(2)}) collective-permute-start(bf16[2,3,104,128]{3,2,1,0:T(8,128)(2,1)S(1)} %collective-permute-done.1.first_ref.refs_0_), channel_id=1, source_target_pairs={{0,8},{8,0},{1,9},{9,1},{2,10},{10,2},{3,11},{11,3},{4,12},{12,4},... | collective-permute-start | bytes 479240 | tf_op jit(solution)/shard_map/ppermute | solution.py:202
  98.5 1.9 %copy-start = (bf16[3,2048,256]{2,1,0:T(8,128)(2,1)S(1)}, bf16[3,2048,256]{2,1,0:T(8,128)(2,1)}, u32[]{:S(2)}) copy-start(bf16[3,2048,256]{2,1,0:T(8,128)(2,1)} %prepare.1.y_ref) | copy-start | bytes 9437188
  107.5 15.6 %collective-permute-start.16 = (f32[2,8,3,2,56,128]{5,4,3,2,1,0:T(8,128)S(1)}, f32[2,8,3,2,56,128]{5,4,3,2,1,0:T(8,128)S(1)}, u32[]{:S(2)}, u32[]{:S(2)}) collective-permute-start(f32[2,8,3,2,56,128]{5,4,3,2,1,0:T(8,128)S(1)} %get-tuple-element.6.keep_ref), channel_id=1, source_target_pairs={{0,16},{16,0},{1,17},{17,1},{2,18},{18,2},{3,19},{19,3},{4,20},{20... | collective-permute-start | bytes 8257544 | tf_op jit(solution)/shard_map/ppermute | solution.py:230
  123.1 46.0 %copy-start.2 = (f32[104,104]{1,0:T(8,128)S(1)}, f32[104,104]{1,0:T(8,128)}, u32[]{:S(2)}) copy-start(f32[104,104]{1,0:T(8,128)} %noise_ref.1) | copy-start | bytes 129796
  123.1 46.0 %copy-start.3 = (f32[104,104]{1,0:T(8,128)S(1)}, f32[104,104]{1,0:T(8,128)}, u32[]{:S(2)}) copy-start(f32[104,104]{1,0:T(8,128)} %first_ref.1) | copy-start | bytes 129796
  123.1 46.0 %copy-start.4 = (f32[104,104]{1,0:T(8,128)S(1)}, f32[104,104]{1,0:T(8,128)}, u32[]{:S(2)}) copy-start(f32[104,104]{1,0:T(8,128)} %second_ref.1) | copy-start | bytes 129796
Sparse Core Ops, SparseCore 0:
  29.3 69.1 all-gather.2

commit v4 on v3

--- a/solution.py
+++ b/solution.py
@@ -16,36 +16,31 @@
 SPARE = 24
 
 
-def stack_kernel(mine_ref, passed_ref, first_ref, out_ref):
+def stack_kernel(mine_ref, passed_ref, near_ref, far_ref, out_ref):
     out_ref[0] = mine_ref[...]
     out_ref[1] = passed_ref[...]
 
 
-def prepare_kernel(place, grads_hbm, *refs, shifts):
-    *pieces, out_ref, held, sems = refs
+def prepare_kernel(place, grads_ref, *refs, shifts):
+    *pieces, out_ref = refs
     part, ring, count = place[0], place[1], place[2]
-    rings = grads_hbm.shape[1]
-    size = grads_hbm.shape[3]
-    copies = [pltpu.make_async_copy(grads_hbm.at[:, ring], held.at[0], sems.at[0])]
-    for i, piece in enumerate(pieces):
-        copies.append(pltpu.make_async_copy(piece, held.at[i + 1], sems.at[i + 1]))
-    for copy in copies:
-        copy.start()
+    rings = grads_ref.shape[1]
+    size = grads_ref.shape[3]
     for j in range(3):
         for h in range(2):
             out_ref[j, :, h * LANES + size : (h + 1) * LANES] = jnp.zeros((out_ref.shape[1], LANES - size), out_ref.dtype)
-    for i, copy in enumerate(copies):
-        copy.wait()
+    for i in range(2 * rings):
         y = lax.rem(ring - shifts[i % rings] + rings, rings)
         row = i // rings
         live = (jnp.bitwise_xor(part, row) * rings + y < count).astype(jnp.float32).astype(jnp.bfloat16)
         at = pl.multiple_of((2 * y + row) * LANES, LANES)
         for h in range(2):
             for j in range(3):
-                out_ref[j, pl.ds(at, LANES), h * LANES : h * LANES + size] = (held[i, h, j] * live).T
-
-
-def multiply_kernel(place, x_hbm, y_ref, out_hbm, sum_ref, x_vmem, out_ref, sems, out_sems):
+                value = pieces[i - 1][h, j] if i else grads_ref[h, ring, j]
+                out_ref[j, pl.ds(at, LANES), h * LANES : h * LANES + size] = (value * live).T
+
+
+def multiply_kernel(place, x_hbm, y_ref, out_ref, sum_ref, x_vmem, sems):
     part, core, count = place[0], place[1], place[2]
     slabs = x_hbm.shape[0]
     blocks = out_ref.shape[1] // 2
@@ -77,12 +72,7 @@
                     out_ref[slot, first + b, j, h, :span] = acc[b * span : (b + 1) * span, h * LANES : (h + 1) * LANES]
                     if span < BIG:
                         out_ref[slot, first + b, j, h, span:] = jnp.zeros((BIG - span, LANES), jnp.float32)
-        some = pl.ds(first, blocks)
-        copies.append(pltpu.make_async_copy(out_ref.at[slot, some], out_hbm.at[slot, some], out_sems.at[t]))
-        copies[-1].start()
     sum_ref[...] = jnp.broadcast_to(jnp.sum(squares, keepdims=True), sum_ref.shape)
-    for copy in copies[len(tiles) :]:
-        copy.wait()
 
 
 def clip_kernel(place, norms_ref, keep_ref, got_ref, out_ref, *, clip, size):
@@ -171,6 +161,7 @@
     sigma = 0.2 * math.sqrt(images) / width
     smem = pl.BlockSpec(memory_space=pltpu.SMEM)
     vmem = pl.BlockSpec(memory_space=pltpu.VMEM)
+    hbm = pl.BlockSpec(memory_space=pltpu.HBM)
     swap = [(0, 1), (1, 0)]
 
     blocks = acts[0, 0].reshape(pairs, 2, size, tokens)
@@ -189,22 +180,21 @@
         heads = lax.dynamic_index_in_dim(grads, lax.rem(ring + shift, rings), 1, keepdims=False)
         return lax.ppermute(heads, "y", [(i, (i + shift) % rings) for i in range(rings)]) if shift else heads
 
-    shifts = (0, 4, 3, 5, 2, 6, 1, 7)
+    shifts = (0, 1, 7, 4, 3, 5, 2, 6)
     pieces = [shifted(shift) for shift in shifts]
     stacked = call(
         stack_kernel,
         jax.ShapeDtypeStruct((2,) + mine.shape, mine.dtype),
-        [vmem, vmem, pl.BlockSpec(memory_space=pl.ANY)],
+        [vmem, vmem, pl.BlockSpec(memory_space=pl.ANY), pl.BlockSpec(memory_space=pl.ANY)],
         name="stack",
-    )(mine, passed, pieces[1])
+    )(mine, passed, pieces[1], pieces[2])
     x = lax.all_gather(stacked, "y")
     x = x.reshape(augs, pairs * (BIG + SMALL), tokens)
     pieces = pieces[1:] + [lax.ppermute(piece, "xl", swap) for piece in pieces]
     y = call(
         functools.partial(prepare_kernel, shifts=shifts),
         jax.ShapeDtypeStruct((3, augs * tokens, 2 * LANES), jnp.bfloat16),
-        [smem] + [pl.BlockSpec(memory_space=pl.ANY)] * augs,
-        scratch_shapes=[pltpu.VMEM((augs, 2, 3, size, tokens), jnp.bfloat16), pltpu.SemaphoreType.DMA((augs,))],
+        [smem] + [vmem] * augs,
         name="prepare",
     )(jnp.stack([part, ring, aug_count[0]]), grads, *pieces)
 
@@ -215,14 +205,9 @@
             jax.ShapeDtypeStruct((2, pairs, 3, 2, BIG, LANES), jnp.float32),
             jax.ShapeDtypeStruct((group, LANES), jnp.float32),
         ],
-        [smem, pl.BlockSpec(memory_space=pl.ANY), vmem],
-        out_specs=[pl.BlockSpec(memory_space=pl.ANY), vmem],
-        scratch_shapes=[
-            pltpu.VMEM(x.shape, x.dtype),
-            pltpu.VMEM((2, pairs, 3, 2, BIG, LANES), jnp.float32),
-            pltpu.SemaphoreType.DMA((4,)),
-            pltpu.SemaphoreType.DMA((4,)),
-        ],
+        [smem, hbm, vmem],
+        out_specs=[vmem, vmem],
+        scratch_shapes=[pltpu.VMEM(x.shape, x.dtype), pltpu.SemaphoreType.DMA((4,))],
         name="multiply",
     )(jnp.stack([part, core, aug_count[0]]), x, y)
 

time: 178 us -> 175 us (0.983)
  Pallas kernels: 19.1 us -> 14.4 us
  waiting for transfers between devices: 20.4 us -> 24.1 us
    all_gather x1, waiting for transfers between devices: 4.95 us -> 12.1 us  [body(): x = lax.all_gather(stacked, 'y')]
    pallas_call x1, Pallas kernels: 7.58 us -> 3.94 us  [body(): call(functools.partial(prepare_kernel, shifts=shifts), jax.ShapeDtypeStru...]
    ppermute x7, starting transfers between devices: 32.7 us -> 30 us  [shifted(): lax.ppermute(heads, 'y', [(i, (i + shift) % rings) for i in range(rings)])]
    ppermute x8, waiting for transfers between devices: 4.86 us -> 3.03 us  [body(): pieces = pieces[1:] + [lax.ppermute(piece, 'xl', swap) for piece in pieces]]
  transfers between devices with their start and end apart: 18 -> 18, of which waited for: 6 -> 7; matrix products, arithmetic and copies ran while one was open for 1% -> 1% of each run, Pallas kernels for 4% -> 2%
where the time goes in v4:
time: 175 us; the launch traced here: 174 us
  starting transfers between devices  58.7 us (34%)
  blocking collectives  56.4 us (32%)
  waiting for transfers between devices  24.1 us (14%)
  between operations  15 us (9%)
  Pallas kernels  14.4 us (8%)
  local copies, waits for them, and re-layouts  5.46 us (3%)
    all_to_all x1, blocking collectives, body(): pieces = lax.all_to_all(pieces, ('z', 'xh', 'xl'), 0, 0, tiled=True)  43.2 us
    ppermute x7, starting transfers between devices, shifted(): lax.ppermute(heads, 'y', [(i, (i + shift) % rings) for i in range(rings)])  30 us
    ppermute x8, starting transfers between devices, body(): pieces = pieces[1:] + [lax.ppermute(piece, 'xl', swap) for piece in pieces]  23.3 us
    all_to_all x1, blocking collectives, body(): norms = lax.all_to_all(square, ('core', 'xl', 'y'), 0, 0, tiled=True)  13.3 us
    all_gather x1, waiting for transfers between devices, body(): x = lax.all_gather(stacked, 'y')  12.1 us
    ppermute x7, waiting for transfers between devices, shifted(): lax.ppermute(heads, 'y', [(i, (i + shift) % rings) for i in range(rings)])  8.86 us
    pallas_call x1, Pallas kernels, body(): call(multiply_kernel, [jax.ShapeDtypeStruct((2, pairs, 3, 2, BIG, LANES),...  6.09 us
    pallas_call x1, Pallas kernels, body(): call(functools.partial(prepare_kernel, shifts=shifts), jax.ShapeDtypeStru...  3.94 us
  transfers between devices with their start and end apart: 18, of which 7 were waited for; matrix products, arithmetic and copies ran while one was open for 1% of the time, Pallas kernels for 2%

profile of v4, /device:TPU:8, one launch (start us, length us, event | category | flops | bytes accessed | tf_op | source)
XLA Modules:
  0.0 174.2 jit_solution(7241501041418806420)
XLA Ops:
  9.3 3.4 %collective-permute-start = (bf16[832,128]{1,0:T(8,128)(2,1)S(1)}, bf16[832,128]{1,0:T(8,128)(2,1)S(1)}, u32[]{:S(2)}, u32[]{:S(2)}) collective-permute-start(bf16[832,128]{1,0:T(8,128)(2,1)S(1)} %pad_maximum_fusion.1), channel_id=1, source_target_pairs={{0,8},{8,0},{1,9},{9,1},{2,10},{10,2},{3,11},{11,3},{4,12},{12,4},... | collective-permute-start | bytes 638984 | tf_op jit(solution)/shard_map/ppermute | solution.py:174
  14.3 9.9 %collective-permute-start.2 = (bf16[2,3,104,128]{3,2,1,0:T(8,128)(2,1)S(1)}, bf16[2,3,104,128]{3,2,1,0:T(8,128)(2,1)S(1)}, u32[]{:S(2)}, u32[]{:S(2)}) collective-permute-start(bf16[2,3,104,128]{3,2,1,0:T(8,128)(2,1)S(1)} %get-tuple-element.13), channel_id=1, source_target_pairs={{0,7},{1,0},{2,1},{3,2},{4,3},{5,4},{6,5},{7,6},{8,15},{9,8},{10,9... | collective-permute-start | bytes 479240 | tf_op jit(solution)/shard_map/ppermute | solution.py:181
  24.2 1.9 %collective-permute-start.1 = (bf16[2,3,104,128]{3,2,1,0:T(8,128)(2,1)S(1)}, bf16[2,3,104,128]{3,2,1,0:T(8,128)(2,1)S(1)}, u32[]{:S(2)}, u32[]{:S(2)}) collective-permute-start(bf16[2,3,104,128]{3,2,1,0:T(8,128)(2,1)S(1)} %get-tuple-element.14), channel_id=1, source_target_pairs={{0,1},{1,2},{2,3},{3,4},{4,5},{5,6},{6,7},{7,0},{8,9},{9,10},{10,1... | collective-permute-start | bytes 479240 | tf_op jit(solution)/shard_map/ppermute | solution.py:181
  26.9 4.4 %collective-permute-done.1.near_ref.refs_0_ = bf16[2,3,104,128]{3,2,1,0:T(8,128)(2,1)S(1)} collective-permute-done((bf16[2,3,104,128]{3,2,1,0:T(8,128)(2,1)S(1)}, bf16[2,3,104,128]{3,2,1,0:T(8,128)(2,1)S(1)}, u32[]{:S(2)}, u32[]{:S(2)}) %collective-permute-start.1) | collective-permute-done | bytes 159776 | tf_op jit(solution)/shard_map/ppermute | solution.py:181
  32.2 3.9 %collective-permute-start.8 = (bf16[2,3,104,128]{3,2,1,0:T(8,128)(2,1)S(1)}, bf16[2,3,104,128]{3,2,1,0:T(8,128)(2,1)S(1)}, u32[]{:S(2)}, u32[]{:S(2)}) collective-permute-start(bf16[2,3,104,128]{3,2,1,0:T(8,128)(2,1)S(1)} %get-tuple-element.7), channel_id=1, source_target_pairs={{0,8},{8,0},{1,9},{9,1},{2,10},{10,2},{3,11},{11,3},{4,12},{12,4},... | collective-permute-start | bytes 479240 | tf_op jit(solution)/shard_map/ppermute | solution.py:193
  36.1 2.1 %collective-permute-start.7 = (bf16[2,3,104,128]{3,2,1,0:T(8,128)(2,1)S(1)}, bf16[2,3,104,128]{3,2,1,0:T(8,128)(2,1)S(1)}, u32[]{:S(2)}, u32[]{:S(2)}) collective-permute-start(bf16[2,3,104,128]{3,2,1,0:T(8,128)(2,1)S(1)} %get-tuple-element.8), channel_id=1, source_target_pairs={{0,6},{1,7},{2,0},{3,1},{4,2},{5,3},{6,4},{7,5},{8,14},{9,15},{10,... | collective-permute-start | bytes 479240 | tf_op jit(solution)/shard_map/ppermute | solution.py:181
  38.2 4.6 %collective-permute-start.6 = (bf16[2,3,104,128]{3,2,1,0:T(8,128)(2,1)S(1)}, bf16[2,3,104,128]{3,2,1,0:T(8,128)(2,1)S(1)}, u32[]{:S(2)}, u32[]{:S(2)}) collective-permute-start(bf16[2,3,104,128]{3,2,1,0:T(8,128)(2,1)S(1)} %get-tuple-element.9), channel_id=1, source_target_pairs={{0,2},{1,3},{2,4},{3,5},{4,6},{5,7},{6,0},{7,1},{8,10},{9,11},{10,... | collective-permute-start | bytes 479240 | tf_op jit(solution)/shard_map/ppermute | solution.py:181
  42.9 3.8 %collective-permute-start.5 = (bf16[2,3,104,128]{3,2,1,0:T(8,128)(2,1)S(1)}, bf16[2,3,104,128]{3,2,1,0:T(8,128)(2,1)S(1)}, u32[]{:S(2)}, u32[]{:S(2)}) collective-permute-start(bf16[2,3,104,128]{3,2,1,0:T(8,128)(2,1)S(1)} %get-tuple-element.10), channel_id=1, source_target_pairs={{0,5},{1,6},{2,7},{3,0},{4,1},{5,2},{6,3},{7,4},{8,13},{9,14},{10,... | collective-permute-start | bytes 479240 | tf_op jit(solution)/shard_map/ppermute | solution.py:181
  46.7 5.1 %collective-permute-start.4 = (bf16[2,3,104,128]{3,2,1,0:T(8,128)(2,1)S(1)}, bf16[2,3,104,128]{3,2,1,0:T(8,128)(2,1)S(1)}, u32[]{:S(2)}, u32[]{:S(2)}) collective-permute-start(bf16[2,3,104,128]{3,2,1,0:T(8,128)(2,1)S(1)} %get-tuple-element.11), channel_id=1, source_target_pairs={{0,3},{1,4},{2,5},{3,6},{4,7},{5,0},{6,1},{7,2},{8,11},{9,12},{10,... | collective-permute-start | bytes 479240 | tf_op jit(solution)/shard_map/ppermute | solution.py:181
  51.7 2.6 %collective-permute-start.3 = (bf16[2,3,104,128]{3,2,1,0:T(8,128)(2,1)S(1)}, bf16[2,3,104,128]{3,2,1,0:T(8,128)(2,1)S(1)}, u32[]{:S(2)}, u32[]{:S(2)}) collective-permute-start(bf16[2,3,104,128]{3,2,1,0:T(8,128)(2,1)S(1)} %get-tuple-element.12), channel_id=1, source_target_pairs={{0,4},{1,5},{2,6},{3,7},{4,0},{5,1},{6,2},{7,3},{8,12},{9,13},{10,... | collective-permute-start | bytes 479240 | tf_op jit(solution)/shard_map/ppermute | solution.py:181
  56.3 3.2 %collective-permute-done.6.refs_5_ = bf16[2,3,104,128]{3,2,1,0:T(8,128)(2,1)S(1)} collective-permute-done((bf16[2,3,104,128]{3,2,1,0:T(8,128)(2,1)S(1)}, bf16[2,3,104,128]{3,2,1,0:T(8,128)(2,1)S(1)}, u32[]{:S(2)}, u32[]{:S(2)}) %collective-permute-start.6) | collective-permute-done | bytes 159776 | tf_op jit(solution)/shard_map/ppermute | solution.py:181
  61.4 3.9 %collective-permute-start.10 = (bf16[2,3,104,128]{3,2,1,0:T(8,128)(2,1)S(1)}, bf16[2,3,104,128]{3,2,1,0:T(8,128)(2,1)S(1)}, u32[]{:S(2)}, u32[]{:S(2)}) collective-permute-start(bf16[2,3,104,128]{3,2,1,0:T(8,128)(2,1)S(1)} %collective-permute-done.2.far_ref.refs_1_), channel_id=1, source_target_pairs={{0,8},{8,0},{1,9},{9,1},{2,10},{10,2},{3,11},{11,3},{4,12},{12,4},... | collective-permute-start | bytes 479240 | tf_op jit(solution)/shard_map/ppermute | solution.py:193
  65.7 2.3 %collective-permute-start.13 = (bf16[2,3,104,128]{3,2,1,0:T(8,128)(2,1)S(1)}, bf16[2,3,104,128]{3,2,1,0:T(8,128)(2,1)S(1)}, u32[]{:S(2)}, u32[]{:S(2)}) collective-permute-start(bf16[2,3,104,128]{3,2,1,0:T(8,128)(2,1)S(1)} %collective-permute-done.5.refs_4_), channel_id=1, source_target_pairs={{0,8},{8,0},{1,9},{9,1},{2,10},{10,2},{3,11},{11,3},{4,12},{12,4},... | collective-permute-start | bytes 479240 | tf_op jit(solution)/shard_map/ppermute | solution.py:193
  68.1 3.5 %collective-permute-start.12 = (bf16[2,3,104,128]{3,2,1,0:T(8,128)(2,1)S(1)}, bf16[2,3,104,128]{3,2,1,0:T(8,128)(2,1)S(1)}, u32[]{:S(2)}, u32[]{:S(2)}) collective-permute-start(bf16[2,3,104,128]{3,2,1,0:T(8,128)(2,1)S(1)} %collective-permute-done.4.refs_3_), channel_id=1, source_target_pairs={{0,8},{8,0},{1,9},{9,1},{2,10},{10,2},{3,11},{11,3},{4,12},{12,4},... | collective-permute-start | bytes 479240 | tf_op jit(solution)/shard_map/ppermute | solution.py:193
  71.6 2.3 %collective-permute-start.11 = (bf16[2,3,104,128]{3,2,1,0:T(8,128)(2,1)S(1)}, bf16[2,3,104,128]{3,2,1,0:T(8,128)(2,1)S(1)}, u32[]{:S(2)}, u32[]{:S(2)}) collective-permute-start(bf16[2,3,104,128]{3,2,1,0:T(8,128)(2,1)S(1)} %collective-permute-done.3.refs_2_), channel_id=1, source_target_pairs={{0,8},{8,0},{1,9},{9,1},{2,10},{10,2},{3,11},{11,3},{4,12},{12,4},... | collective-permute-start | bytes 479240 | tf_op jit(solution)/shard_map/ppermute | solution.py:193
  74.0 3.5 %collective-permute-start.9 = (bf16[2,3,104,128]{3,2,1,0:T(8,128)(2,1)S(1)}, bf16[2,3,104,128]{3,2,1,0:T(8,128)(2,1)}, u32[]{:S(2)}, u32[]{:S(2)}) collective-permute-start(bf16[2,3,104,128]{3,2,1,0:T(8,128)(2,1)S(1)} %collective-permute-done.1.near_ref.refs_0_), channel_id=1, source_target_pairs={{0,8},{8,0},{1,9},{9,1},{2,10},{10,2},{3,11},{11,3},{4,12},{12,4},... | collective-permute-start | bytes 479240 | tf_op jit(solution)/shard_map/ppermute | solution.py:193
  78.8 2.5 %collective-permute-done.9.refs_8_ = bf16[2,3,104,128]{3,2,1,0:T(8,128)(2,1)} collective-permute-done((bf16[2,3,104,128]{3,2,1,0:T(8,128)(2,1)S(1)}, bf16[2,3,104,128]{3,2,1,0:T(8,128)(2,1)}, u32[]{:S(2)}, u32[]{:S(2)}) %collective-permute-start.9) | collective-permute-done | bytes 159776 | tf_op jit(solution)/shard_map/ppermute | solution.py:193
  81.2 3.9 %prepare.1.y_ref = bf16[3,2048,256]{2,1,0:T(8,128)(2,1)} custom-call(s32[3]{0:T(128)S(1)} %get-tuple-element.20.place, bf16[2,8,3,104,128]{4,3,2,1,0:T(8,128)(2,1)S(1)} %bitcast.40, bf16[2,3,104,128]{3,2,1,0:T(8,128)(2,1)S(1)} %collective-permute-done.1.near_ref.refs_0_, bf16[2,3,104,128]{3,2,1,0:T(8,128)(2,1)S(1)} %collective-permute-done.2.far_ref.refs_1_, ...), custom_call_target="tpu_custom_call" | custom-call | tf_op jit(solution)/shard_map/prepare/pallas_call | solution.py:194
  85.2 12.1 %all-gather.3.cloned.1.call-done.x_hbm = bf16[16,832,128]{2,1,0:T(8,128)(2,1)} async-done(((bf16[2,832,128]{2,1,0:T(8,128)(2,1)}), bf16[16,832,128]{2,1,0:T(8,128)(2,1)}) %all-gather.3.cloned.1.call-update) | async-done | bytes 3407888 | tf_op jit(solution)/shard_map/all_gather | solution.py:191
  99.2 6.1 %multiply.1 = (f32[2,8,3,2,56,128]{5,4,3,2,1,0:T(8,128)S(1)}, f32[32,128]{1,0:T(8,128)S(1)}) custom-call(s32[3]{0:T(128)S(1)} %get-tuple-element.19.place, bf16[16,832,128]{2,1,0:T(8,128)(2,1)} %all-gather.3.cloned.1.call-done.x_hbm, bf16[3,2048,256]{2,1,0:T(8,128)(2,1)S(1)} %copy-done), custom_call_target="tpu_custom_call" | custom-call | tf_op jit(solution)/shard_map/multiply/pallas_call | solution.py:202
  105.3 1.9 %collective-permute-start.16 = (f32[2,8,3,2,56,128]{5,4,3,2,1,0:T(8,128)S(1)}, f32[2,8,3,2,56,128]{5,4,3,2,1,0:T(8,128)S(1)}, u32[]{:S(2)}, u32[]{:S(2)}) collective-permute-start(f32[2,8,3,2,56,128]{5,4,3,2,1,0:T(8,128)S(1)} %get-tuple-element.6.keep_ref), channel_id=1, source_target_pairs={{0,16},{16,0},{1,17},{17,1},{2,18},{18,2},{3,19},{19,3},{4,20},{20... | collective-permute-start | bytes 8257544 | tf_op jit(solution)/shard_map/ppermute | solution.py:215
  107.2 13.3 %all_to_all.16 = f32[32,1,128]{2,1,0:T(1,128)S(1)} all-to-all(f32[32,1,128]{2,1,0:T(1,128)S(1)} %bitcast.44), channel_id=1, replica_groups=mesh['z'=12,'xh'=2,'core'=2,'xl'=2,'y'=8] {'core','xl','y'}, dimensions={0} | all-to-all | bytes 32768 | tf_op jit(solution)/shard_map/all_to_all | solution.py:214
  120.5 2.2 %clip.1 = s16[3,8,2,48,128]{4,3,2,1,0:T(8,128)(2,1)S(1)} custom-call(s32[1]{0:T(128)} %bitcast.place, f32[32,128]{1,0:T(8,128)S(1)} %bitcast.43, f32[2,8,3,2,56,128]{5,4,3,2,1,0:T(8,128)S(1)} %get-tuple-element.6.keep_ref, f32[2,8,3,2,56,128]{5,4,3,2,1,0:T(8,128)S(1)} %collective-permute-done.16.got_ref), custom_call_target="tpu_custom_call" | custom-call | tf_op jit(solution)/shard_map/clip/pallas_call | solution.py:217
  122.7 43.2 %all_to_all.17 = s16[48,48,128]{2,1,0:T(8,128)(2,1)S(1)} all-to-all(s16[48,48,128]{2,1,0:T(8,128)(2,1)S(1)} %bitcast.41), channel_id=1, replica_groups=mesh['z'=12,'xh'=2,'core'=2,'xl'=2,'y'=8] {'z','xh','xl'}, dimensions={0} | all-to-all | bytes 1179648 | tf_op jit(solution)/shard_map/all_to_all | solution.py:232
  (36 shorter events, 13.5 us)
Async XLA Ops:
  7.2 90.2 %all-gather.3.cloned.1.call-start = ((), (), s32[]{:S(2)}) async-start(), calls=%async_computation.2 | async-start | bytes 3833856 | tf_op jit(solution)/shard_map/all_gather | solution.py:191
  8.2 73.1 %copy-start.1 = (bf16[1,1,16,312,128]{4,3,2,1,0:T(8,128)(2,1)S(1)}, bf16[1,1,16,312,128]{4,3,2,1,0:T(8,128)(2,1)}, u32[]{:S(2)}) copy-start(bf16[1,1,16,312,128]{4,3,2,1,0:T(8,128)(2,1)} %param.7) | copy-start | bytes 3833860
  9.3 22.0 %collective-permute-start = (bf16[832,128]{1,0:T(8,128)(2,1)S(1)}, bf16[832,128]{1,0:T(8,128)(2,1)S(1)}, u32[]{:S(2)}, u32[]{:S(2)}) collective-permute-start(bf16[832,128]{1,0:T(8,128)(2,1)S(1)} %pad_maximum_fusion.1), channel_id=1, source_target_pairs={{0,8},{8,0},{1,9},{9,1},{2,10},{10,2},{3,11},{11,3},{4,12},{12,4},... | collective-permute-start | bytes 638984 | tf_op jit(solution)/shard_map/ppermute | solution.py:174
  14.3 12.7 %collective-permute-start.2 = (bf16[2,3,104,128]{3,2,1,0:T(8,128)(2,1)S(1)}, bf16[2,3,104,128]{3,2,1,0:T(8,128)(2,1)S(1)}, u32[]{:S(2)}, u32[]{:S(2)}) collective-permute-start(bf16[2,3,104,128]{3,2,1,0:T(8,128)(2,1)S(1)} %get-tuple-element.13), channel_id=1, source_target_pairs={{0,7},{1,0},{2,1},{3,2},{4,3},{5,4},{6,5},{7,6},{8,15},{9,8},{10,9... | collective-permute-start | bytes 479240 | tf_op jit(solution)/shard_map/ppermute | solution.py:181
  24.2 7.2 %collective-permute-start.1 = (bf16[2,3,104,128]{3,2,1,0:T(8,128)(2,1)S(1)}, bf16[2,3,104,128]{3,2,1,0:T(8,128)(2,1)S(1)}, u32[]{:S(2)}, u32[]{:S(2)}) collective-permute-start(bf16[2,3,104,128]{3,2,1,0:T(8,128)(2,1)S(1)} %get-tuple-element.14), channel_id=1, source_target_pairs={{0,1},{1,2},{2,3},{3,4},{4,5},{5,6},{6,7},{7,0},{8,9},{9,10},{10,1... | collective-permute-start | bytes 479240 | tf_op jit(solution)/shard_map/ppermute | solution.py:181
  32.2 19.6 %collective-permute-start.8 = (bf16[2,3,104,128]{3,2,1,0:T(8,128)(2,1)S(1)}, bf16[2,3,104,128]{3,2,1,0:T(8,128)(2,1)S(1)}, u32[]{:S(2)}, u32[]{:S(2)}) collective-permute-start(bf16[2,3,104,128]{3,2,1,0:T(8,128)(2,1)S(1)} %get-tuple-element.7), channel_id=1, source_target_pairs={{0,8},{8,0},{1,9},{9,1},{2,10},{10,2},{3,11},{11,3},{4,12},{12,4},... | collective-permute-start | bytes 479240 | tf_op jit(solution)/shard_map/ppermute | solution.py:193
  36.1 18.2 %collective-permute-start.7 = (bf16[2,3,104,128]{3,2,1,0:T(8,128)(2,1)S(1)}, bf16[2,3,104,128]{3,2,1,0:T(8,128)(2,1)S(1)}, u32[]{:S(2)}, u32[]{:S(2)}) collective-permute-start(bf16[2,3,104,128]{3,2,1,0:T(8,128)(2,1)S(1)} %get-tuple-element.8), channel_id=1, source_target_pairs={{0,6},{1,7},{2,0},{3,1},{4,2},{5,3},{6,4},{7,5},{8,14},{9,15},{10,... | collective-permute-start | bytes 479240 | tf_op jit(solution)/shard_map/ppermute | solution.py:181
  38.2 21.2 %collective-permute-start.6 = (bf16[2,3,104,128]{3,2,1,0:T(8,128)(2,1)S(1)}, bf16[2,3,104,128]{3,2,1,0:T(8,128)(2,1)S(1)}, u32[]{:S(2)}, u32[]{:S(2)}) collective-permute-start(bf16[2,3,104,128]{3,2,1,0:T(8,128)(2,1)S(1)} %get-tuple-element.9), channel_id=1, source_target_pairs={{0,2},{1,3},{2,4},{3,5},{4,6},{5,7},{6,0},{7,1},{8,10},{9,11},{10,... | collective-permute-start | bytes 479240 | tf_op jit(solution)/shard_map/ppermute | solution.py:181
  42.9 18.5 %collective-permute-start.5 = (bf16[2,3,104,128]{3,2,1,0:T(8,128)(2,1)S(1)}, bf16[2,3,104,128]{3,2,1,0:T(8,128)(2,1)S(1)}, u32[]{:S(2)}, u32[]{:S(2)}) collective-permute-start(bf16[2,3,104,128]{3,2,1,0:T(8,128)(2,1)S(1)} %get-tuple-element.10), channel_id=1, source_target_pairs={{0,5},{1,6},{2,7},{3,0},{4,1},{5,2},{6,3},{7,4},{8,13},{9,14},{10,... | collective-permute-start | bytes 479240 | tf_op jit(solution)/shard_map/ppermute | solution.py:181
  46.7 19.1 %collective-permute-start.4 = (bf16[2,3,104,128]{3,2,1,0:T(8,128)(2,1)S(1)}, bf16[2,3,104,128]{3,2,1,0:T(8,128)(2,1)S(1)}, u32[]{:S(2)}, u32[]{:S(2)}) collective-permute-start(bf16[2,3,104,128]{3,2,1,0:T(8,128)(2,1)S(1)} %get-tuple-element.11), channel_id=1, source_target_pairs={{0,3},{1,4},{2,5},{3,6},{4,7},{5,0},{6,1},{7,2},{8,11},{9,12},{10,... | collective-permute-start | bytes 479240 | tf_op jit(solution)/shard_map/ppermute | solution.py:181
  51.7 16.4 %collective-permute-start.3 = (bf16[2,3,104,128]{3,2,1,0:T(8,128)(2,1)S(1)}, bf16[2,3,104,128]{3,2,1,0:T(8,128)(2,1)S(1)}, u32[]{:S(2)}, u32[]{:S(2)}) collective-permute-start(bf16[2,3,104,128]{3,2,1,0:T(8,128)(2,1)S(1)} %get-tuple-element.12), channel_id=1, source_target_pairs={{0,4},{1,5},{2,6},{3,7},{4,0},{5,1},{6,2},{7,3},{8,12},{9,13},{10,... | collective-permute-start | bytes 479240 | tf_op jit(solution)/shard_map/ppermute | solution.py:181
  54.3 17.3 %collective-permute-start.15 = (bf16[2,3,104,128]{3,2,1,0:T(8,128)(2,1)S(1)}, bf16[2,3,104,128]{3,2,1,0:T(8,128)(2,1)S(1)}, u32[]{:S(2)}, u32[]{:S(2)}) collective-permute-start(bf16[2,3,104,128]{3,2,1,0:T(8,128)(2,1)S(1)} %collective-permute-done.7.refs_6_), channel_id=1, source_target_pairs={{0,8},{8,0},{1,9},{9,1},{2,10},{10,2},{3,11},{11,3},{4,12},{12,4},... | collective-permute-start | bytes 479240 | tf_op jit(solution)/shard_map/ppermute | solution.py:193
  59.4 14.5 %collective-permute-start.14 = (bf16[2,3,104,128]{3,2,1,0:T(8,128)(2,1)S(1)}, bf16[2,3,104,128]{3,2,1,0:T(8,128)(2,1)S(1)}, u32[]{:S(2)}, u32[]{:S(2)}) collective-permute-start(bf16[2,3,104,128]{3,2,1,0:T(8,128)(2,1)S(1)} %collective-permute-done.6.refs_5_), channel_id=1, source_target_pairs={{0,8},{8,0},{1,9},{9,1},{2,10},{10,2},{3,11},{11,3},{4,12},{12,4},... | collective-permute-start | bytes 479240 | tf_op jit(solution)/shard_map/ppermute | solution.py:193
  61.4 17.4 %collective-permute-start.10 = (bf16[2,3,104,128]{3,2,1,0:T(8,128)(2,1)S(1)}, bf16[2,3,104,128]{3,2,1,0:T(8,128)(2,1)S(1)}, u32[]{:S(2)}, u32[]{:S(2)}) collective-permute-start(bf16[2,3,104,128]{3,2,1,0:T(8,128)(2,1)S(1)} %collective-permute-done.2.far_ref.refs_1_), channel_id=1, source_target_pairs={{0,8},{8,0},{1,9},{9,1},{2,10},{10,2},{3,11},{11,3},{4,12},{12,4},... | collective-permute-start | bytes 479240 | tf_op jit(solution)/shard_map/ppermute | solution.py:193
  65.7 12.5 %collective-permute-start.13 = (bf16[2,3,104,128]{3,2,1,0:T(8,128)(2,1)S(1)}, bf16[2,3,104,128]{3,2,1,0:T(8,128)(2,1)S(1)}, u32[]{:S(2)}, u32[]{:S(2)}) collective-permute-start(bf16[2,3,104,128]{3,2,1,0:T(8,128)(2,1)S(1)} %collective-permute-done.5.refs_4_), channel_id=1, source_target_pairs={{0,8},{8,0},{1,9},{9,1},{2,10},{10,2},{3,11},{11,3},{4,12},{12,4},... | collective-permute-start | bytes 479240 | tf_op jit(solution)/shard_map/ppermute | solution.py:193
  68.1 10.1 %collective-permute-start.12 = (bf16[2,3,104,128]{3,2,1,0:T(8,128)(2,1)S(1)}, bf16[2,3,104,128]{3,2,1,0:T(8,128)(2,1)S(1)}, u32[]{:S(2)}, u32[]{:S(2)}) collective-permute-start(bf16[2,3,104,128]{3,2,1,0:T(8,128)(2,1)S(1)} %collective-permute-done.4.refs_3_), channel_id=1, source_target_pairs={{0,8},{8,0},{1,9},{9,1},{2,10},{10,2},{3,11},{11,3},{4,12},{12,4},... | collective-permute-start | bytes 479240 | tf_op jit(solution)/shard_map/ppermute | solution.py:193
  71.6 7.2 %collective-permute-start.11 = (bf16[2,3,104,128]{3,2,1,0:T(8,128)(2,1)S(1)}, bf16[2,3,104,128]{3,2,1,0:T(8,128)(2,1)S(1)}, u32[]{:S(2)}, u32[]{:S(2)}) collective-permute-start(bf16[2,3,104,128]{3,2,1,0:T(8,128)(2,1)S(1)} %collective-permute-done.3.refs_2_), channel_id=1, source_target_pairs={{0,8},{8,0},{1,9},{9,1},{2,10},{10,2},{3,11},{11,3},{4,12},{12,4},... | collective-permute-start | bytes 479240 | tf_op jit(solution)/shard_map/ppermute | solution.py:193
  74.0 7.3 %collective-permute-start.9 = (bf16[2,3,104,128]{3,2,1,0:T(8,128)(2,1)S(1)}, bf16[2,3,104,128]{3,2,1,0:T(8,128)(2,1)}, u32[]{:S(2)}, u32[]{:S(2)}) collective-permute-start(bf16[2,3,104,128]{3,2,1,0:T(8,128)(2,1)S(1)} %collective-permute-done.1.near_ref.refs_0_), channel_id=1, source_target_pairs={{0,8},{8,0},{1,9},{9,1},{2,10},{10,2},{3,11},{11,3},{4,12},{12,4},... | collective-permute-start | bytes 479240 | tf_op jit(solution)/shard_map/ppermute | solution.py:193
  97.3 1.9 %copy-start = (bf16[3,2048,256]{2,1,0:T(8,128)(2,1)S(1)}, bf16[3,2048,256]{2,1,0:T(8,128)(2,1)}, u32[]{:S(2)}) copy-start(bf16[3,2048,256]{2,1,0:T(8,128)(2,1)} %prepare.1.y_ref) | copy-start | bytes 9437188
  105.3 15.2 %collective-permute-start.16 = (f32[2,8,3,2,56,128]{5,4,3,2,1,0:T(8,128)S(1)}, f32[2,8,3,2,56,128]{5,4,3,2,1,0:T(8,128)S(1)}, u32[]{:S(2)}, u32[]{:S(2)}) collective-permute-start(f32[2,8,3,2,56,128]{5,4,3,2,1,0:T(8,128)S(1)} %get-tuple-element.6.keep_ref), channel_id=1, source_target_pairs={{0,16},{16,0},{1,17},{17,1},{2,18},{18,2},{3,19},{19,3},{4,20},{20... | collective-permute-start | bytes 8257544 | tf_op jit(solution)/shard_map/ppermute | solution.py:215
  120.5 45.4 %copy-start.2 = (f32[104,104]{1,0:T(8,128)S(1)}, f32[104,104]{1,0:T(8,128)}, u32[]{:S(2)}) copy-start(f32[104,104]{1,0:T(8,128)} %noise_ref.1) | copy-start | bytes 129796
  120.5 45.4 %copy-start.3 = (f32[104,104]{1,0:T(8,128)S(1)}, f32[104,104]{1,0:T(8,128)}, u32[]{:S(2)}) copy-start(f32[104,104]{1,0:T(8,128)} %first_ref.1) | copy-start | bytes 129796
  120.5 45.4 %copy-start.4 = (f32[104,104]{1,0:T(8,128)S(1)}, f32[104,104]{1,0:T(8,128)}, u32[]{:S(2)}) copy-start(f32[104,104]{1,0:T(8,128)} %second_ref.1) | copy-start | bytes 129796
Sparse Core Ops, SparseCore 0:
  32.3 64.9 all-gather.2

commit v5 on v4

--- a/solution.py
+++ b/solution.py
@@ -12,13 +12,9 @@
 LANES = 128
 TOP = 32767.0
 VMEM = 48 * 1024 * 1024
+MOST_VMEM = 51200 * 1024
 BIG, SMALL = 56, 48
 SPARE = 24
-
-
-def stack_kernel(mine_ref, passed_ref, near_ref, far_ref, out_ref):
-    out_ref[0] = mine_ref[...]
-    out_ref[1] = passed_ref[...]
 
 
 def prepare_kernel(place, grads_ref, *refs, shifts):
@@ -40,7 +36,7 @@
                 out_ref[j, pl.ds(at, LANES), h * LANES : h * LANES + size] = (value * live).T
 
 
-def multiply_kernel(place, x_hbm, y_ref, out_ref, sum_ref, x_vmem, sems):
+def multiply_kernel(place, x_hbm, y_hbm, out_ref, sum_ref, x_vmem, y_vmem, sems, y_sems):
     part, core, count = place[0], place[1], place[2]
     slabs = x_hbm.shape[0]
     blocks = out_ref.shape[1] // 2
@@ -54,7 +50,12 @@
     for t, (row, span, _) in enumerate(tiles):
         rows = pl.ds(row, blocks * span)
         copies.append(pltpu.make_async_copy(x_hbm.at[:, rows], x_vmem.at[:, rows], sems.at[t]))
-        copies[-1].start()
+    y_copies = [pltpu.make_async_copy(y_hbm.at[j], y_vmem.at[j], y_sems.at[j]) for j in range(3)]
+    copies[0].start()
+    for copy in y_copies:
+        copy.start()
+    for copy in copies[1:]:
+        copy.start()
     scale = 1.0 / count.astype(jnp.float32)
     big_slot = (part != core).astype(jnp.int32)
     squares = jnp.zeros((8, LANES), jnp.float32)
@@ -64,7 +65,9 @@
         x = jnp.concatenate([x_vmem[k, row : row + rows] for k in range(slabs)], axis=1)
         slot = big_slot if span == BIG else 1 - big_slot
         for j in range(3):
-            acc = jnp.dot(x, y_ref[j], preferred_element_type=jnp.float32) * scale
+            if t == 0:
+                y_copies[j].wait()
+            acc = jnp.dot(x, y_vmem[j], preferred_element_type=jnp.float32) * scale
             square = jnp.sum((acc * acc).reshape(rows // 8, 8, 2 * LANES), axis=0)
             squares += square[:, :LANES] + square[:, LANES:]
             for b in range(blocks):
@@ -138,12 +141,12 @@
     new_second_ref[...] = 0.999 * second_ref[...] + 0.001 * grad * grad
 
 
-def call(kernel, out_shape, in_specs, **kw):
+def call(kernel, out_shape, in_specs, limit=VMEM, **kw):
     return pl.pallas_call(
         kernel,
         in_specs=in_specs,
         out_shape=out_shape,
-        compiler_params=pltpu.CompilerParams(vmem_limit_bytes=VMEM),
+        compiler_params=pltpu.CompilerParams(vmem_limit_bytes=limit),
         **kw,
     )
 
@@ -180,15 +183,9 @@
         heads = lax.dynamic_index_in_dim(grads, lax.rem(ring + shift, rings), 1, keepdims=False)
         return lax.ppermute(heads, "y", [(i, (i + shift) % rings) for i in range(rings)]) if shift else heads
 
-    shifts = (0, 1, 7, 4, 3, 5, 2, 6)
+    shifts = (0, 4, 3, 5, 2, 6, 1, 7)
     pieces = [shifted(shift) for shift in shifts]
-    stacked = call(
-        stack_kernel,
-        jax.ShapeDtypeStruct((2,) + mine.shape, mine.dtype),
-        [vmem, vmem, pl.BlockSpec(memory_space=pl.ANY), pl.BlockSpec(memory_space=pl.ANY)],
-        name="stack",
-    )(mine, passed, pieces[1], pieces[2])
-    x = lax.all_gather(stacked, "y")
+    x = lax.all_gather(jnp.stack([mine, passed]), "y")
     x = x.reshape(augs, pairs * (BIG + SMALL), tokens)
     pieces = pieces[1:] + [lax.ppermute(piece, "xl", swap) for piece in pieces]
     y = call(
@@ -205,9 +202,15 @@
             jax.ShapeDtypeStruct((2, pairs, 3, 2, BIG, LANES), jnp.float32),
             jax.ShapeDtypeStruct((group, LANES), jnp.float32),
         ],
-        [smem, hbm, vmem],
+        [smem, hbm, hbm],
         out_specs=[vmem, vmem],
-        scratch_shapes=[pltpu.VMEM(x.shape, x.dtype), pltpu.SemaphoreType.DMA((4,))],
+        scratch_shapes=[
+            pltpu.VMEM(x.shape, x.dtype),
+            pltpu.VMEM(y.shape, y.dtype),
+            pltpu.SemaphoreType.DMA((4,)),
+            pltpu.SemaphoreType.DMA((3,)),
+        ],
+        limit=MOST_VMEM,
         name="multiply",
     )(jnp.stack([part, core, aug_count[0]]), x, y)
 

time: 175 us -> 173 us (0.989)
  starting transfers between devices: 58.7 us -> 63.3 us
  waiting for transfers between devices: 24.1 us -> 20.2 us
  local copies, waits for them, and re-layouts: 5.46 us -> 2.21 us
    ppermute x7, waiting for transfers between devices: 8.86 us -> 2.65 us  [shifted(): lax.ppermute(heads, 'y', [(i, (i + shift) % rings) for i in range(rings)])]
    ppermute x1, waiting for transfers between devices: 0.01 us -> 5.45 us  [body(): passed = lax.ppermute(half_of(1 - part), 'xl', swap)]
    all_gather x1, waiting for transfers between devices: 12.1 us -> 6.93 us  [body(): x = lax.all_gather(jnp.stack([mine, passed]), 'y')]
    ppermute x8, starting transfers between devices: 23.3 us -> 27 us  [body(): pieces = pieces[1:] + [lax.ppermute(piece, 'xl', swap) for piece in pieces]]
    ppermute x8, waiting for transfers between devices: 3.03 us -> 5.19 us  [body(): pieces = pieces[1:] + [lax.ppermute(piece, 'xl', swap) for piece in pieces]]
    unnamed x10 -> x8, local copies, waits for them, and re-layouts: 1.91 us -> 0.02 us
  transfers between devices with their start and end apart: 18 -> 18, of which waited for: 7 -> 6; matrix products, arithmetic and copies ran while one was open for 1% -> 0% of each run, Pallas kernels for 2% -> 2%
where the time goes in v5:
time: 173 us; the launch traced here: 172 us
  starting transfers between devices  63.3 us (37%)
  blocking collectives  55.8 us (32%)
  waiting for transfers between devices  20.2 us (12%)
  between operations  15 us (9%)
  Pallas kernels  14.8 us (9%)
  local copies, waits for them, and re-layouts  2.21 us (1%)
    all_to_all x1, blocking collectives, body(): pieces = lax.all_to_all(pieces, ('z', 'xh', 'xl'), 0, 0, tiled=True)  42.8 us
    ppermute x7, starting transfers between devices, shifted(): lax.ppermute(heads, 'y', [(i, (i + shift) % rings) for i in range(rings)])  31 us
    ppermute x8, starting transfers between devices, body(): pieces = pieces[1:] + [lax.ppermute(piece, 'xl', swap) for piece in pieces]  27 us
    all_to_all x1, blocking collectives, body(): norms = lax.all_to_all(square, ('core', 'xl', 'y'), 0, 0, tiled=True)  13 us
    pallas_call x1, Pallas kernels, body(): call(multiply_kernel, [jax.ShapeDtypeStruct((2, pairs, 3, 2, BIG, LANES),...  7.2 us
    all_gather x1, waiting for transfers between devices, body(): x = lax.all_gather(jnp.stack([mine, passed]), 'y')  6.93 us
    ppermute x1, waiting for transfers between devices, body(): passed = lax.ppermute(half_of(1 - part), 'xl', swap)  5.45 us
    ppermute x8, waiting for transfers between devices, body(): pieces = pieces[1:] + [lax.ppermute(piece, 'xl', swap) for piece in pieces]  5.19 us
  transfers between devices with their start and end apart: 18, of which 6 were waited for; matrix products, arithmetic and copies ran while one was open for 0% of the time, Pallas kernels for 2%

profile of v5, /device:TPU:8, one launch (start us, length us, event | category | flops | bytes accessed | tf_op | source)
XLA Modules:
  0.0 172.3 jit_solution(13002592139339538227)
XLA Ops:
  9.3 3.4 %collective-permute-start = (bf16[832,128]{1,0:T(8,128)(2,1)S(1)}, bf16[832,128]{1,0:T(8,128)(2,1)S(1)}, u32[]{:S(2)}, u32[]{:S(2)}) collective-permute-start(bf16[832,128]{1,0:T(8,128)(2,1)S(1)} %pad_maximum_fusion.1), channel_id=1, source_target_pairs={{0,8},{8,0},{1,9},{9,1},{2,10},{10,2},{3,11},{11,3},{4,12},{12,4},... | collective-permute-start | bytes 638984 | tf_op jit(solution)/shard_map/ppermute | solution.py:177
  12.7 5.5 %collective-permute-done = bf16[832,128]{1,0:T(8,128)(2,1)S(1)} collective-permute-done((bf16[832,128]{1,0:T(8,128)(2,1)S(1)}, bf16[832,128]{1,0:T(8,128)(2,1)S(1)}, u32[]{:S(2)}, u32[]{:S(2)}) %collective-permute-start) | collective-permute-done | bytes 213024 | tf_op jit(solution)/shard_map/ppermute | solution.py:177
  19.2 3.4 %collective-permute-start.8 = (bf16[2,3,104,128]{3,2,1,0:T(8,128)(2,1)S(1)}, bf16[2,3,104,128]{3,2,1,0:T(8,128)(2,1)S(1)}, u32[]{:S(2)}, u32[]{:S(2)}) collective-permute-start(bf16[2,3,104,128]{3,2,1,0:T(8,128)(2,1)S(1)} %get-tuple-element.7), channel_id=1, source_target_pairs={{0,8},{8,0},{1,9},{9,1},{2,10},{10,2},{3,11},{11,3},{4,12},{12,4},... | collective-permute-start | bytes 479240 | tf_op jit(solution)/shard_map/ppermute | solution.py:190
  22.6 9.4 %collective-permute-start.7 = (bf16[2,3,104,128]{3,2,1,0:T(8,128)(2,1)S(1)}, bf16[2,3,104,128]{3,2,1,0:T(8,128)(2,1)S(1)}, u32[]{:S(2)}, u32[]{:S(2)}) collective-permute-start(bf16[2,3,104,128]{3,2,1,0:T(8,128)(2,1)S(1)} %get-tuple-element.8), channel_id=1, source_target_pairs={{0,7},{1,0},{2,1},{3,2},{4,3},{5,4},{6,5},{7,6},{8,15},{9,8},{10,9... | collective-permute-start | bytes 479240 | tf_op jit(solution)/shard_map/ppermute | solution.py:184
  32.1 1.9 %collective-permute-start.6 = (bf16[2,3,104,128]{3,2,1,0:T(8,128)(2,1)S(1)}, bf16[2,3,104,128]{3,2,1,0:T(8,128)(2,1)S(1)}, u32[]{:S(2)}, u32[]{:S(2)}) collective-permute-start(bf16[2,3,104,128]{3,2,1,0:T(8,128)(2,1)S(1)} %get-tuple-element.9), channel_id=1, source_target_pairs={{0,1},{1,2},{2,3},{3,4},{4,5},{5,6},{6,7},{7,0},{8,9},{9,10},{10,1... | collective-permute-start | bytes 479240 | tf_op jit(solution)/shard_map/ppermute | solution.py:184
  34.0 4.6 %collective-permute-start.5 = (bf16[2,3,104,128]{3,2,1,0:T(8,128)(2,1)S(1)}, bf16[2,3,104,128]{3,2,1,0:T(8,128)(2,1)S(1)}, u32[]{:S(2)}, u32[]{:S(2)}) collective-permute-start(bf16[2,3,104,128]{3,2,1,0:T(8,128)(2,1)S(1)} %get-tuple-element.10), channel_id=1, source_target_pairs={{0,6},{1,7},{2,0},{3,1},{4,2},{5,3},{6,4},{7,5},{8,14},{9,15},{10,... | collective-permute-start | bytes 479240 | tf_op jit(solution)/shard_map/ppermute | solution.py:184
  38.6 2.2 %collective-permute-start.4 = (bf16[2,3,104,128]{3,2,1,0:T(8,128)(2,1)S(1)}, bf16[2,3,104,128]{3,2,1,0:T(8,128)(2,1)S(1)}, u32[]{:S(2)}, u32[]{:S(2)}) collective-permute-start(bf16[2,3,104,128]{3,2,1,0:T(8,128)(2,1)S(1)} %get-tuple-element.11), channel_id=1, source_target_pairs={{0,2},{1,3},{2,4},{3,5},{4,6},{5,7},{6,0},{7,1},{8,10},{9,11},{10,... | collective-permute-start | bytes 479240 | tf_op jit(solution)/shard_map/ppermute | solution.py:184
  40.8 4.6 %collective-permute-start.3 = (bf16[2,3,104,128]{3,2,1,0:T(8,128)(2,1)S(1)}, bf16[2,3,104,128]{3,2,1,0:T(8,128)(2,1)S(1)}, u32[]{:S(2)}, u32[]{:S(2)}) collective-permute-start(bf16[2,3,104,128]{3,2,1,0:T(8,128)(2,1)S(1)} %get-tuple-element.12), channel_id=1, source_target_pairs={{0,5},{1,6},{2,7},{3,0},{4,1},{5,2},{6,3},{7,4},{8,13},{9,14},{10,... | collective-permute-start | bytes 479240 | tf_op jit(solution)/shard_map/ppermute | solution.py:184
  45.4 4.3 %collective-permute-start.2 = (bf16[2,3,104,128]{3,2,1,0:T(8,128)(2,1)S(1)}, bf16[2,3,104,128]{3,2,1,0:T(8,128)(2,1)S(1)}, u32[]{:S(2)}, u32[]{:S(2)}) collective-permute-start(bf16[2,3,104,128]{3,2,1,0:T(8,128)(2,1)S(1)} %get-tuple-element.13), channel_id=1, source_target_pairs={{0,3},{1,4},{2,5},{3,6},{4,7},{5,0},{6,1},{7,2},{8,11},{9,12},{10,... | collective-permute-start | bytes 479240 | tf_op jit(solution)/shard_map/ppermute | solution.py:184
  49.6 4.0 %collective-permute-start.1 = (bf16[2,3,104,128]{3,2,1,0:T(8,128)(2,1)S(1)}, bf16[2,3,104,128]{3,2,1,0:T(8,128)(2,1)S(1)}, u32[]{:S(2)}, u32[]{:S(2)}) collective-permute-start(bf16[2,3,104,128]{3,2,1,0:T(8,128)(2,1)S(1)} %get-tuple-element.14), channel_id=1, source_target_pairs={{0,4},{1,5},{2,6},{3,7},{4,0},{5,1},{6,2},{7,3},{8,12},{9,13},{10,... | collective-permute-start | bytes 479240 | tf_op jit(solution)/shard_map/ppermute | solution.py:184
  53.7 3.3 %collective-permute-start.15 = (bf16[2,3,104,128]{3,2,1,0:T(8,128)(2,1)S(1)}, bf16[2,3,104,128]{3,2,1,0:T(8,128)(2,1)S(1)}, u32[]{:S(2)}, u32[]{:S(2)}) collective-permute-start(bf16[2,3,104,128]{3,2,1,0:T(8,128)(2,1)S(1)} %collective-permute-done.7.refs_6_), channel_id=1, source_target_pairs={{0,8},{8,0},{1,9},{9,1},{2,10},{10,2},{3,11},{11,3},{4,12},{12,4},... | collective-permute-start | bytes 479240 | tf_op jit(solution)/shard_map/ppermute | solution.py:190
  58.5 5.3 %collective-permute-start.14 = (bf16[2,3,104,128]{3,2,1,0:T(8,128)(2,1)S(1)}, bf16[2,3,104,128]{3,2,1,0:T(8,128)(2,1)S(1)}, u32[]{:S(2)}, u32[]{:S(2)}) collective-permute-start(bf16[2,3,104,128]{3,2,1,0:T(8,128)(2,1)S(1)} %collective-permute-done.6.refs_5_), channel_id=1, source_target_pairs={{0,8},{8,0},{1,9},{9,1},{2,10},{10,2},{3,11},{11,3},{4,12},{12,4},... | collective-permute-start | bytes 479240 | tf_op jit(solution)/shard_map/ppermute | solution.py:190
  64.5 1.9 %collective-permute-start.13 = (bf16[2,3,104,128]{3,2,1,0:T(8,128)(2,1)S(1)}, bf16[2,3,104,128]{3,2,1,0:T(8,128)(2,1)S(1)}, u32[]{:S(2)}, u32[]{:S(2)}) collective-permute-start(bf16[2,3,104,128]{3,2,1,0:T(8,128)(2,1)S(1)} %collective-permute-done.5.refs_4_), channel_id=1, source_target_pairs={{0,8},{8,0},{1,9},{9,1},{2,10},{10,2},{3,11},{11,3},{4,12},{12,4},... | collective-permute-start | bytes 479240 | tf_op jit(solution)/shard_map/ppermute | solution.py:190
  67.5 5.4 %collective-permute-start.12 = (bf16[2,3,104,128]{3,2,1,0:T(8,128)(2,1)S(1)}, bf16[2,3,104,128]{3,2,1,0:T(8,128)(2,1)S(1)}, u32[]{:S(2)}, u32[]{:S(2)}) collective-permute-start(bf16[2,3,104,128]{3,2,1,0:T(8,128)(2,1)S(1)} %collective-permute-done.4.refs_3_), channel_id=1, source_target_pairs={{0,8},{8,0},{1,9},{9,1},{2,10},{10,2},{3,11},{11,3},{4,12},{12,4},... | collective-permute-start | bytes 479240 | tf_op jit(solution)/shard_map/ppermute | solution.py:190
  72.9 1.9 %collective-permute-start.11 = (bf16[2,3,104,128]{3,2,1,0:T(8,128)(2,1)S(1)}, bf16[2,3,104,128]{3,2,1,0:T(8,128)(2,1)S(1)}, u32[]{:S(2)}, u32[]{:S(2)}) collective-permute-start(bf16[2,3,104,128]{3,2,1,0:T(8,128)(2,1)S(1)} %collective-permute-done.3.refs_2_), channel_id=1, source_target_pairs={{0,8},{8,0},{1,9},{9,1},{2,10},{10,2},{3,11},{11,3},{4,12},{12,4},... | collective-permute-start | bytes 479240 | tf_op jit(solution)/shard_map/ppermute | solution.py:190
  74.8 3.9 %collective-permute-start.10 = (bf16[2,3,104,128]{3,2,1,0:T(8,128)(2,1)S(1)}, bf16[2,3,104,128]{3,2,1,0:T(8,128)(2,1)S(1)}, u32[]{:S(2)}, u32[]{:S(2)}) collective-permute-start(bf16[2,3,104,128]{3,2,1,0:T(8,128)(2,1)S(1)} %collective-permute-done.2.refs_1_), channel_id=1, source_target_pairs={{0,8},{8,0},{1,9},{9,1},{2,10},{10,2},{3,11},{11,3},{4,12},{12,4},... | collective-permute-start | bytes 479240 | tf_op jit(solution)/shard_map/ppermute | solution.py:190
  78.8 1.9 %collective-permute-start.9 = (bf16[2,3,104,128]{3,2,1,0:T(8,128)(2,1)S(1)}, bf16[2,3,104,128]{3,2,1,0:T(8,128)(2,1)}, u32[]{:S(2)}, u32[]{:S(2)}) collective-permute-start(bf16[2,3,104,128]{3,2,1,0:T(8,128)(2,1)S(1)} %collective-permute-done.1.refs_0_), channel_id=1, source_target_pairs={{0,8},{8,0},{1,9},{9,1},{2,10},{10,2},{3,11},{11,3},{4,12},{12,4},... | collective-permute-start | bytes 479240 | tf_op jit(solution)/shard_map/ppermute | solution.py:190
  82.0 4.0 %collective-permute-done.9.refs_8_ = bf16[2,3,104,128]{3,2,1,0:T(8,128)(2,1)} collective-permute-done((bf16[2,3,104,128]{3,2,1,0:T(8,128)(2,1)S(1)}, bf16[2,3,104,128]{3,2,1,0:T(8,128)(2,1)}, u32[]{:S(2)}, u32[]{:S(2)}) %collective-permute-start.9) | collective-permute-done | bytes 159776 | tf_op jit(solution)/shard_map/ppermute | solution.py:190
  86.0 4.0 %prepare.1.y_hbm = bf16[3,2048,256]{2,1,0:T(8,128)(2,1)} custom-call(s32[3]{0:T(128)S(1)} %add_add_fusion.1.place, bf16[2,8,3,104,128]{4,3,2,1,0:T(8,128)(2,1)S(1)} %bitcast.43, bf16[2,3,104,128]{3,2,1,0:T(8,128)(2,1)S(1)} %collective-permute-done.1.refs_0_, bf16[2,3,104,128]{3,2,1,0:T(8,128)(2,1)S(1)} %collective-permute-done.2.refs_1_, ...), custom_call_target="tpu_custom_call" | custom-call | tf_op jit(solution)/shard_map/prepare/pallas_call | solution.py:191
  90.0 6.9 %all-gather.3.cloned.1.call-done.x_hbm = bf16[16,832,128]{2,1,0:T(8,128)(2,1)} async-done(((bf16[2,832,128]{2,1,0:T(8,128)(2,1)}), bf16[16,832,128]{2,1,0:T(8,128)(2,1)}) %all-gather.3.cloned.1.call-update) | async-done | bytes 3407888 | tf_op jit(solution)/shard_map/all_gather | solution.py:188
  96.9 7.2 %multiply.1 = (f32[2,8,3,2,56,128]{5,4,3,2,1,0:T(8,128)S(1)}, f32[32,128]{1,0:T(8,128)S(1)}) custom-call(s32[3]{0:T(128)S(1)} %add_add_fusion.place, bf16[16,832,128]{2,1,0:T(8,128)(2,1)} %all-gather.3.cloned.1.call-done.x_hbm, bf16[3,2048,256]{2,1,0:T(8,128)(2,1)} %prepare.1.y_hbm), custom_call_target="tpu_custom_call" | custom-call | tf_op jit(solution)/shard_map/multiply/pallas_call | solution.py:199
  106.0 13.0 %all_to_all.16 = f32[32,1,128]{2,1,0:T(1,128)S(1)} all-to-all(f32[32,1,128]{2,1,0:T(1,128)S(1)} %bitcast.47), channel_id=1, replica_groups=mesh['z'=12,'xh'=2,'core'=2,'xl'=2,'y'=8] {'core','xl','y'}, dimensions={0} | all-to-all | bytes 32768 | tf_op jit(solution)/shard_map/all_to_all | solution.py:217
  119.1 2.2 %clip.1 = s16[3,8,2,48,128]{4,3,2,1,0:T(8,128)(2,1)S(1)} custom-call(s32[1]{0:T(128)} %bitcast.place, f32[32,128]{1,0:T(8,128)S(1)} %bitcast.46, f32[2,8,3,2,56,128]{5,4,3,2,1,0:T(8,128)S(1)} %get-tuple-element.6.keep_ref, f32[2,8,3,2,56,128]{5,4,3,2,1,0:T(8,128)S(1)} %collective-permute-done.16.got_ref), custom_call_target="tpu_custom_call" | custom-call | tf_op jit(solution)/shard_map/clip/pallas_call | solution.py:220
  121.2 42.8 %all_to_all.17 = s16[48,48,128]{2,1,0:T(8,128)(2,1)S(1)} all-to-all(s16[48,48,128]{2,1,0:T(8,128)(2,1)S(1)} %bitcast.44), channel_id=1, replica_groups=mesh['z'=12,'xh'=2,'core'=2,'xl'=2,'y'=8] {'z','xh','xl'}, dimensions={0} | all-to-all | bytes 1179648 | tf_op jit(solution)/shard_map/all_to_all | solution.py:235
  (35 shorter events, 10.4 us)
Async XLA Ops:
  7.2 11.9 %copy-start = (bf16[1,1,16,312,128]{4,3,2,1,0:T(8,128)(2,1)S(1)}, bf16[1,1,16,312,128]{4,3,2,1,0:T(8,128)(2,1)}, u32[]{:S(2)}) copy-start(bf16[1,1,16,312,128]{4,3,2,1,0:T(8,128)(2,1)} %param.7) | copy-start | bytes 3833860
  7.2 89.7 %all-gather.3.cloned.1.call-start = ((), (), s32[]{:S(2)}) async-start(), calls=%async_computation.2 | async-start | bytes 3833856 | tf_op jit(solution)/shard_map/all_gather | solution.py:188
  9.3 8.9 %collective-permute-start = (bf16[832,128]{1,0:T(8,128)(2,1)S(1)}, bf16[832,128]{1,0:T(8,128)(2,1)S(1)}, u32[]{:S(2)}, u32[]{:S(2)}) collective-permute-start(bf16[832,128]{1,0:T(8,128)(2,1)S(1)} %pad_maximum_fusion.1), channel_id=1, source_target_pairs={{0,8},{8,0},{1,9},{9,1},{2,10},{10,2},{3,11},{11,3},{4,12},{12,4},... | collective-permute-start | bytes 638984 | tf_op jit(solution)/shard_map/ppermute | solution.py:177
  19.2 21.5 %collective-permute-start.8 = (bf16[2,3,104,128]{3,2,1,0:T(8,128)(2,1)S(1)}, bf16[2,3,104,128]{3,2,1,0:T(8,128)(2,1)S(1)}, u32[]{:S(2)}, u32[]{:S(2)}) collective-permute-start(bf16[2,3,104,128]{3,2,1,0:T(8,128)(2,1)S(1)} %get-tuple-element.7), channel_id=1, source_target_pairs={{0,8},{8,0},{1,9},{9,1},{2,10},{10,2},{3,11},{11,3},{4,12},{12,4},... | collective-permute-start | bytes 479240 | tf_op jit(solution)/shard_map/ppermute | solution.py:190
  22.6 22.7 %collective-permute-start.7 = (bf16[2,3,104,128]{3,2,1,0:T(8,128)(2,1)S(1)}, bf16[2,3,104,128]{3,2,1,0:T(8,128)(2,1)S(1)}, u32[]{:S(2)}, u32[]{:S(2)}) collective-permute-start(bf16[2,3,104,128]{3,2,1,0:T(8,128)(2,1)S(1)} %get-tuple-element.8), channel_id=1, source_target_pairs={{0,7},{1,0},{2,1},{3,2},{4,3},{5,4},{6,5},{7,6},{8,15},{9,8},{10,9... | collective-permute-start | bytes 479240 | tf_op jit(solution)/shard_map/ppermute | solution.py:184
  32.1 17.6 %collective-permute-start.6 = (bf16[2,3,104,128]{3,2,1,0:T(8,128)(2,1)S(1)}, bf16[2,3,104,128]{3,2,1,0:T(8,128)(2,1)S(1)}, u32[]{:S(2)}, u32[]{:S(2)}) collective-permute-start(bf16[2,3,104,128]{3,2,1,0:T(8,128)(2,1)S(1)} %get-tuple-element.9), channel_id=1, source_target_pairs={{0,1},{1,2},{2,3},{3,4},{4,5},{5,6},{6,7},{7,0},{8,9},{9,10},{10,1... | collective-permute-start | bytes 479240 | tf_op jit(solution)/shard_map/ppermute | solution.py:184
  34.0 19.7 %collective-permute-start.5 = (bf16[2,3,104,128]{3,2,1,0:T(8,128)(2,1)S(1)}, bf16[2,3,104,128]{3,2,1,0:T(8,128)(2,1)S(1)}, u32[]{:S(2)}, u32[]{:S(2)}) collective-permute-start(bf16[2,3,104,128]{3,2,1,0:T(8,128)(2,1)S(1)} %get-tuple-element.10), channel_id=1, source_target_pairs={{0,6},{1,7},{2,0},{3,1},{4,2},{5,3},{6,4},{7,5},{8,14},{9,15},{10,... | collective-permute-start | bytes 479240 | tf_op jit(solution)/shard_map/ppermute | solution.py:184
  38.6 19.9 %collective-permute-start.4 = (bf16[2,3,104,128]{3,2,1,0:T(8,128)(2,1)S(1)}, bf16[2,3,104,128]{3,2,1,0:T(8,128)(2,1)S(1)}, u32[]{:S(2)}, u32[]{:S(2)}) collective-permute-start(bf16[2,3,104,128]{3,2,1,0:T(8,128)(2,1)S(1)} %get-tuple-element.11), channel_id=1, source_target_pairs={{0,2},{1,3},{2,4},{3,5},{4,6},{5,7},{6,0},{7,1},{8,10},{9,11},{10,... | collective-permute-start | bytes 479240 | tf_op jit(solution)/shard_map/ppermute | solution.py:184
  40.8 23.7 %collective-permute-start.3 = (bf16[2,3,104,128]{3,2,1,0:T(8,128)(2,1)S(1)}, bf16[2,3,104,128]{3,2,1,0:T(8,128)(2,1)S(1)}, u32[]{:S(2)}, u32[]{:S(2)}) collective-permute-start(bf16[2,3,104,128]{3,2,1,0:T(8,128)(2,1)S(1)} %get-tuple-element.12), channel_id=1, source_target_pairs={{0,5},{1,6},{2,7},{3,0},{4,1},{5,2},{6,3},{7,4},{8,13},{9,14},{10,... | collective-permute-start | bytes 479240 | tf_op jit(solution)/shard_map/ppermute | solution.py:184
  45.4 22.1 %collective-permute-start.2 = (bf16[2,3,104,128]{3,2,1,0:T(8,128)(2,1)S(1)}, bf16[2,3,104,128]{3,2,1,0:T(8,128)(2,1)S(1)}, u32[]{:S(2)}, u32[]{:S(2)}) collective-permute-start(bf16[2,3,104,128]{3,2,1,0:T(8,128)(2,1)S(1)} %get-tuple-element.13), channel_id=1, source_target_pairs={{0,3},{1,4},{2,5},{3,6},{4,7},{5,0},{6,1},{7,2},{8,11},{9,12},{10,... | collective-permute-start | bytes 479240 | tf_op jit(solution)/shard_map/ppermute | solution.py:184
  49.6 23.2 %collective-permute-start.1 = (bf16[2,3,104,128]{3,2,1,0:T(8,128)(2,1)S(1)}, bf16[2,3,104,128]{3,2,1,0:T(8,128)(2,1)S(1)}, u32[]{:S(2)}, u32[]{:S(2)}) collective-permute-start(bf16[2,3,104,128]{3,2,1,0:T(8,128)(2,1)S(1)} %get-tuple-element.14), channel_id=1, source_target_pairs={{0,4},{1,5},{2,6},{3,7},{4,0},{5,1},{6,2},{7,3},{8,12},{9,13},{10,... | collective-permute-start | bytes 479240 | tf_op jit(solution)/shard_map/ppermute | solution.py:184
  53.7 21.1 %collective-permute-start.15 = (bf16[2,3,104,128]{3,2,1,0:T(8,128)(2,1)S(1)}, bf16[2,3,104,128]{3,2,1,0:T(8,128)(2,1)S(1)}, u32[]{:S(2)}, u32[]{:S(2)}) collective-permute-start(bf16[2,3,104,128]{3,2,1,0:T(8,128)(2,1)S(1)} %collective-permute-done.7.refs_6_), channel_id=1, source_target_pairs={{0,8},{8,0},{1,9},{9,1},{2,10},{10,2},{3,11},{11,3},{4,12},{12,4},... | collective-permute-start | bytes 479240 | tf_op jit(solution)/shard_map/ppermute | solution.py:190
  58.5 20.3 %collective-permute-start.14 = (bf16[2,3,104,128]{3,2,1,0:T(8,128)(2,1)S(1)}, bf16[2,3,104,128]{3,2,1,0:T(8,128)(2,1)S(1)}, u32[]{:S(2)}, u32[]{:S(2)}) collective-permute-start(bf16[2,3,104,128]{3,2,1,0:T(8,128)(2,1)S(1)} %collective-permute-done.6.refs_5_), channel_id=1, source_target_pairs={{0,8},{8,0},{1,9},{9,1},{2,10},{10,2},{3,11},{11,3},{4,12},{12,4},... | collective-permute-start | bytes 479240 | tf_op jit(solution)/shard_map/ppermute | solution.py:190
  64.5 16.4 %collective-permute-start.13 = (bf16[2,3,104,128]{3,2,1,0:T(8,128)(2,1)S(1)}, bf16[2,3,104,128]{3,2,1,0:T(8,128)(2,1)S(1)}, u32[]{:S(2)}, u32[]{:S(2)}) collective-permute-start(bf16[2,3,104,128]{3,2,1,0:T(8,128)(2,1)S(1)} %collective-permute-done.5.refs_4_), channel_id=1, source_target_pairs={{0,8},{8,0},{1,9},{9,1},{2,10},{10,2},{3,11},{11,3},{4,12},{12,4},... | collective-permute-start | bytes 479240 | tf_op jit(solution)/shard_map/ppermute | solution.py:190
  67.5 13.3 %collective-permute-start.12 = (bf16[2,3,104,128]{3,2,1,0:T(8,128)(2,1)S(1)}, bf16[2,3,104,128]{3,2,1,0:T(8,128)(2,1)S(1)}, u32[]{:S(2)}, u32[]{:S(2)}) collective-permute-start(bf16[2,3,104,128]{3,2,1,0:T(8,128)(2,1)S(1)} %collective-permute-done.4.refs_3_), channel_id=1, source_target_pairs={{0,8},{8,0},{1,9},{9,1},{2,10},{10,2},{3,11},{11,3},{4,12},{12,4},... | collective-permute-start | bytes 479240 | tf_op jit(solution)/shard_map/ppermute | solution.py:190
  72.9 8.0 %collective-permute-start.11 = (bf16[2,3,104,128]{3,2,1,0:T(8,128)(2,1)S(1)}, bf16[2,3,104,128]{3,2,1,0:T(8,128)(2,1)S(1)}, u32[]{:S(2)}, u32[]{:S(2)}) collective-permute-start(bf16[2,3,104,128]{3,2,1,0:T(8,128)(2,1)S(1)} %collective-permute-done.3.refs_2_), channel_id=1, source_target_pairs={{0,8},{8,0},{1,9},{9,1},{2,10},{10,2},{3,11},{11,3},{4,12},{12,4},... | collective-permute-start | bytes 479240 | tf_op jit(solution)/shard_map/ppermute | solution.py:190
  74.8 7.2 %collective-permute-start.10 = (bf16[2,3,104,128]{3,2,1,0:T(8,128)(2,1)S(1)}, bf16[2,3,104,128]{3,2,1,0:T(8,128)(2,1)S(1)}, u32[]{:S(2)}, u32[]{:S(2)}) collective-permute-start(bf16[2,3,104,128]{3,2,1,0:T(8,128)(2,1)S(1)} %collective-permute-done.2.refs_1_), channel_id=1, source_target_pairs={{0,8},{8,0},{1,9},{9,1},{2,10},{10,2},{3,11},{11,3},{4,12},{12,4},... | collective-permute-start | bytes 479240 | tf_op jit(solution)/shard_map/ppermute | solution.py:190
  78.8 7.3 %collective-permute-start.9 = (bf16[2,3,104,128]{3,2,1,0:T(8,128)(2,1)S(1)}, bf16[2,3,104,128]{3,2,1,0:T(8,128)(2,1)}, u32[]{:S(2)}, u32[]{:S(2)}) collective-permute-start(bf16[2,3,104,128]{3,2,1,0:T(8,128)(2,1)S(1)} %collective-permute-done.1.refs_0_), channel_id=1, source_target_pairs={{0,8},{8,0},{1,9},{9,1},{2,10},{10,2},{3,11},{11,3},{4,12},{12,4},... | collective-permute-start | bytes 479240 | tf_op jit(solution)/shard_map/ppermute | solution.py:190
  104.1 14.9 %collective-permute-start.16 = (f32[2,8,3,2,56,128]{5,4,3,2,1,0:T(8,128)S(1)}, f32[2,8,3,2,56,128]{5,4,3,2,1,0:T(8,128)S(1)}, u32[]{:S(2)}, u32[]{:S(2)}) collective-permute-start(f32[2,8,3,2,56,128]{5,4,3,2,1,0:T(8,128)S(1)} %get-tuple-element.6.keep_ref), channel_id=1, source_target_pairs={{0,16},{16,0},{1,17},{17,1},{2,18},{18,2},{3,19},{19,3},{4,20},{20... | collective-permute-start | bytes 8257544 | tf_op jit(solution)/shard_map/ppermute | solution.py:218
  119.0 45.0 %copy-start.1 = (f32[104,104]{1,0:T(8,128)S(1)}, f32[104,104]{1,0:T(8,128)}, u32[]{:S(2)}) copy-start(f32[104,104]{1,0:T(8,128)} %noise_ref.1) | copy-start | bytes 129796
  119.0 45.0 %copy-start.2 = (f32[104,104]{1,0:T(8,128)S(1)}, f32[104,104]{1,0:T(8,128)}, u32[]{:S(2)}) copy-start(f32[104,104]{1,0:T(8,128)} %first_ref.1) | copy-start | bytes 129796
  119.0 45.0 %copy-start.3 = (f32[104,104]{1,0:T(8,128)S(1)}, f32[104,104]{1,0:T(8,128)}, u32[]{:S(2)}) copy-start(f32[104,104]{1,0:T(8,128)} %second_ref.1) | copy-start | bytes 129796
Sparse Core Ops, SparseCore 0:
  19.2 77.7 all-gather.2

commit v6 on v2

--- a/solution.py
+++ b/solution.py
@@ -12,55 +12,49 @@
 LANES = 128
 TOP = 32767.0
 VMEM = 48 * 1024 * 1024
+LESS_VMEM = 32 * 1024 * 1024
 BIG, SMALL = 56, 48
 SPARE = 24
 
 
-def prepare_kernel(place, *refs):
-    *ins, out_ref = refs
-    part, count = place[0], place[1]
-    half = len(ins) // 2
-    rings = ins[0].shape[0] // 2
-    size = ins[0].shape[2]
-    out_ref[...] = jnp.zeros_like(out_ref)
-    for y in range(rings):
-        for s in range(2):
-            aug = jnp.bitwise_xor(part, s) * rings + y
+def prepare_kernel(place, grads_ref, out_ref):
+    part, ring, count = place[0], place[1], place[2]
+    rings = grads_ref.shape[0] // 2
+    size = grads_ref.shape[2]
+    for j in range(3):
+        out_ref[j, :, size:] = jnp.zeros((out_ref.shape[1], LANES - size), out_ref.dtype)
+    for s in range(rings):
+        for row in range(2):
+            aug = jnp.bitwise_xor(part, row) * rings + lax.rem(ring - s + rings, rings)
             live = (aug < count).astype(jnp.float32).astype(jnp.bfloat16)
-            at = (2 * y + s) * LANES
-            for h in range(2):
-                j = 0
-                for ref in ins[h * half : (h + 1) * half]:
-                    for k in range(ref.shape[1]):
-                        out_ref[j, at : at + LANES, h * LANES : h * LANES + size] = (ref[aug, k] * live).T
-                        j += 1
-
-
-def multiply_kernel(place, x_hbm, y_ref, out_ref, sum_ref, x_vmem, sems):
+            at = (2 * s + row) * LANES
+            for j in range(3):
+                out_ref[j, at : at + LANES, :size] = (grads_ref[aug, j] * live).T
+
+
+def multiply_kernel(place, *refs):
+    *x_refs, own_ref, other_ref, out_ref, sum_ref = refs
     part, core, count = place[0], place[1], place[2]
-    slabs = x_hbm.shape[0]
     blocks = out_ref.shape[1] // 2
+    slabs = [(ref, row) for ref in x_refs[:-2] for row in range(2)]
+    slabs = slabs[:8] + [(ref, None) for ref in x_refs[-2:]] + slabs[8:]
     tiles = []
     at = 0
     for span in (BIG, SMALL):
         for i in range(2):
             tiles.append((at, span, i * blocks))
             at += blocks * span
-    copies = []
-    for t, (row, span, _) in enumerate(tiles):
-        rows = pl.ds(row, blocks * span)
-        copies.append(pltpu.make_async_copy(x_hbm.at[:, rows], x_vmem.at[:, rows], sems.at[t]))
-        copies[-1].start()
     scale = 1.0 / count.astype(jnp.float32)
     big_slot = (part != core).astype(jnp.int32)
     squares = jnp.zeros((8, LANES), jnp.float32)
-    for t, (row, span, first) in enumerate(tiles):
-        rows = blocks * span
-        copies[t].wait()
-        x = jnp.concatenate([x_vmem[k, row : row + rows] for k in range(slabs)], axis=1)
-        slot = big_slot if span == BIG else 1 - big_slot
-        for j in range(3):
-            acc = jnp.dot(x, y_ref[j], preferred_element_type=jnp.float32) * scale
+    for j in range(3):
+        y = jnp.concatenate([own_ref[j], other_ref[j]], axis=1)
+        for row, span, first in tiles:
+            rows = blocks * span
+            window = slice(row, row + rows)
+            x = jnp.concatenate([ref[window] if k is None else ref[k, window] for ref, k in slabs], axis=1)
+            slot = big_slot if span == BIG else 1 - big_slot
+            acc = jnp.dot(x, y, preferred_element_type=jnp.float32) * scale
             square = jnp.sum((acc * acc).reshape(rows // 8, 8, 2 * LANES), axis=0)
             squares += square[:, :LANES] + square[:, LANES:]
             for b in range(blocks):
@@ -134,19 +128,20 @@
     new_second_ref[...] = 0.999 * second_ref[...] + 0.001 * grad * grad
 
 
-def call(kernel, out_shape, in_specs, **kw):
+def call(kernel, out_shape, in_specs, limit=VMEM, **kw):
     return pl.pallas_call(
         kernel,
         in_specs=in_specs,
         out_shape=out_shape,
-        compiler_params=pltpu.CompilerParams(vmem_limit_bytes=VMEM),
+        compiler_params=pltpu.CompilerParams(vmem_limit_bytes=limit),
         **kw,
     )
 
 
 def body(acts, out_grads, aug_count, noise, first_moment, second_moment):
-    part, core = lax.axis_index("xl"), lax.axis_index("core")
-    augs = 2 * lax.axis_size("y")
+    part, core, ring = lax.axis_index("xl"), lax.axis_index("core"), lax.axis_index("y")
+    rings = lax.axis_size("y")
+    augs = 2 * rings
     chips = lax.axis_size("z") * lax.axis_size("xh")
     images = 2 * chips
     width, tokens = acts.shape[2:]
@@ -166,18 +161,30 @@
         return jnp.concatenate([big.reshape(pairs * BIG, tokens), small.reshape(pairs * SMALL, tokens)])
 
     passed = lax.ppermute(half_of(1 - part), "xl", swap)
-    x = lax.all_gather(jnp.stack([half_of(part), passed]), "y")
-    x = x.reshape(augs, pairs * (BIG + SMALL), tokens)
+    mine = half_of(part)
+
+    block = jnp.stack([mine, passed])
+    up = [(i, (i + 1) % rings) for i in range(rings)]
+    down = [(i, (i - 1) % rings) for i in range(rings)]
+    back, ahead = [block], [block]
+    for _ in range(rings // 2 - 1):
+        back.append(lax.ppermute(back[-1], "y", up))
+        ahead.append(lax.ppermute(ahead[-1], "y", down))
+    x = back + ahead[:0:-1] + [lax.ppermute(back[-1][0], "y", up), lax.ppermute(ahead[-1][1], "y", down)]
 
     grads = out_grads[0, 0].reshape(augs, 3, size, tokens)
-    own = [lax.all_to_all(g, ("xl", "y"), 0, 0, tiled=True) for g in (grads[:, :2], grads[:, 2:])]
-    other = [lax.ppermute(g, "xl", swap) for g in own]
-    y = call(
-        prepare_kernel,
-        jax.ShapeDtypeStruct((3, augs * tokens, 2 * LANES), jnp.bfloat16),
-        [smem] + [vmem] * 4,
-        name="prepare",
-    )(jnp.stack([part, aug_count[0]]), *own, *other)
+    own = lax.all_to_all(grads, ("xl", "y"), 0, 0, tiled=True)
+    other = lax.ppermute(own, "xl", swap)
+    y = [
+        call(
+            prepare_kernel,
+            jax.ShapeDtypeStruct((3, augs * tokens, LANES), jnp.bfloat16),
+            [smem, vmem],
+            limit=LESS_VMEM,
+            name="prepare",
+        )(jnp.stack([part, ring, aug_count[0]]), g)
+        for g in (own, other)
+    ]
 
     group = 2 * augs
     share, square = call(
@@ -186,11 +193,11 @@
             jax.ShapeDtypeStruct((2, pairs, 3, 2, BIG, LANES), jnp.float32),
             jax.ShapeDtypeStruct((group, LANES), jnp.float32),
         ],
-        [smem, pl.BlockSpec(memory_space=pl.ANY), vmem],
+        [smem] + [vmem] * (len(x) + 2),
         out_specs=[vmem, vmem],
-        scratch_shapes=[pltpu.VMEM(x.shape, x.dtype), pltpu.SemaphoreType.DMA((4,))],
+        limit=LESS_VMEM,
         name="multiply",
-    )(jnp.stack([part, core, aug_count[0]]), x, y)
+    )(jnp.stack([part, core, aug_count[0]]), *x, *y)
 
     norms = lax.all_to_all(square, ("core", "xl", "y"), 0, 0, tiled=True)
     got = lax.ppermute(share, "core", swap)

time: 183 us -> 165 us (0.902)
  starting transfers between devices: 38.5 us -> 59.2 us
  between operations: 14.8 us -> 1.53 us
  waiting for transfers between devices: 53.5 us -> 40.4 us
  local copies, waits for them, and re-layouts: 10.6 us -> 2.98 us
  blocking collectives: 49.8 us -> 47.4 us
    all_to_all x2 -> x1, waiting for transfers between devices: 30.4 us -> 0.01 us  [body(): own = lax.all_to_all(grads, ('xl', 'y'), 0, 0, tiled=True)]
    ppermute x2 -> x9, starting transfers between devices: 6.72 us -> 28.5 us  [the longest x3 12.1 us: body(): back.append(lax.ppermute(back[-1], 'y', up))]
    ppermute x2 -> x9, waiting for transfers between devices: 10.6 us -> 24.9 us  [the longest x3 24.5 us: body(): ahead.append(lax.ppermute(ahead[-1], 'y', down))]
    all_to_all x2 -> x1, starting transfers between devices: 18.9 us -> 13.1 us  [body(): own = lax.all_to_all(grads, ('xl', 'y'), 0, 0, tiled=True)]
    unnamed x24 -> x16, local copies, waits for them, and re-layouts: 6.76 us -> 1.53 us
    all_to_all x1, starting transfers between devices: 7.53 us -> 12.3 us  [body(): norms = lax.all_to_all(square, ('core', 'xl', 'y'), 0, 0, tiled=True)]
    ppermute x1, waiting for transfers between devices: 5.45 us -> 8.54 us  [body(): passed = lax.ppermute(half_of(1 - part), 'xl', swap)]
    pallas_call x1, Pallas kernels: 7.52 us -> 5.06 us  [body(): call(multiply_kernel, [jax.ShapeDtypeStruct((2, pairs, 3, 2, BIG, LANES),...]
  transfers between devices with their start and end apart: 8 -> 13, of which waited for: 5 -> 6; matrix products, arithmetic and copies ran while one was open for 1% -> 1% of each run, Pallas kernels for 1% -> 2%
where the time goes in v6:
time: 165 us; the launch traced here: 164 us
  starting transfers between devices  59.2 us (36%)
  blocking collectives  47.4 us (29%)
  waiting for transfers between devices  40.4 us (24%)
  Pallas kernels  12.5 us (8%)
  local copies, waits for them, and re-layouts  2.98 us (2%)
    all_to_all x1, blocking collectives, body(): pieces = lax.all_to_all(pieces, ('z', 'xh', 'xl'), 0, 0, tiled=True)  47.4 us
    ppermute x3, waiting for transfers between devices, body(): ahead.append(lax.ppermute(ahead[-1], 'y', down))  24.5 us
    all_to_all x1, starting transfers between devices, body(): own = lax.all_to_all(grads, ('xl', 'y'), 0, 0, tiled=True)  13.1 us
    all_to_all x1, starting transfers between devices, body(): norms = lax.all_to_all(square, ('core', 'xl', 'y'), 0, 0, tiled=True)  12.3 us
    ppermute x3, starting transfers between devices, body(): back.append(lax.ppermute(back[-1], 'y', up))  12.1 us
    ppermute x1, waiting for transfers between devices, body(): passed = lax.ppermute(half_of(1 - part), 'xl', swap)  8.54 us
    all_to_all x1, waiting for transfers between devices, body(): norms = lax.all_to_all(square, ('core', 'xl', 'y'), 0, 0, tiled=True)  6.97 us
    ppermute x3, starting transfers between devices, body(): ahead.append(lax.ppermute(ahead[-1], 'y', down))  6.52 us
  transfers between devices with their start and end apart: 13, of which 6 were waited for; matrix products, arithmetic and copies ran while one was open for 1% of the time, Pallas kernels for 2%

profile of v6, /device:TPU:8, one launch (start us, length us, event | category | flops | bytes accessed | tf_op | source)
XLA Modules:
  0.0 164.2 jit_solution(8921796823150351046)
XLA Ops:
  0.6 13.1 %all-to-all-start = ((bf16[16,3,104,128]{3,2,1,0:T(8,128)(2,1)}), bf16[16,3,104,128]{3,2,1,0:T(8,128)(2,1)S(1)}, u32[]{:S(2)}, u32[]{:S(2)}) async-start(bf16[16,3,104,128]{3,2,1,0:T(8,128)(2,1)} %bitcast.33), calls=%async_computation | async-start | bytes 2555904 | tf_op jit(solution)/shard_map/all_to_all | solution.py:176
  13.8 3.4 %collective-permute-start = (bf16[832,128]{1,0:T(8,128)(2,1)S(1)}, bf16[832,128]{1,0:T(8,128)(2,1)S(1)}, u32[]{:S(2)}, u32[]{:S(2)}) collective-permute-start(bf16[832,128]{1,0:T(8,128)(2,1)S(1)} %pad_maximum_fusion.1), channel_id=1, source_target_pairs={{0,8},{8,0},{1,9},{9,1},{2,10},{10,2},{3,11},{11,3},{4,12},{12,4},... | collective-permute-start | bytes 638984 | tf_op jit(solution)/shard_map/ppermute | solution.py:163
  17.3 8.5 %collective-permute-done = bf16[832,128]{1,0:T(8,128)(2,1)S(1)} collective-permute-done((bf16[832,128]{1,0:T(8,128)(2,1)S(1)}, bf16[832,128]{1,0:T(8,128)(2,1)S(1)}, u32[]{:S(2)}, u32[]{:S(2)}) %collective-permute-start) | collective-permute-done | bytes 213024 | tf_op jit(solution)/shard_map/ppermute | solution.py:163
  25.9 1.9 %collective-permute-start.4 = (bf16[2,832,128]{2,1,0:T(8,128)(2,1)S(1)}, bf16[2,832,128]{2,1,0:T(8,128)(2,1)}, u32[]{:S(2)}, u32[]{:S(2)}) collective-permute-start(bf16[2,832,128]{2,1,0:T(8,128)(2,1)S(1)} %pad_maximum_fusion.refs_0_), channel_id=1, source_target_pairs={{0,7},{1,0},{2,1},{3,2},{4,3},{5,4},{6,5},{7,6},{8,15},{9,8},{10,9... | collective-permute-start | bytes 1277960 | tf_op jit(solution)/shard_map/ppermute | solution.py:172
  27.8 3.9 %collective-permute-start.1 = (bf16[2,832,128]{2,1,0:T(8,128)(2,1)S(1)}, bf16[2,832,128]{2,1,0:T(8,128)(2,1)}, u32[]{:S(2)}, u32[]{:S(2)}) collective-permute-start(bf16[2,832,128]{2,1,0:T(8,128)(2,1)S(1)} %pad_maximum_fusion.refs_0_), channel_id=1, source_target_pairs={{0,1},{1,2},{2,3},{3,4},{4,5},{5,6},{6,7},{7,0},{8,9},{9,10},{10,1... | collective-permute-start | bytes 1277960 | tf_op jit(solution)/shard_map/ppermute | solution.py:171
  31.7 16.0 %collective-permute-done.4.refs_6_ = bf16[2,832,128]{2,1,0:T(8,128)(2,1)} collective-permute-done((bf16[2,832,128]{2,1,0:T(8,128)(2,1)S(1)}, bf16[2,832,128]{2,1,0:T(8,128)(2,1)}, u32[]{:S(2)}, u32[]{:S(2)}) %collective-permute-start.4) | collective-permute-done | bytes 426016 | tf_op jit(solution)/shard_map/ppermute | solution.py:172
  47.7 2.4 %collective-permute-start.5 = (bf16[2,832,128]{2,1,0:T(8,128)(2,1)}, bf16[2,832,128]{2,1,0:T(8,128)(2,1)}, u32[]{:S(2)}, u32[]{:S(2)}) collective-permute-start(bf16[2,832,128]{2,1,0:T(8,128)(2,1)} %collective-permute-done.4.refs_6_), channel_id=1, source_target_pairs={{0,7},{1,0},{2,1},{3,2},{4,3},{5,4},{6,5},{7,6},{8,15},{9,8},{10,9... | collective-permute-start | bytes 1277960 | tf_op jit(solution)/shard_map/ppermute | solution.py:172
  50.2 3.4 %collective-permute-start.2 = (bf16[2,832,128]{2,1,0:T(8,128)(2,1)}, bf16[2,832,128]{2,1,0:T(8,128)(2,1)}, u32[]{:S(2)}, u32[]{:S(2)}) collective-permute-start(bf16[2,832,128]{2,1,0:T(8,128)(2,1)} %collective-permute-done.1.refs_1_), channel_id=1, source_target_pairs={{0,1},{1,2},{2,3},{3,4},{4,5},{5,6},{6,7},{7,0},{8,9},{9,10},{10,1... | collective-permute-start | bytes 1277960 | tf_op jit(solution)/shard_map/ppermute | solution.py:171
  53.6 3.4 %collective-permute-start.9 = (bf16[16,3,104,128]{3,2,1,0:T(8,128)(2,1)S(1)}, bf16[16,3,104,128]{3,2,1,0:T(8,128)(2,1)S(1)}, u32[]{:S(2)}, u32[]{:S(2)}) collective-permute-start(bf16[16,3,104,128]{3,2,1,0:T(8,128)(2,1)S(1)} %all-to-all-done.grads_ref), channel_id=1, source_target_pairs={{0,8},{8,0},{1,9},{9,1},{2,10},{10,2},{3,11},{11,3},{4,12},{12,4},... | collective-permute-start | bytes 3833864 | tf_op jit(solution)/shard_map/ppermute | solution.py:177
  57.0 2.4 %collective-permute-done.5.refs_5_ = bf16[2,832,128]{2,1,0:T(8,128)(2,1)} collective-permute-done((bf16[2,832,128]{2,1,0:T(8,128)(2,1)}, bf16[2,832,128]{2,1,0:T(8,128)(2,1)}, u32[]{:S(2)}, u32[]{:S(2)}) %collective-permute-start.5) | collective-permute-done | bytes 426016 | tf_op jit(solution)/shard_map/ppermute | solution.py:172
  59.4 2.2 %collective-permute-start.6 = (bf16[2,832,128]{2,1,0:T(8,128)(2,1)}, bf16[2,832,128]{2,1,0:T(8,128)(2,1)S(1)}, u32[]{:S(2)}, u32[]{:S(2)}) collective-permute-start(bf16[2,832,128]{2,1,0:T(8,128)(2,1)} %collective-permute-done.5.refs_5_), channel_id=1, source_target_pairs={{0,7},{1,0},{2,1},{3,2},{4,3},{5,4},{6,5},{7,6},{8,15},{9,8},{10,9... | collective-permute-start | bytes 1277960 | tf_op jit(solution)/shard_map/ppermute | solution.py:172
  61.6 4.8 %collective-permute-start.3 = (bf16[2,832,128]{2,1,0:T(8,128)(2,1)}, bf16[2,832,128]{2,1,0:T(8,128)(2,1)S(1)}, u32[]{:S(2)}, u32[]{:S(2)}) collective-permute-start(bf16[2,832,128]{2,1,0:T(8,128)(2,1)} %collective-permute-done.2.refs_2_), channel_id=1, source_target_pairs={{0,1},{1,2},{2,3},{3,4},{4,5},{5,6},{6,7},{7,0},{8,9},{9,10},{10,1... | collective-permute-start | bytes 1277960 | tf_op jit(solution)/shard_map/ppermute | solution.py:171
  66.4 6.1 %collective-permute-done.6.refs_4_ = bf16[2,832,128]{2,1,0:T(8,128)(2,1)S(1)} collective-permute-done((bf16[2,832,128]{2,1,0:T(8,128)(2,1)}, bf16[2,832,128]{2,1,0:T(8,128)(2,1)S(1)}, u32[]{:S(2)}, u32[]{:S(2)}) %collective-permute-start.6) | collective-permute-done | bytes 426016 | tf_op jit(solution)/shard_map/ppermute | solution.py:172
  73.9 1.9 %collective-permute-start.8 = (bf16[832,128]{1,0:T(8,128)(2,1)}, bf16[832,128]{1,0:T(8,128)(2,1)S(1)}, u32[]{:S(2)}, u32[]{:S(2)}) collective-permute-start(bf16[832,128]{1,0:T(8,128)(2,1)} %slice_bitcast_fusion), channel_id=1, source_target_pairs={{0,7},{1,0},{2,1},{3,2},{4,3},{5,4},{6,5},{7,6},{8,15},{9,8},{10,9... | collective-permute-start | bytes 638984 | tf_op jit(solution)/shard_map/ppermute | solution.py:173
  77.3 4.6 %collective-permute-start.7 = (bf16[832,128]{1,0:T(8,128)(2,1)}, bf16[832,128]{1,0:T(8,128)(2,1)}, u32[]{:S(2)}, u32[]{:S(2)}) collective-permute-start(bf16[832,128]{1,0:T(8,128)(2,1)} %slice_bitcast_fusion.1), channel_id=1, source_target_pairs={{0,1},{1,2},{2,3},{3,4},{4,5},{5,6},{6,7},{7,0},{8,9},{9,10},{10,1... | collective-permute-start | bytes 638984 | tf_op jit(solution)/shard_map/ppermute | solution.py:173
  82.6 1.3 prepare.2.refs_9_
  83.9 1.3 prepare.3.refs_10_
  85.5 5.1 %multiply.1 = (f32[2,8,3,2,56,128]{5,4,3,2,1,0:T(8,128)S(1)}, f32[32,128]{1,0:T(8,128)}) custom-call(s32[3]{0:T(128)S(1)} %get-tuple-element.11.place, bf16[2,832,128]{2,1,0:T(8,128)(2,1)S(1)} %pad_maximum_fusion.refs_0_, bf16[2,832,128]{2,1,0:T(8,128)(2,1)} %collective-permute-done.1.refs_1_, bf16[2,832,128]{2,1,0:T(8,128)(2,1)} %collective-permute-done.2.refs_2_, ...), custom_call_target="tpu_custom_call" | custom-call | tf_op jit(solution)/shard_map/multiply/pallas_call | solution.py:190
  90.6 1.9 %collective-permute-start.10 = (f32[2,8,3,2,56,128]{5,4,3,2,1,0:T(8,128)S(1)}, f32[2,8,3,2,56,128]{5,4,3,2,1,0:T(8,128)}, u32[]{:S(2)}, u32[]{:S(2)}) collective-permute-start(f32[2,8,3,2,56,128]{5,4,3,2,1,0:T(8,128)S(1)} %get-tuple-element.6.keep_ref), channel_id=1, source_target_pairs={{0,16},{16,0},{1,17},{17,1},{2,18},{18,2},{3,19},{19,3},{4,20},{20... | collective-permute-start | bytes 8257544 | tf_op jit(solution)/shard_map/ppermute | solution.py:203
  92.5 12.3 %all-to-all-start.1 = ((f32[32,1,128]{2,1,0:T(1,128)}), f32[32,1,128]{2,1,0:T(1,128)S(1)}, u32[]{:S(2)}, u32[]{:S(2)}) async-start(f32[32,1,128]{2,1,0:T(1,128)} %bitcast.14), calls=%async_computation.1 | async-start | bytes 32768 | tf_op jit(solution)/shard_map/all_to_all | solution.py:202
  104.9 7.0 %all-to-all-done.1 = f32[32,1,128]{2,1,0:T(1,128)S(1)} async-done(((f32[32,1,128]{2,1,0:T(1,128)}), f32[32,1,128]{2,1,0:T(1,128)S(1)}, u32[]{:S(2)}, u32[]{:S(2)}) %all-to-all-start.1) | async-done | bytes 16416 | tf_op jit(solution)/shard_map/all_to_all | solution.py:202
  111.9 3.5 %clip.1 = s16[3,8,2,48,128]{4,3,2,1,0:T(8,128)(2,1)S(1)} custom-call(s32[2]{0:T(128)S(1)} %pad_add_fusion.place, f32[32,128]{1,0:T(8,128)S(1)} %bitcast.32, f32[2,8,3,2,56,128]{5,4,3,2,1,0:T(8,128)S(1)} %get-tuple-element.6.keep_ref, f32[2,8,3,2,56,128]{5,4,3,2,1,0:T(8,128)} %collective-permute-done.10.got_ref), custom_call_target="tpu_custom_call" | custom-call | tf_op jit(solution)/shard_map/clip/pallas_call | solution.py:205
  115.4 47.4 %all_to_all.21 = s16[48,48,128]{2,1,0:T(8,128)(2,1)S(1)} all-to-all(s16[48,48,128]{2,1,0:T(8,128)(2,1)S(1)} %bitcast.30), channel_id=1, replica_groups=mesh['z'=12,'xh'=2,'core'=2,'xl'=2,'y'=8] {'z','xh','xl'}, dimensions={0} | all-to-all | bytes 1179648 | tf_op jit(solution)/shard_map/all_to_all | solution.py:220
  162.8 1.4 update.1
  (33 shorter events, 3.6 us)
Async XLA Ops:
  0.6 13.1 %copy-start.7 = (bf16[1,1,1664,128]{3,2,1,0:T(8,128)(2,1)S(1)}, bf16[1,1,1664,128]{3,2,1,0:T(8,128)(2,1)}, u32[]{:S(2)}) copy-start(bf16[1,1,1664,128]{3,2,1,0:T(8,128)(2,1)} %param.6) | copy-start | bytes 1277956
  0.6 53.0 %all-to-all-start = ((bf16[16,3,104,128]{3,2,1,0:T(8,128)(2,1)}), bf16[16,3,104,128]{3,2,1,0:T(8,128)(2,1)S(1)}, u32[]{:S(2)}, u32[]{:S(2)}) async-start(bf16[16,3,104,128]{3,2,1,0:T(8,128)(2,1)} %bitcast.33), calls=%async_computation | async-start | bytes 2555904 | tf_op jit(solution)/shard_map/all_to_all | solution.py:176
  13.8 12.0 %collective-permute-start = (bf16[832,128]{1,0:T(8,128)(2,1)S(1)}, bf16[832,128]{1,0:T(8,128)(2,1)S(1)}, u32[]{:S(2)}, u32[]{:S(2)}) collective-permute-start(bf16[832,128]{1,0:T(8,128)(2,1)S(1)} %pad_maximum_fusion.1), channel_id=1, source_target_pairs={{0,8},{8,0},{1,9},{9,1},{2,10},{10,2},{3,11},{11,3},{4,12},{12,4},... | collective-permute-start | bytes 638984 | tf_op jit(solution)/shard_map/ppermute | solution.py:163
  25.9 21.8 %collective-permute-start.4 = (bf16[2,832,128]{2,1,0:T(8,128)(2,1)S(1)}, bf16[2,832,128]{2,1,0:T(8,128)(2,1)}, u32[]{:S(2)}, u32[]{:S(2)}) collective-permute-start(bf16[2,832,128]{2,1,0:T(8,128)(2,1)S(1)} %pad_maximum_fusion.refs_0_), channel_id=1, source_target_pairs={{0,7},{1,0},{2,1},{3,2},{4,3},{5,4},{6,5},{7,6},{8,15},{9,8},{10,9... | collective-permute-start | bytes 1277960 | tf_op jit(solution)/shard_map/ppermute | solution.py:172
  27.8 22.3 %collective-permute-start.1 = (bf16[2,832,128]{2,1,0:T(8,128)(2,1)S(1)}, bf16[2,832,128]{2,1,0:T(8,128)(2,1)}, u32[]{:S(2)}, u32[]{:S(2)}) collective-permute-start(bf16[2,832,128]{2,1,0:T(8,128)(2,1)S(1)} %pad_maximum_fusion.refs_0_), channel_id=1, source_target_pairs={{0,1},{1,2},{2,3},{3,4},{4,5},{5,6},{6,7},{7,0},{8,9},{9,10},{10,1... | collective-permute-start | bytes 1277960 | tf_op jit(solution)/shard_map/ppermute | solution.py:171
  47.7 11.6 %collective-permute-start.5 = (bf16[2,832,128]{2,1,0:T(8,128)(2,1)}, bf16[2,832,128]{2,1,0:T(8,128)(2,1)}, u32[]{:S(2)}, u32[]{:S(2)}) collective-permute-start(bf16[2,832,128]{2,1,0:T(8,128)(2,1)} %collective-permute-done.4.refs_6_), channel_id=1, source_target_pairs={{0,7},{1,0},{2,1},{3,2},{4,3},{5,4},{6,5},{7,6},{8,15},{9,8},{10,9... | collective-permute-start | bytes 1277960 | tf_op jit(solution)/shard_map/ppermute | solution.py:172
  50.2 11.4 %collective-permute-start.2 = (bf16[2,832,128]{2,1,0:T(8,128)(2,1)}, bf16[2,832,128]{2,1,0:T(8,128)(2,1)}, u32[]{:S(2)}, u32[]{:S(2)}) collective-permute-start(bf16[2,832,128]{2,1,0:T(8,128)(2,1)} %collective-permute-done.1.refs_1_), channel_id=1, source_target_pairs={{0,1},{1,2},{2,3},{3,4},{4,5},{5,6},{6,7},{7,0},{8,9},{9,10},{10,1... | collective-permute-start | bytes 1277960 | tf_op jit(solution)/shard_map/ppermute | solution.py:171
  53.6 30.3 %collective-permute-start.9 = (bf16[16,3,104,128]{3,2,1,0:T(8,128)(2,1)S(1)}, bf16[16,3,104,128]{3,2,1,0:T(8,128)(2,1)S(1)}, u32[]{:S(2)}, u32[]{:S(2)}) collective-permute-start(bf16[16,3,104,128]{3,2,1,0:T(8,128)(2,1)S(1)} %all-to-all-done.grads_ref), channel_id=1, source_target_pairs={{0,8},{8,0},{1,9},{9,1},{2,10},{10,2},{3,11},{11,3},{4,12},{12,4},... | collective-permute-start | bytes 3833864 | tf_op jit(solution)/shard_map/ppermute | solution.py:177
  59.4 13.1 %collective-permute-start.6 = (bf16[2,832,128]{2,1,0:T(8,128)(2,1)}, bf16[2,832,128]{2,1,0:T(8,128)(2,1)S(1)}, u32[]{:S(2)}, u32[]{:S(2)}) collective-permute-start(bf16[2,832,128]{2,1,0:T(8,128)(2,1)} %collective-permute-done.5.refs_5_), channel_id=1, source_target_pairs={{0,7},{1,0},{2,1},{3,2},{4,3},{5,4},{6,5},{7,6},{8,15},{9,8},{10,9... | collective-permute-start | bytes 1277960 | tf_op jit(solution)/shard_map/ppermute | solution.py:172
  61.6 14.3 %collective-permute-start.3 = (bf16[2,832,128]{2,1,0:T(8,128)(2,1)}, bf16[2,832,128]{2,1,0:T(8,128)(2,1)S(1)}, u32[]{:S(2)}, u32[]{:S(2)}) collective-permute-start(bf16[2,832,128]{2,1,0:T(8,128)(2,1)} %collective-permute-done.2.refs_2_), channel_id=1, source_target_pairs={{0,1},{1,2},{2,3},{3,4},{4,5},{5,6},{6,7},{7,0},{8,9},{9,10},{10,1... | collective-permute-start | bytes 1277960 | tf_op jit(solution)/shard_map/ppermute | solution.py:171
  73.2 0.7 copy-start
  73.9 11.2 %collective-permute-start.8 = (bf16[832,128]{1,0:T(8,128)(2,1)}, bf16[832,128]{1,0:T(8,128)(2,1)S(1)}, u32[]{:S(2)}, u32[]{:S(2)}) collective-permute-start(bf16[832,128]{1,0:T(8,128)(2,1)} %slice_bitcast_fusion), channel_id=1, source_target_pairs={{0,7},{1,0},{2,1},{3,2},{4,3},{5,4},{6,5},{7,6},{8,15},{9,8},{10,9... | collective-permute-start | bytes 638984 | tf_op jit(solution)/shard_map/ppermute | solution.py:173
  76.6 0.8 copy-start.2
  77.3 8.2 %collective-permute-start.7 = (bf16[832,128]{1,0:T(8,128)(2,1)}, bf16[832,128]{1,0:T(8,128)(2,1)}, u32[]{:S(2)}, u32[]{:S(2)}) collective-permute-start(bf16[832,128]{1,0:T(8,128)(2,1)} %slice_bitcast_fusion.1), channel_id=1, source_target_pairs={{0,1},{1,2},{2,3},{3,4},{4,5},{5,6},{6,7},{7,0},{8,9},{9,10},{10,1... | collective-permute-start | bytes 638984 | tf_op jit(solution)/shard_map/ppermute | solution.py:173
  83.9 1.7 %copy-start.1 = (bf16[2,832,128]{2,1,0:T(8,128)(2,1)S(1)}, bf16[2,832,128]{2,1,0:T(8,128)(2,1)}, u32[]{:S(2)}) copy-start(bf16[2,832,128]{2,1,0:T(8,128)(2,1)} %copy-done) | copy-start | bytes 1277956
  83.9 1.7 %copy-start.3 = (bf16[2,832,128]{2,1,0:T(8,128)(2,1)S(1)}, bf16[2,832,128]{2,1,0:T(8,128)(2,1)}, u32[]{:S(2)}) copy-start(bf16[2,832,128]{2,1,0:T(8,128)(2,1)} %copy-done.2) | copy-start | bytes 1277956
  90.6 21.3 %collective-permute-start.10 = (f32[2,8,3,2,56,128]{5,4,3,2,1,0:T(8,128)S(1)}, f32[2,8,3,2,56,128]{5,4,3,2,1,0:T(8,128)}, u32[]{:S(2)}, u32[]{:S(2)}) collective-permute-start(f32[2,8,3,2,56,128]{5,4,3,2,1,0:T(8,128)S(1)} %get-tuple-element.6.keep_ref), channel_id=1, source_target_pairs={{0,16},{16,0},{1,17},{17,1},{2,18},{18,2},{3,19},{19,3},{4,20},{20... | collective-permute-start | bytes 8257544 | tf_op jit(solution)/shard_map/ppermute | solution.py:203
  92.5 19.3 %all-to-all-start.1 = ((f32[32,1,128]{2,1,0:T(1,128)}), f32[32,1,128]{2,1,0:T(1,128)S(1)}, u32[]{:S(2)}, u32[]{:S(2)}) async-start(f32[32,1,128]{2,1,0:T(1,128)} %bitcast.14), calls=%async_computation.1 | async-start | bytes 32768 | tf_op jit(solution)/shard_map/all_to_all | solution.py:202
  111.9 50.9 %copy-start.4 = (f32[104,104]{1,0:T(8,128)S(1)}, f32[104,104]{1,0:T(8,128)}, u32[]{:S(2)}) copy-start(f32[104,104]{1,0:T(8,128)} %noise_ref.1) | copy-start | bytes 129796
  111.9 50.9 %copy-start.5 = (f32[104,104]{1,0:T(8,128)S(1)}, f32[104,104]{1,0:T(8,128)}, u32[]{:S(2)}) copy-start(f32[104,104]{1,0:T(8,128)} %first_ref.1) | copy-start | bytes 129796
  111.9 50.9 %copy-start.6 = (f32[104,104]{1,0:T(8,128)S(1)}, f32[104,104]{1,0:T(8,128)}, u32[]{:S(2)}) copy-start(f32[104,104]{1,0:T(8,128)} %second_ref.1) | copy-start | bytes 129796

commit v7 on v6

--- a/solution.py
+++ b/solution.py
@@ -36,8 +36,7 @@
     *x_refs, own_ref, other_ref, out_ref, sum_ref = refs
     part, core, count = place[0], place[1], place[2]
     blocks = out_ref.shape[1] // 2
-    slabs = [(ref, row) for ref in x_refs[:-2] for row in range(2)]
-    slabs = slabs[:8] + [(ref, None) for ref in x_refs[-2:]] + slabs[8:]
+    slabs = [(ref, row) for ref in x_refs for row in range(2)]
     tiles = []
     at = 0
     for span in (BIG, SMALL):
@@ -52,7 +51,7 @@
         for row, span, first in tiles:
             rows = blocks * span
             window = slice(row, row + rows)
-            x = jnp.concatenate([ref[window] if k is None else ref[k, window] for ref, k in slabs], axis=1)
+            x = jnp.concatenate([ref[k, window] for ref, k in slabs], axis=1)
             slot = big_slot if span == BIG else 1 - big_slot
             acc = jnp.dot(x, y, preferred_element_type=jnp.float32) * scale
             square = jnp.sum((acc * acc).reshape(rows // 8, 8, 2 * LANES), axis=0)
@@ -170,7 +169,8 @@
     for _ in range(rings // 2 - 1):
         back.append(lax.ppermute(back[-1], "y", up))
         ahead.append(lax.ppermute(ahead[-1], "y", down))
-    x = back + ahead[:0:-1] + [lax.ppermute(back[-1][0], "y", up), lax.ppermute(ahead[-1][1], "y", down)]
+    back.append(lax.ppermute(back[-1], "y", up))
+    x = back + ahead[:0:-1]
 
     grads = out_grads[0, 0].reshape(augs, 3, size, tokens)
     own = lax.all_to_all(grads, ("xl", "y"), 0, 0, tiled=True)
@@ -213,6 +213,7 @@
         ],
         grid=(1,),
         out_specs=pl.BlockSpec((3, pairs, 2, SMALL, LANES), lambda i: (0, 0, 0, 0, 0)),
+        limit=LESS_VMEM,
         name="clip",
     )(jnp.stack([part, core]), norms, share, got)
 

time: 165 us -> 163 us (0.988)
  starting transfers between devices: 59.2 us -> 53.7 us
  blocking collectives: 47.4 us -> 50.8 us
  waiting for transfers between devices: 40.4 us -> 43 us
  local copies, waits for them, and re-layouts: 2.98 us -> 0.85 us
    ppermute x3, waiting for transfers between devices: 24.5 us -> 0.01 us  [body(): ahead.append(lax.ppermute(ahead[-1], 'y', down))]
    ppermute x3 -> x4, waiting for transfers between devices: 0.01 us -> 17 us  [body(): back.append(lax.ppermute(back[-1], 'y', up))]
    all_to_all x1, waiting for transfers between devices: 0.01 us -> 10.5 us  [body(): own = lax.all_to_all(grads, ('xl', 'y'), 0, 0, tiled=True)]
    ppermute x2 -> x0, starting transfers between devices: 6.47 us -> none  [the longest x1 4.56 us: body(): lax.ppermute(back[-1][0], 'y', up)]
    all_to_all x1, blocking collectives: 47.4 us -> 50.8 us  [body(): pieces = lax.all_to_all(pieces, ('z', 'xh', 'xl'), 0, 0, tiled=True)]
    ppermute x3, starting transfers between devices: 6.52 us -> 9.4 us  [body(): ahead.append(lax.ppermute(ahead[-1], 'y', down))]
    ppermute x3 -> x4, starting transfers between devices: 12.1 us -> 12.3 us  [body(): back.append(lax.ppermute(back[-1], 'y', up))]
  transfers between devices with their start and end apart: 13 -> 12, of which waited for: 6 -> 7; matrix products, arithmetic and copies ran while one was open for 1% -> 0% of each run, Pallas kernels for 2% -> 2%
where the time goes in v7:
time: 163 us
  starting transfers between devices  53.7 us (33%)
  blocking collectives  50.8 us (31%)
  waiting for transfers between devices  43 us (26%)
  Pallas kernels  12.7 us (8%)
    all_to_all x1, blocking collectives, body(): pieces = lax.all_to_all(pieces, ('z', 'xh', 'xl'), 0, 0, tiled=True)  50.8 us
    ppermute x4, waiting for transfers between devices, body(): back.append(lax.ppermute(back[-1], 'y', up))  17 us
    all_to_all x1, starting transfers between devices, body(): own = lax.all_to_all(grads, ('xl', 'y'), 0, 0, tiled=True)  13.1 us
    ppermute x4, starting transfers between devices, body(): back.append(lax.ppermute(back[-1], 'y', up))  12.3 us
    all_to_all x1, starting transfers between devices, body(): norms = lax.all_to_all(square, ('core', 'xl', 'y'), 0, 0, tiled=True)  10.8 us
    all_to_all x1, waiting for transfers between devices, body(): own = lax.all_to_all(grads, ('xl', 'y'), 0, 0, tiled=True)  10.5 us
    ppermute x3, starting transfers between devices, body(): ahead.append(lax.ppermute(ahead[-1], 'y', down))  9.4 us
    ppermute x1, waiting for transfers between devices, body(): passed = lax.ppermute(half_of(1 - part), 'xl', swap)  8.54 us
  transfers between devices with their start and end apart: 12, of which 7 were waited for; matrix products, arithmetic and copies ran while one was open for 0% of the time, Pallas kernels for 2%

profile of v7, /device:TPU:8, one launch (start us, length us, event | category | flops | bytes accessed | tf_op | source)
XLA Modules:
  0.0 162.8 jit_solution(7371985247243894560)
XLA Ops:
  0.6 13.1 %all-to-all-start = ((bf16[16,3,104,128]{3,2,1,0:T(8,128)(2,1)}), bf16[16,3,104,128]{3,2,1,0:T(8,128)(2,1)S(1)}, u32[]{:S(2)}, u32[]{:S(2)}) async-start(bf16[16,3,104,128]{3,2,1,0:T(8,128)(2,1)} %bitcast.29), calls=%async_computation | async-start | bytes 2555904 | tf_op jit(solution)/shard_map/all_to_all | solution.py:176
  13.8 3.4 %collective-permute-start = (bf16[832,128]{1,0:T(8,128)(2,1)S(1)}, bf16[832,128]{1,0:T(8,128)(2,1)S(1)}, u32[]{:S(2)}, u32[]{:S(2)}) collective-permute-start(bf16[832,128]{1,0:T(8,128)(2,1)S(1)} %pad_maximum_fusion.1), channel_id=1, source_target_pairs={{0,8},{8,0},{1,9},{9,1},{2,10},{10,2},{3,11},{11,3},{4,12},{12,4},... | collective-permute-start | bytes 638984 | tf_op jit(solution)/shard_map/ppermute | solution.py:162
  17.3 8.5 %collective-permute-done = bf16[832,128]{1,0:T(8,128)(2,1)S(1)} collective-permute-done((bf16[832,128]{1,0:T(8,128)(2,1)S(1)}, bf16[832,128]{1,0:T(8,128)(2,1)S(1)}, u32[]{:S(2)}, u32[]{:S(2)}) %collective-permute-start) | collective-permute-done | bytes 213024 | tf_op jit(solution)/shard_map/ppermute | solution.py:162
  25.9 3.6 %collective-permute-start.1 = (bf16[2,832,128]{2,1,0:T(8,128)(2,1)S(1)}, bf16[2,832,128]{2,1,0:T(8,128)(2,1)}, u32[]{:S(2)}, u32[]{:S(2)}) collective-permute-start(bf16[2,832,128]{2,1,0:T(8,128)(2,1)S(1)} %pad_maximum_fusion.refs_0_), channel_id=1, source_target_pairs={{0,1},{1,2},{2,3},{3,4},{4,5},{5,6},{6,7},{7,0},{8,9},{9,10},{10,1... | collective-permute-start | bytes 1277960 | tf_op jit(solution)/shard_map/ppermute | solution.py:170
  29.5 2.2 %collective-permute-start.5 = (bf16[2,832,128]{2,1,0:T(8,128)(2,1)S(1)}, bf16[2,832,128]{2,1,0:T(8,128)(2,1)}, u32[]{:S(2)}, u32[]{:S(2)}) collective-permute-start(bf16[2,832,128]{2,1,0:T(8,128)(2,1)S(1)} %pad_maximum_fusion.refs_0_), channel_id=1, source_target_pairs={{0,7},{1,0},{2,1},{3,2},{4,3},{5,4},{6,5},{7,6},{8,15},{9,8},{10,9... | collective-permute-start | bytes 1277960 | tf_op jit(solution)/shard_map/ppermute | solution.py:171
  31.7 10.5 %all-to-all-done.grads_ref = bf16[16,3,104,128]{3,2,1,0:T(8,128)(2,1)S(1)} async-done(((bf16[16,3,104,128]{3,2,1,0:T(8,128)(2,1)}), bf16[16,3,104,128]{3,2,1,0:T(8,128)(2,1)S(1)}, u32[]{:S(2)}, u32[]{:S(2)}) %all-to-all-start) | async-done | bytes 1277984 | tf_op jit(solution)/shard_map/all_to_all | solution.py:176
  42.3 2.7 %collective-permute-start.8 = (bf16[16,3,104,128]{3,2,1,0:T(8,128)(2,1)S(1)}, bf16[16,3,104,128]{3,2,1,0:T(8,128)(2,1)S(1)}, u32[]{:S(2)}, u32[]{:S(2)}) collective-permute-start(bf16[16,3,104,128]{3,2,1,0:T(8,128)(2,1)S(1)} %all-to-all-done.grads_ref), channel_id=1, source_target_pairs={{0,8},{8,0},{1,9},{9,1},{2,10},{10,2},{3,11},{11,3},{4,12},{12,4},... | collective-permute-start | bytes 3833864 | tf_op jit(solution)/shard_map/ppermute | solution.py:177
  44.9 1.6 %collective-permute-done.1.refs_1_ = bf16[2,832,128]{2,1,0:T(8,128)(2,1)} collective-permute-done((bf16[2,832,128]{2,1,0:T(8,128)(2,1)S(1)}, bf16[2,832,128]{2,1,0:T(8,128)(2,1)}, u32[]{:S(2)}, u32[]{:S(2)}) %collective-permute-start.1) | collective-permute-done | bytes 426016 | tf_op jit(solution)/shard_map/ppermute | solution.py:170
  46.6 3.3 %collective-permute-start.2 = (bf16[2,832,128]{2,1,0:T(8,128)(2,1)}, bf16[2,832,128]{2,1,0:T(8,128)(2,1)S(1)}, u32[]{:S(2)}, u32[]{:S(2)}) collective-permute-start(bf16[2,832,128]{2,1,0:T(8,128)(2,1)} %collective-permute-done.1.refs_1_), channel_id=1, source_target_pairs={{0,1},{1,2},{2,3},{3,4},{4,5},{5,6},{6,7},{7,0},{8,9},{9,10},{10,1... | collective-permute-start | bytes 1277960 | tf_op jit(solution)/shard_map/ppermute | solution.py:170
  49.9 3.4 %collective-permute-start.6 = (bf16[2,832,128]{2,1,0:T(8,128)(2,1)}, bf16[2,832,128]{2,1,0:T(8,128)(2,1)}, u32[]{:S(2)}, u32[]{:S(2)}) collective-permute-start(bf16[2,832,128]{2,1,0:T(8,128)(2,1)} %collective-permute-done.5.refs_7_), channel_id=1, source_target_pairs={{0,7},{1,0},{2,1},{3,2},{4,3},{5,4},{6,5},{7,6},{8,15},{9,8},{10,9... | collective-permute-start | bytes 1277960 | tf_op jit(solution)/shard_map/ppermute | solution.py:171
  53.3 5.8 %collective-permute-done.2.refs_2_ = bf16[2,832,128]{2,1,0:T(8,128)(2,1)S(1)} collective-permute-done((bf16[2,832,128]{2,1,0:T(8,128)(2,1)}, bf16[2,832,128]{2,1,0:T(8,128)(2,1)S(1)}, u32[]{:S(2)}, u32[]{:S(2)}) %collective-permute-start.2) | collective-permute-done | bytes 426016 | tf_op jit(solution)/shard_map/ppermute | solution.py:170
  59.1 2.9 %collective-permute-start.3 = (bf16[2,832,128]{2,1,0:T(8,128)(2,1)S(1)}, bf16[2,832,128]{2,1,0:T(8,128)(2,1)}, u32[]{:S(2)}, u32[]{:S(2)}) collective-permute-start(bf16[2,832,128]{2,1,0:T(8,128)(2,1)S(1)} %collective-permute-done.2.refs_2_), channel_id=1, source_target_pairs={{0,1},{1,2},{2,3},{3,4},{4,5},{5,6},{6,7},{7,0},{8,9},{9,10},{10,1... | collective-permute-start | bytes 1277960 | tf_op jit(solution)/shard_map/ppermute | solution.py:170
  62.8 3.8 %collective-permute-start.7 = (bf16[2,832,128]{2,1,0:T(8,128)(2,1)}, bf16[2,832,128]{2,1,0:T(8,128)(2,1)}, u32[]{:S(2)}, u32[]{:S(2)}) collective-permute-start(bf16[2,832,128]{2,1,0:T(8,128)(2,1)} %collective-permute-done.6.refs_6_), channel_id=1, source_target_pairs={{0,7},{1,0},{2,1},{3,2},{4,3},{5,4},{6,5},{7,6},{8,15},{9,8},{10,9... | collective-permute-start | bytes 1277960 | tf_op jit(solution)/shard_map/ppermute | solution.py:171
  66.7 4.0 %collective-permute-done.3.refs_3_ = bf16[2,832,128]{2,1,0:T(8,128)(2,1)} collective-permute-done((bf16[2,832,128]{2,1,0:T(8,128)(2,1)S(1)}, bf16[2,832,128]{2,1,0:T(8,128)(2,1)}, u32[]{:S(2)}, u32[]{:S(2)}) %collective-permute-start.3) | collective-permute-done | bytes 426016 | tf_op jit(solution)/shard_map/ppermute | solution.py:170
  70.7 2.4 %collective-permute-start.4 = (bf16[2,832,128]{2,1,0:T(8,128)(2,1)}, bf16[2,832,128]{2,1,0:T(8,128)(2,1)}, u32[]{:S(2)}, u32[]{:S(2)}) collective-permute-start(bf16[2,832,128]{2,1,0:T(8,128)(2,1)} %collective-permute-done.3.refs_3_), channel_id=1, source_target_pairs={{0,1},{1,2},{2,3},{3,4},{4,5},{5,6},{6,7},{7,0},{8,9},{9,10},{10,1... | collective-permute-start | bytes 1277960 | tf_op jit(solution)/shard_map/ppermute | solution.py:172
  73.9 1.3 prepare.2.refs_8_
  76.4 5.5 %collective-permute-done.4.refs_4_ = bf16[2,832,128]{2,1,0:T(8,128)(2,1)} collective-permute-done((bf16[2,832,128]{2,1,0:T(8,128)(2,1)}, bf16[2,832,128]{2,1,0:T(8,128)(2,1)}, u32[]{:S(2)}, u32[]{:S(2)}) %collective-permute-start.4) | collective-permute-done | bytes 426016 | tf_op jit(solution)/shard_map/ppermute | solution.py:172
  81.9 5.2 %multiply.1 = (f32[2,8,3,2,56,128]{5,4,3,2,1,0:T(8,128)S(1)}, f32[32,128]{1,0:T(8,128)}) custom-call(s32[3]{0:T(128)S(1)} %get-tuple-element.11.place, bf16[2,832,128]{2,1,0:T(8,128)(2,1)S(1)} %pad_maximum_fusion.refs_0_, bf16[2,832,128]{2,1,0:T(8,128)(2,1)} %collective-permute-done.1.refs_1_, bf16[2,832,128]{2,1,0:T(8,128)(2,1)S(1)} %copy-done.1, ...), custom_call_target="tpu_custom_call" | custom-call | tf_op jit(solution)/shard_map/multiply/pallas_call | solution.py:190
  87.2 1.9 %collective-permute-start.9 = (f32[2,8,3,2,56,128]{5,4,3,2,1,0:T(8,128)S(1)}, f32[2,8,3,2,56,128]{5,4,3,2,1,0:T(8,128)}, u32[]{:S(2)}, u32[]{:S(2)}) collective-permute-start(f32[2,8,3,2,56,128]{5,4,3,2,1,0:T(8,128)S(1)} %get-tuple-element.6.keep_ref), channel_id=1, source_target_pairs={{0,16},{16,0},{1,17},{17,1},{2,18},{18,2},{3,19},{19,3},{4,20},{20... | collective-permute-start | bytes 8257544 | tf_op jit(solution)/shard_map/ppermute | solution.py:203
  89.1 10.8 %all-to-all-start.1 = ((f32[32,1,128]{2,1,0:T(1,128)}), f32[32,1,128]{2,1,0:T(1,128)S(1)}, u32[]{:S(2)}, u32[]{:S(2)}) async-start(f32[32,1,128]{2,1,0:T(1,128)} %bitcast.12), calls=%async_computation.1 | async-start | bytes 32768 | tf_op jit(solution)/shard_map/all_to_all | solution.py:202
  100.0 7.0 %all-to-all-done.1 = f32[32,1,128]{2,1,0:T(1,128)S(1)} async-done(((f32[32,1,128]{2,1,0:T(1,128)}), f32[32,1,128]{2,1,0:T(1,128)S(1)}, u32[]{:S(2)}, u32[]{:S(2)}) %all-to-all-start.1) | async-done | bytes 16416 | tf_op jit(solution)/shard_map/all_to_all | solution.py:202
  107.0 3.5 %clip.1 = s16[3,8,2,48,128]{4,3,2,1,0:T(8,128)(2,1)S(1)} custom-call(s32[2]{0:T(128)S(1)} %pad_add_fusion.place, f32[32,128]{1,0:T(8,128)S(1)} %bitcast.28, f32[2,8,3,2,56,128]{5,4,3,2,1,0:T(8,128)S(1)} %get-tuple-element.6.keep_ref, f32[2,8,3,2,56,128]{5,4,3,2,1,0:T(8,128)} %collective-permute-done.9.got_ref), custom_call_target="tpu_custom_call" | custom-call | tf_op jit(solution)/shard_map/clip/pallas_call | solution.py:205
  110.5 50.8 %all_to_all.21 = s16[48,48,128]{2,1,0:T(8,128)(2,1)S(1)} all-to-all(s16[48,48,128]{2,1,0:T(8,128)(2,1)S(1)} %bitcast.26), channel_id=1, replica_groups=mesh['z'=12,'xh'=2,'core'=2,'xl'=2,'y'=8] {'z','xh','xl'}, dimensions={0} | all-to-all | bytes 1179648 | tf_op jit(solution)/shard_map/all_to_all | solution.py:221
  161.4 1.4 update.1
  (25 shorter events, 2.3 us)
Async XLA Ops:
  0.6 13.1 %copy-start.5 = (bf16[1,1,1664,128]{3,2,1,0:T(8,128)(2,1)S(1)}, bf16[1,1,1664,128]{3,2,1,0:T(8,128)(2,1)}, u32[]{:S(2)}) copy-start(bf16[1,1,1664,128]{3,2,1,0:T(8,128)(2,1)} %param.6) | copy-start | bytes 1277956
  0.6 41.6 %all-to-all-start = ((bf16[16,3,104,128]{3,2,1,0:T(8,128)(2,1)}), bf16[16,3,104,128]{3,2,1,0:T(8,128)(2,1)S(1)}, u32[]{:S(2)}, u32[]{:S(2)}) async-start(bf16[16,3,104,128]{3,2,1,0:T(8,128)(2,1)} %bitcast.29), calls=%async_computation | async-start | bytes 2555904 | tf_op jit(solution)/shard_map/all_to_all | solution.py:176
  13.8 12.0 %collective-permute-start = (bf16[832,128]{1,0:T(8,128)(2,1)S(1)}, bf16[832,128]{1,0:T(8,128)(2,1)S(1)}, u32[]{:S(2)}, u32[]{:S(2)}) collective-permute-start(bf16[832,128]{1,0:T(8,128)(2,1)S(1)} %pad_maximum_fusion.1), channel_id=1, source_target_pairs={{0,8},{8,0},{1,9},{9,1},{2,10},{10,2},{3,11},{11,3},{4,12},{12,4},... | collective-permute-start | bytes 638984 | tf_op jit(solution)/shard_map/ppermute | solution.py:162
  25.9 20.7 %collective-permute-start.1 = (bf16[2,832,128]{2,1,0:T(8,128)(2,1)S(1)}, bf16[2,832,128]{2,1,0:T(8,128)(2,1)}, u32[]{:S(2)}, u32[]{:S(2)}) collective-permute-start(bf16[2,832,128]{2,1,0:T(8,128)(2,1)S(1)} %pad_maximum_fusion.refs_0_), channel_id=1, source_target_pairs={{0,1},{1,2},{2,3},{3,4},{4,5},{5,6},{6,7},{7,0},{8,9},{9,10},{10,1... | collective-permute-start | bytes 1277960 | tf_op jit(solution)/shard_map/ppermute | solution.py:170
  29.5 20.4 %collective-permute-start.5 = (bf16[2,832,128]{2,1,0:T(8,128)(2,1)S(1)}, bf16[2,832,128]{2,1,0:T(8,128)(2,1)}, u32[]{:S(2)}, u32[]{:S(2)}) collective-permute-start(bf16[2,832,128]{2,1,0:T(8,128)(2,1)S(1)} %pad_maximum_fusion.refs_0_), channel_id=1, source_target_pairs={{0,7},{1,0},{2,1},{3,2},{4,3},{5,4},{6,5},{7,6},{8,15},{9,8},{10,9... | collective-permute-start | bytes 1277960 | tf_op jit(solution)/shard_map/ppermute | solution.py:171
  42.3 32.9 %collective-permute-start.8 = (bf16[16,3,104,128]{3,2,1,0:T(8,128)(2,1)S(1)}, bf16[16,3,104,128]{3,2,1,0:T(8,128)(2,1)S(1)}, u32[]{:S(2)}, u32[]{:S(2)}) collective-permute-start(bf16[16,3,104,128]{3,2,1,0:T(8,128)(2,1)S(1)} %all-to-all-done.grads_ref), channel_id=1, source_target_pairs={{0,8},{8,0},{1,9},{9,1},{2,10},{10,2},{3,11},{11,3},{4,12},{12,4},... | collective-permute-start | bytes 3833864 | tf_op jit(solution)/shard_map/ppermute | solution.py:177
  46.6 12.5 %collective-permute-start.2 = (bf16[2,832,128]{2,1,0:T(8,128)(2,1)}, bf16[2,832,128]{2,1,0:T(8,128)(2,1)S(1)}, u32[]{:S(2)}, u32[]{:S(2)}) collective-permute-start(bf16[2,832,128]{2,1,0:T(8,128)(2,1)} %collective-permute-done.1.refs_1_), channel_id=1, source_target_pairs={{0,1},{1,2},{2,3},{3,4},{4,5},{5,6},{6,7},{7,0},{8,9},{9,10},{10,1... | collective-permute-start | bytes 1277960 | tf_op jit(solution)/shard_map/ppermute | solution.py:170
  49.9 12.9 %collective-permute-start.6 = (bf16[2,832,128]{2,1,0:T(8,128)(2,1)}, bf16[2,832,128]{2,1,0:T(8,128)(2,1)}, u32[]{:S(2)}, u32[]{:S(2)}) collective-permute-start(bf16[2,832,128]{2,1,0:T(8,128)(2,1)} %collective-permute-done.5.refs_7_), channel_id=1, source_target_pairs={{0,7},{1,0},{2,1},{3,2},{4,3},{5,4},{6,5},{7,6},{8,15},{9,8},{10,9... | collective-permute-start | bytes 1277960 | tf_op jit(solution)/shard_map/ppermute | solution.py:171
  59.1 11.6 %collective-permute-start.3 = (bf16[2,832,128]{2,1,0:T(8,128)(2,1)S(1)}, bf16[2,832,128]{2,1,0:T(8,128)(2,1)}, u32[]{:S(2)}, u32[]{:S(2)}) collective-permute-start(bf16[2,832,128]{2,1,0:T(8,128)(2,1)S(1)} %collective-permute-done.2.refs_2_), channel_id=1, source_target_pairs={{0,1},{1,2},{2,3},{3,4},{4,5},{5,6},{6,7},{7,0},{8,9},{9,10},{10,1... | collective-permute-start | bytes 1277960 | tf_op jit(solution)/shard_map/ppermute | solution.py:170
  62.0 0.8 copy-start
  62.8 13.6 %collective-permute-start.7 = (bf16[2,832,128]{2,1,0:T(8,128)(2,1)}, bf16[2,832,128]{2,1,0:T(8,128)(2,1)}, u32[]{:S(2)}, u32[]{:S(2)}) collective-permute-start(bf16[2,832,128]{2,1,0:T(8,128)(2,1)} %collective-permute-done.6.refs_6_), channel_id=1, source_target_pairs={{0,7},{1,0},{2,1},{3,2},{4,3},{5,4},{6,5},{7,6},{8,15},{9,8},{10,9... | collective-permute-start | bytes 1277960 | tf_op jit(solution)/shard_map/ppermute | solution.py:171
  70.7 11.3 %collective-permute-start.4 = (bf16[2,832,128]{2,1,0:T(8,128)(2,1)}, bf16[2,832,128]{2,1,0:T(8,128)(2,1)}, u32[]{:S(2)}, u32[]{:S(2)}) collective-permute-start(bf16[2,832,128]{2,1,0:T(8,128)(2,1)} %collective-permute-done.3.refs_3_), channel_id=1, source_target_pairs={{0,1},{1,2},{2,3},{3,4},{4,5},{5,6},{6,7},{7,0},{8,9},{9,10},{10,1... | collective-permute-start | bytes 1277960 | tf_op jit(solution)/shard_map/ppermute | solution.py:172
  75.1 6.8 %copy-start.1 = (bf16[2,832,128]{2,1,0:T(8,128)(2,1)S(1)}, bf16[2,832,128]{2,1,0:T(8,128)(2,1)}, u32[]{:S(2)}) copy-start(bf16[2,832,128]{2,1,0:T(8,128)(2,1)} %copy-done) | copy-start | bytes 1277956
  87.2 19.8 %collective-permute-start.9 = (f32[2,8,3,2,56,128]{5,4,3,2,1,0:T(8,128)S(1)}, f32[2,8,3,2,56,128]{5,4,3,2,1,0:T(8,128)}, u32[]{:S(2)}, u32[]{:S(2)}) collective-permute-start(f32[2,8,3,2,56,128]{5,4,3,2,1,0:T(8,128)S(1)} %get-tuple-element.6.keep_ref), channel_id=1, source_target_pairs={{0,16},{16,0},{1,17},{17,1},{2,18},{18,2},{3,19},{19,3},{4,20},{20... | collective-permute-start | bytes 8257544 | tf_op jit(solution)/shard_map/ppermute | solution.py:203
  89.1 17.9 %all-to-all-start.1 = ((f32[32,1,128]{2,1,0:T(1,128)}), f32[32,1,128]{2,1,0:T(1,128)S(1)}, u32[]{:S(2)}, u32[]{:S(2)}) async-start(f32[32,1,128]{2,1,0:T(1,128)} %bitcast.12), calls=%async_computation.1 | async-start | bytes 32768 | tf_op jit(solution)/shard_map/all_to_all | solution.py:202
  107.0 54.4 %copy-start.2 = (f32[104,104]{1,0:T(8,128)S(1)}, f32[104,104]{1,0:T(8,128)}, u32[]{:S(2)}) copy-start(f32[104,104]{1,0:T(8,128)} %noise_ref.1) | copy-start | bytes 129796
  107.0 54.4 %copy-start.3 = (f32[104,104]{1,0:T(8,128)S(1)}, f32[104,104]{1,0:T(8,128)}, u32[]{:S(2)}) copy-start(f32[104,104]{1,0:T(8,128)} %first_ref.1) | copy-start | bytes 129796
  107.0 54.4 %copy-start.4 = (f32[104,104]{1,0:T(8,128)S(1)}, f32[104,104]{1,0:T(8,128)}, u32[]{:S(2)}) copy-start(f32[104,104]{1,0:T(8,128)} %second_ref.1) | copy-start | bytes 129796

commit v8 on v7

--- a/solution.py
+++ b/solution.py
@@ -32,28 +32,48 @@
                 out_ref[j, at : at + LANES, :size] = (grads_ref[aug, j] * live).T
 
 
-def multiply_kernel(place, *refs):
-    *x_refs, own_ref, other_ref, out_ref, sum_ref = refs
-    part, core, count = place[0], place[1], place[2]
-    blocks = out_ref.shape[1] // 2
-    slabs = [(ref, row) for ref in x_refs for row in range(2)]
+def tiles_of(blocks):
     tiles = []
     at = 0
     for span in (BIG, SMALL):
         for i in range(2):
             tiles.append((at, span, i * blocks))
             at += blocks * span
+    return tiles
+
+
+def sum_kernel(*refs, near):
+    *x_refs, own_ref, other_ref, out_ref = refs
+    slabs = [(ref, k) for ref in x_refs for k in range(2)]
+    tokens = x_refs[0].shape[2]
+    for j in range(3):
+        pieces = []
+        for lo, hi in near:
+            rows = slice(lo * tokens, hi * tokens)
+            pieces.append(jnp.concatenate([own_ref[j, rows], other_ref[j, rows]], axis=1))
+        y = jnp.concatenate(pieces, axis=0)
+        for row, span, _ in tiles_of(x_refs[0].shape[1] // (2 * (BIG + SMALL))):
+            window = slice(row, row + span * (x_refs[0].shape[1] // (2 * (BIG + SMALL))))
+            x = jnp.concatenate([ref[k, window] for ref, k in slabs], axis=1)
+            out_ref[j, window] = jnp.dot(x, y, preferred_element_type=jnp.float32)
+
+
+def multiply_kernel(place, partial_ref, x_ref, own_ref, other_ref, out_ref, sum_ref, *, far):
+    part, core, count = place[0], place[1], place[2]
+    blocks = out_ref.shape[1] // 2
+    tokens = x_ref.shape[2]
     scale = 1.0 / count.astype(jnp.float32)
     big_slot = (part != core).astype(jnp.int32)
     squares = jnp.zeros((8, LANES), jnp.float32)
+    which = slice(far * tokens, (far + 2) * tokens)
     for j in range(3):
-        y = jnp.concatenate([own_ref[j], other_ref[j]], axis=1)
-        for row, span, first in tiles:
+        y = jnp.concatenate([own_ref[j, which], other_ref[j, which]], axis=1)
+        for row, span, first in tiles_of(blocks):
             rows = blocks * span
             window = slice(row, row + rows)
-            x = jnp.concatenate([ref[k, window] for ref, k in slabs], axis=1)
+            x = jnp.concatenate([x_ref[0, window], x_ref[1, window]], axis=1)
             slot = big_slot if span == BIG else 1 - big_slot
-            acc = jnp.dot(x, y, preferred_element_type=jnp.float32) * scale
+            acc = (partial_ref[j, window] + jnp.dot(x, y, preferred_element_type=jnp.float32)) * scale
             square = jnp.sum((acc * acc).reshape(rows // 8, 8, 2 * LANES), axis=0)
             squares += square[:, :LANES] + square[:, LANES:]
             for b in range(blocks):
@@ -64,8 +84,14 @@
     sum_ref[...] = jnp.broadcast_to(jnp.sum(squares, keepdims=True), sum_ref.shape)
 
 
-def clip_kernel(place, norms_ref, keep_ref, got_ref, out_ref, *, clip, size):
+def clip_kernel(place, norms_ref, keep_ref, got_hbm, out_ref, got_ref, sems, *, clip, size):
     part, core = place[0], place[1]
+    step = got_ref.shape[0] // 4
+    copies = []
+    for q in range(4):
+        some = pl.ds(q * step, step)
+        copies.append(pltpu.make_async_copy(got_hbm.at[1, some], got_ref.at[some], sems.at[q]))
+        copies[q].start()
     half = norms_ref.shape[0] // 2
     factors = []
     for c in range(2):
@@ -78,7 +104,7 @@
     def block(k, carry):
         for j in range(3):
             for h in range(2):
-                value = keep_ref[0, k, j, h] * mine + got_ref[0, k, j, h] * theirs
+                value = keep_ref[0, k, j, h] * mine + got_ref[k, j, h] * theirs
                 top = jnp.maximum(jnp.max(jnp.abs(value), axis=1, keepdims=True), 1e-30)
                 code = jnp.ceil(jnp.log2(top) * 8.0 + 0.05)
                 value = jnp.round(value * (jnp.exp2(code * -0.125) * TOP))
@@ -95,7 +121,9 @@
                 out_ref[j, k, jnp.bitwise_xor(part, h)] = piece.astype(jnp.int32).astype(jnp.int16)
         return carry
 
-    lax.fori_loop(0, keep_ref.shape[1], block, 0)
+    for q in range(4):
+        copies[q].wait()
+        lax.fori_loop(q * step, (q + 1) * step, block, 0)
 
 
 def update_kernel(place, got_ref, noise_ref, first_ref, second_ref, grad_ref, new_first_ref, new_second_ref, *, weight, images):
@@ -170,7 +198,7 @@
         back.append(lax.ppermute(back[-1], "y", up))
         ahead.append(lax.ppermute(ahead[-1], "y", down))
     back.append(lax.ppermute(back[-1], "y", up))
-    x = back + ahead[:0:-1]
+    x = back[:-1] + ahead[:0:-1]
 
     grads = out_grads[0, 0].reshape(augs, 3, size, tokens)
     own = lax.all_to_all(grads, ("xl", "y"), 0, 0, tiled=True)
@@ -186,18 +214,28 @@
         for g in (own, other)
     ]
 
+    rows = pairs * (BIG + SMALL)
+    far = rings
+    partial = call(
+        functools.partial(sum_kernel, near=((0, far), (far + 2, augs))),
+        jax.ShapeDtypeStruct((3, rows, 2 * LANES), jnp.float32),
+        [vmem] * (len(x) + 2),
+        limit=LESS_VMEM,
+        cost_estimate=pl.CostEstimate(flops=12 * rows * LANES * (augs - 2) * tokens, bytes_accessed=1 << 23, transcendentals=0),
+        name="sum",
+    )(*x, *y)
     group = 2 * augs
     share, square = call(
-        multiply_kernel,
+        functools.partial(multiply_kernel, far=far),
         [
             jax.ShapeDtypeStruct((2, pairs, 3, 2, BIG, LANES), jnp.float32),
             jax.ShapeDtypeStruct((group, LANES), jnp.float32),
         ],
-        [smem] + [vmem] * (len(x) + 2),
+        [smem] + [vmem] * 4,
         out_specs=[vmem, vmem],
         limit=LESS_VMEM,
         name="multiply",
-    )(jnp.stack([part, core, aug_count[0]]), *x, *y)
+    )(jnp.stack([part, core, aug_count[0]]), partial, back[-1], *y)
 
     norms = lax.all_to_all(square, ("core", "xl", "y"), 0, 0, tiled=True)
     got = lax.ppermute(share, "core", swap)
@@ -209,10 +247,11 @@
             smem,
             pl.BlockSpec((group, LANES), lambda i: (0, 0)),
             pl.BlockSpec(half, lambda i: (0, 0, 0, 0, 0, 0)),
-            pl.BlockSpec(half, lambda i: (1, 0, 0, 0, 0, 0)),
+            pl.BlockSpec(memory_space=pltpu.HBM),
         ],
         grid=(1,),
         out_specs=pl.BlockSpec((3, pairs, 2, SMALL, LANES), lambda i: (0, 0, 0, 0, 0)),
+        scratch_shapes=[pltpu.VMEM(half[1:], jnp.float32), pltpu.SemaphoreType.DMA((4,))],
         limit=LESS_VMEM,
         name="clip",
     )(jnp.stack([part, core]), norms, share, got)

time: 163 us -> 160 us (0.982)
  waiting for transfers between devices: 43 us -> 39.4 us
    ppermute x4, waiting for transfers between devices: 17 us -> 13.3 us  [body(): back.append(lax.ppermute(back[-1], 'y', up))]
    pallas_call x1 -> x2, Pallas kernels: 5.25 us -> 5.83 us  [the longest x1 4.01 us: body(): call(functools.partial(sum_kernel, near=((0, far), (far + 2, augs))), jax...]
  transfers between devices with their start and end apart: 12 -> 12, of which waited for: 7 -> 7; matrix products, arithmetic and copies ran while one was open for 0% -> 0% of each run, Pallas kernels for 2% -> 4%
where the time goes in v8:
time: 160 us; the launch traced here: 159 us
  starting transfers between devices  53.9 us (34%)
  blocking collectives  50.8 us (32%)
  waiting for transfers between devices  39.4 us (25%)
  Pallas kernels  13.4 us (8%)
    all_to_all x1, blocking collectives, body(): pieces = lax.all_to_all(pieces, ('z', 'xh', 'xl'), 0, 0, tiled=True)  50.8 us
    ppermute x4, waiting for transfers between devices, body(): back.append(lax.ppermute(back[-1], 'y', up))  13.3 us
    all_to_all x1, starting transfers between devices, body(): own = lax.all_to_all(grads, ('xl', 'y'), 0, 0, tiled=True)  13.1 us
    ppermute x4, starting transfers between devices, body(): back.append(lax.ppermute(back[-1], 'y', up))  12.6 us
    all_to_all x1, starting transfers between devices, body(): norms = lax.all_to_all(square, ('core', 'xl', 'y'), 0, 0, tiled=True)  10.8 us
    all_to_all x1, waiting for transfers between devices, body(): own = lax.all_to_all(grads, ('xl', 'y'), 0, 0, tiled=True)  10.5 us
    ppermute x3, starting transfers between devices, body(): ahead.append(lax.ppermute(ahead[-1], 'y', down))  9.31 us
    ppermute x1, waiting for transfers between devices, body(): passed = lax.ppermute(half_of(1 - part), 'xl', swap)  8.54 us
  transfers between devices with their start and end apart: 12, of which 7 were waited for; matrix products, arithmetic and copies ran while one was open for 0% of the time, Pallas kernels for 4%

profile of v8, /device:TPU:8, one launch (start us, length us, event | category | flops | bytes accessed | tf_op | source)
XLA Modules:
  0.0 159.4 jit_solution(17987697508454558179)
XLA Ops:
  0.6 13.1 %all-to-all-start = ((bf16[16,3,104,128]{3,2,1,0:T(8,128)(2,1)}), bf16[16,3,104,128]{3,2,1,0:T(8,128)(2,1)S(1)}, u32[]{:S(2)}, u32[]{:S(2)}) async-start(bf16[16,3,104,128]{3,2,1,0:T(8,128)(2,1)} %bitcast.29), calls=%async_computation | async-start | bytes 2555904 | tf_op jit(solution)/shard_map/all_to_all | solution.py:204
  13.8 3.4 %collective-permute-start = (bf16[832,128]{1,0:T(8,128)(2,1)S(1)}, bf16[832,128]{1,0:T(8,128)(2,1)S(1)}, u32[]{:S(2)}, u32[]{:S(2)}) collective-permute-start(bf16[832,128]{1,0:T(8,128)(2,1)S(1)} %pad_maximum_fusion.1), channel_id=1, source_target_pairs={{0,8},{8,0},{1,9},{9,1},{2,10},{10,2},{3,11},{11,3},{4,12},{12,4},... | collective-permute-start | bytes 638984 | tf_op jit(solution)/shard_map/ppermute | solution.py:190
  17.3 8.5 %collective-permute-done = bf16[832,128]{1,0:T(8,128)(2,1)S(1)} collective-permute-done((bf16[832,128]{1,0:T(8,128)(2,1)S(1)}, bf16[832,128]{1,0:T(8,128)(2,1)S(1)}, u32[]{:S(2)}, u32[]{:S(2)}) %collective-permute-start) | collective-permute-done | bytes 213024 | tf_op jit(solution)/shard_map/ppermute | solution.py:190
  25.9 3.6 %collective-permute-start.1 = (bf16[2,832,128]{2,1,0:T(8,128)(2,1)S(1)}, bf16[2,832,128]{2,1,0:T(8,128)(2,1)S(1)}, u32[]{:S(2)}, u32[]{:S(2)}) collective-permute-start(bf16[2,832,128]{2,1,0:T(8,128)(2,1)S(1)} %pad_maximum_fusion.refs_0_), channel_id=1, source_target_pairs={{0,1},{1,2},{2,3},{3,4},{4,5},{5,6},{6,7},{7,0},{8,9},{9,10},{10,1... | collective-permute-start | bytes 1277960 | tf_op jit(solution)/shard_map/ppermute | solution.py:198
  29.5 2.2 %collective-permute-start.4 = (bf16[2,832,128]{2,1,0:T(8,128)(2,1)S(1)}, bf16[2,832,128]{2,1,0:T(8,128)(2,1)}, u32[]{:S(2)}, u32[]{:S(2)}) collective-permute-start(bf16[2,832,128]{2,1,0:T(8,128)(2,1)S(1)} %pad_maximum_fusion.refs_0_), channel_id=1, source_target_pairs={{0,7},{1,0},{2,1},{3,2},{4,3},{5,4},{6,5},{7,6},{8,15},{9,8},{10,9... | collective-permute-start | bytes 1277960 | tf_op jit(solution)/shard_map/ppermute | solution.py:199
  31.7 10.5 %all-to-all-done.grads_ref = bf16[16,3,104,128]{3,2,1,0:T(8,128)(2,1)S(1)} async-done(((bf16[16,3,104,128]{3,2,1,0:T(8,128)(2,1)}), bf16[16,3,104,128]{3,2,1,0:T(8,128)(2,1)S(1)}, u32[]{:S(2)}, u32[]{:S(2)}) %all-to-all-start) | async-done | bytes 1277984 | tf_op jit(solution)/shard_map/all_to_all | solution.py:204
  42.3 2.7 %collective-permute-start.7 = (bf16[16,3,104,128]{3,2,1,0:T(8,128)(2,1)S(1)}, bf16[16,3,104,128]{3,2,1,0:T(8,128)(2,1)S(1)}, u32[]{:S(2)}, u32[]{:S(2)}) collective-permute-start(bf16[16,3,104,128]{3,2,1,0:T(8,128)(2,1)S(1)} %all-to-all-done.grads_ref), channel_id=1, source_target_pairs={{0,8},{8,0},{1,9},{9,1},{2,10},{10,2},{3,11},{11,3},{4,12},{12,4},... | collective-permute-start | bytes 3833864 | tf_op jit(solution)/shard_map/ppermute | solution.py:205
  44.9 1.5 collective-permute-done.1.refs_1_
  46.5 3.3 %collective-permute-start.2 = (bf16[2,832,128]{2,1,0:T(8,128)(2,1)S(1)}, bf16[2,832,128]{2,1,0:T(8,128)(2,1)}, u32[]{:S(2)}, u32[]{:S(2)}) collective-permute-start(bf16[2,832,128]{2,1,0:T(8,128)(2,1)S(1)} %collective-permute-done.1.refs_1_), channel_id=1, source_target_pairs={{0,1},{1,2},{2,3},{3,4},{4,5},{5,6},{6,7},{7,0},{8,9},{9,10},{10,1... | collective-permute-start | bytes 1277960 | tf_op jit(solution)/shard_map/ppermute | solution.py:198
  49.8 3.4 %collective-permute-start.5 = (bf16[2,832,128]{2,1,0:T(8,128)(2,1)}, bf16[2,832,128]{2,1,0:T(8,128)(2,1)}, u32[]{:S(2)}, u32[]{:S(2)}) collective-permute-start(bf16[2,832,128]{2,1,0:T(8,128)(2,1)} %collective-permute-done.4.refs_6_), channel_id=1, source_target_pairs={{0,7},{1,0},{2,1},{3,2},{4,3},{5,4},{6,5},{7,6},{8,15},{9,8},{10,9... | collective-permute-start | bytes 1277960 | tf_op jit(solution)/shard_map/ppermute | solution.py:199
  53.2 5.7 %collective-permute-done.2.refs_2_ = bf16[2,832,128]{2,1,0:T(8,128)(2,1)} collective-permute-done((bf16[2,832,128]{2,1,0:T(8,128)(2,1)S(1)}, bf16[2,832,128]{2,1,0:T(8,128)(2,1)}, u32[]{:S(2)}, u32[]{:S(2)}) %collective-permute-start.2) | collective-permute-done | bytes 426016 | tf_op jit(solution)/shard_map/ppermute | solution.py:198
  58.9 3.0 %collective-permute-start.3 = (bf16[2,832,128]{2,1,0:T(8,128)(2,1)}, bf16[2,832,128]{2,1,0:T(8,128)(2,1)}, u32[]{:S(2)}, u32[]{:S(2)}) collective-permute-start(bf16[2,832,128]{2,1,0:T(8,128)(2,1)} %collective-permute-done.2.refs_2_), channel_id=1, source_target_pairs={{0,1},{1,2},{2,3},{3,4},{4,5},{5,6},{6,7},{7,0},{8,9},{9,10},{10,1... | collective-permute-start | bytes 1277960 | tf_op jit(solution)/shard_map/ppermute | solution.py:198
  61.9 3.7 %collective-permute-start.6 = (bf16[2,832,128]{2,1,0:T(8,128)(2,1)}, bf16[2,832,128]{2,1,0:T(8,128)(2,1)}, u32[]{:S(2)}, u32[]{:S(2)}) collective-permute-start(bf16[2,832,128]{2,1,0:T(8,128)(2,1)} %collective-permute-done.5.refs_5_), channel_id=1, source_target_pairs={{0,7},{1,0},{2,1},{3,2},{4,3},{5,4},{6,5},{7,6},{8,15},{9,8},{10,9... | collective-permute-start | bytes 1277960 | tf_op jit(solution)/shard_map/ppermute | solution.py:199
  66.3 4.3 %collective-permute-done.3.refs_3_ = bf16[2,832,128]{2,1,0:T(8,128)(2,1)} collective-permute-done((bf16[2,832,128]{2,1,0:T(8,128)(2,1)}, bf16[2,832,128]{2,1,0:T(8,128)(2,1)}, u32[]{:S(2)}, u32[]{:S(2)}) %collective-permute-start.3) | collective-permute-done | bytes 426016 | tf_op jit(solution)/shard_map/ppermute | solution.py:198
  70.7 2.7 %collective-permute-start.8 = (bf16[2,832,128]{2,1,0:T(8,128)(2,1)}, bf16[2,832,128]{2,1,0:T(8,128)(2,1)S(1)}, u32[]{:S(2)}, u32[]{:S(2)}) collective-permute-start(bf16[2,832,128]{2,1,0:T(8,128)(2,1)} %collective-permute-done.3.refs_3_), channel_id=1, source_target_pairs={{0,1},{1,2},{2,3},{3,4},{4,5},{5,6},{6,7},{7,0},{8,9},{9,10},{10,1... | collective-permute-start | bytes 1277960 | tf_op jit(solution)/shard_map/ppermute | solution.py:200
  76.0 4.0 %sum.1.partial_ref = f32[3,832,256]{2,1,0:T(8,128)S(1)} custom-call(bf16[2,832,128]{2,1,0:T(8,128)(2,1)S(1)} %pad_maximum_fusion.refs_0_, bf16[2,832,128]{2,1,0:T(8,128)(2,1)S(1)} %collective-permute-done.1.refs_1_, bf16[2,832,128]{2,1,0:T(8,128)(2,1)} %collective-permute-done.2.refs_2_, bf16[2,832,128]{2,1,0:T(8,128)(2,1)} %collective-permute-done.3.refs_3_, ...), custom_call_target="tpu_custom_call" | custom-call | flops 2290089984 | bytes 8388608 | tf_op jit(solution)/shard_map/sum/pallas_call | solution.py:219
  80.0 1.8 %collective-permute-done.8.x_ref = bf16[2,832,128]{2,1,0:T(8,128)(2,1)S(1)} collective-permute-done((bf16[2,832,128]{2,1,0:T(8,128)(2,1)}, bf16[2,832,128]{2,1,0:T(8,128)(2,1)S(1)}, u32[]{:S(2)}, u32[]{:S(2)}) %collective-permute-start.8) | collective-permute-done | bytes 426016 | tf_op jit(solution)/shard_map/ppermute | solution.py:200
  81.8 1.8 %multiply.1 = (f32[2,8,3,2,56,128]{5,4,3,2,1,0:T(8,128)S(1)}, f32[32,128]{1,0:T(8,128)}) custom-call(s32[3]{0:T(128)S(1)} %add_add_fusion.place, f32[3,832,256]{2,1,0:T(8,128)S(1)} %sum.1.partial_ref, bf16[2,832,128]{2,1,0:T(8,128)(2,1)S(1)} %collective-permute-done.8.x_ref, bf16[3,2048,128]{2,1,0:T(8,128)(2,1)S(1)} %prepare.2.refs_7_.own_ref, ...), custom_call_target="tpu_custom_call" | custom-call | tf_op jit(solution)/shard_map/multiply/pallas_call | solution.py:228
  83.6 1.9 %collective-permute-start.9 = (f32[2,8,3,2,56,128]{5,4,3,2,1,0:T(8,128)S(1)}, f32[2,8,3,2,56,128]{5,4,3,2,1,0:T(8,128)}, u32[]{:S(2)}, u32[]{:S(2)}) collective-permute-start(f32[2,8,3,2,56,128]{5,4,3,2,1,0:T(8,128)S(1)} %get-tuple-element.6.keep_ref), channel_id=1, source_target_pairs={{0,16},{16,0},{1,17},{17,1},{2,18},{18,2},{3,19},{19,3},{4,20},{20... | collective-permute-start | bytes 8257544 | tf_op jit(solution)/shard_map/ppermute | solution.py:241
  85.6 10.8 %all-to-all-start.1 = ((f32[32,1,128]{2,1,0:T(1,128)}), f32[32,1,128]{2,1,0:T(1,128)S(1)}, u32[]{:S(2)}, u32[]{:S(2)}) async-start(f32[32,1,128]{2,1,0:T(1,128)} %bitcast.12), calls=%async_computation.1 | async-start | bytes 32768 | tf_op jit(solution)/shard_map/all_to_all | solution.py:240
  96.5 7.0 %all-to-all-done.1 = f32[32,1,128]{2,1,0:T(1,128)S(1)} async-done(((f32[32,1,128]{2,1,0:T(1,128)}), f32[32,1,128]{2,1,0:T(1,128)S(1)}, u32[]{:S(2)}, u32[]{:S(2)}) %all-to-all-start.1) | async-done | bytes 16416 | tf_op jit(solution)/shard_map/all_to_all | solution.py:240
  103.5 3.7 %clip.1 = s16[3,8,2,48,128]{4,3,2,1,0:T(8,128)(2,1)S(1)} custom-call(s32[2]{0:T(128)S(1)} %pad_add_fusion.place, f32[32,128]{1,0:T(8,128)S(1)} %bitcast.28, f32[2,8,3,2,56,128]{5,4,3,2,1,0:T(8,128)S(1)} %get-tuple-element.6.keep_ref, f32[2,8,3,2,56,128]{5,4,3,2,1,0:T(8,128)} %collective-permute-done.9.got_hbm), custom_call_target="tpu_custom_call" | custom-call | tf_op jit(solution)/shard_map/clip/pallas_call | solution.py:243
  107.2 50.8 %all_to_all.21 = s16[48,48,128]{2,1,0:T(8,128)(2,1)S(1)} all-to-all(s16[48,48,128]{2,1,0:T(8,128)(2,1)S(1)} %bitcast.26), channel_id=1, replica_groups=mesh['z'=12,'xh'=2,'core'=2,'xl'=2,'y'=8] {'z','xh','xl'}, dimensions={0} | all-to-all | bytes 1179648 | tf_op jit(solution)/shard_map/all_to_all | solution.py:260
  158.0 1.4 update.1
  (23 shorter events, 2.9 us)
Async XLA Ops:
  0.6 13.1 %copy-start.3 = (bf16[1,1,1664,128]{3,2,1,0:T(8,128)(2,1)S(1)}, bf16[1,1,1664,128]{3,2,1,0:T(8,128)(2,1)}, u32[]{:S(2)}) copy-start(bf16[1,1,1664,128]{3,2,1,0:T(8,128)(2,1)} %param.6) | copy-start | bytes 1277956
  0.6 41.6 %all-to-all-start = ((bf16[16,3,104,128]{3,2,1,0:T(8,128)(2,1)}), bf16[16,3,104,128]{3,2,1,0:T(8,128)(2,1)S(1)}, u32[]{:S(2)}, u32[]{:S(2)}) async-start(bf16[16,3,104,128]{3,2,1,0:T(8,128)(2,1)} %bitcast.29), calls=%async_computation | async-start | bytes 2555904 | tf_op jit(solution)/shard_map/all_to_all | solution.py:204
  13.8 12.0 %collective-permute-start = (bf16[832,128]{1,0:T(8,128)(2,1)S(1)}, bf16[832,128]{1,0:T(8,128)(2,1)S(1)}, u32[]{:S(2)}, u32[]{:S(2)}) collective-permute-start(bf16[832,128]{1,0:T(8,128)(2,1)S(1)} %pad_maximum_fusion.1), channel_id=1, source_target_pairs={{0,8},{8,0},{1,9},{9,1},{2,10},{10,2},{3,11},{11,3},{4,12},{12,4},... | collective-permute-start | bytes 638984 | tf_op jit(solution)/shard_map/ppermute | solution.py:190
  25.9 20.6 %collective-permute-start.1 = (bf16[2,832,128]{2,1,0:T(8,128)(2,1)S(1)}, bf16[2,832,128]{2,1,0:T(8,128)(2,1)S(1)}, u32[]{:S(2)}, u32[]{:S(2)}) collective-permute-start(bf16[2,832,128]{2,1,0:T(8,128)(2,1)S(1)} %pad_maximum_fusion.refs_0_), channel_id=1, source_target_pairs={{0,1},{1,2},{2,3},{3,4},{4,5},{5,6},{6,7},{7,0},{8,9},{9,10},{10,1... | collective-permute-start | bytes 1277960 | tf_op jit(solution)/shard_map/ppermute | solution.py:198
  29.5 20.3 %collective-permute-start.4 = (bf16[2,832,128]{2,1,0:T(8,128)(2,1)S(1)}, bf16[2,832,128]{2,1,0:T(8,128)(2,1)}, u32[]{:S(2)}, u32[]{:S(2)}) collective-permute-start(bf16[2,832,128]{2,1,0:T(8,128)(2,1)S(1)} %pad_maximum_fusion.refs_0_), channel_id=1, source_target_pairs={{0,7},{1,0},{2,1},{3,2},{4,3},{5,4},{6,5},{7,6},{8,15},{9,8},{10,9... | collective-permute-start | bytes 1277960 | tf_op jit(solution)/shard_map/ppermute | solution.py:199
  42.3 32.5 %collective-permute-start.7 = (bf16[16,3,104,128]{3,2,1,0:T(8,128)(2,1)S(1)}, bf16[16,3,104,128]{3,2,1,0:T(8,128)(2,1)S(1)}, u32[]{:S(2)}, u32[]{:S(2)}) collective-permute-start(bf16[16,3,104,128]{3,2,1,0:T(8,128)(2,1)S(1)} %all-to-all-done.grads_ref), channel_id=1, source_target_pairs={{0,8},{8,0},{1,9},{9,1},{2,10},{10,2},{3,11},{11,3},{4,12},{12,4},... | collective-permute-start | bytes 3833864 | tf_op jit(solution)/shard_map/ppermute | solution.py:205
  46.5 12.4 %collective-permute-start.2 = (bf16[2,832,128]{2,1,0:T(8,128)(2,1)S(1)}, bf16[2,832,128]{2,1,0:T(8,128)(2,1)}, u32[]{:S(2)}, u32[]{:S(2)}) collective-permute-start(bf16[2,832,128]{2,1,0:T(8,128)(2,1)S(1)} %collective-permute-done.1.refs_1_), channel_id=1, source_target_pairs={{0,1},{1,2},{2,3},{3,4},{4,5},{5,6},{6,7},{7,0},{8,9},{9,10},{10,1... | collective-permute-start | bytes 1277960 | tf_op jit(solution)/shard_map/ppermute | solution.py:198
  49.8 12.1 %collective-permute-start.5 = (bf16[2,832,128]{2,1,0:T(8,128)(2,1)}, bf16[2,832,128]{2,1,0:T(8,128)(2,1)}, u32[]{:S(2)}, u32[]{:S(2)}) collective-permute-start(bf16[2,832,128]{2,1,0:T(8,128)(2,1)} %collective-permute-done.4.refs_6_), channel_id=1, source_target_pairs={{0,7},{1,0},{2,1},{3,2},{4,3},{5,4},{6,5},{7,6},{8,15},{9,8},{10,9... | collective-permute-start | bytes 1277960 | tf_op jit(solution)/shard_map/ppermute | solution.py:199
  58.9 11.8 %collective-permute-start.3 = (bf16[2,832,128]{2,1,0:T(8,128)(2,1)}, bf16[2,832,128]{2,1,0:T(8,128)(2,1)}, u32[]{:S(2)}, u32[]{:S(2)}) collective-permute-start(bf16[2,832,128]{2,1,0:T(8,128)(2,1)} %collective-permute-done.2.refs_2_), channel_id=1, source_target_pairs={{0,1},{1,2},{2,3},{3,4},{4,5},{5,6},{6,7},{7,0},{8,9},{9,10},{10,1... | collective-permute-start | bytes 1277960 | tf_op jit(solution)/shard_map/ppermute | solution.py:198
  61.9 14.1 %collective-permute-start.6 = (bf16[2,832,128]{2,1,0:T(8,128)(2,1)}, bf16[2,832,128]{2,1,0:T(8,128)(2,1)}, u32[]{:S(2)}, u32[]{:S(2)}) collective-permute-start(bf16[2,832,128]{2,1,0:T(8,128)(2,1)} %collective-permute-done.5.refs_5_), channel_id=1, source_target_pairs={{0,7},{1,0},{2,1},{3,2},{4,3},{5,4},{6,5},{7,6},{8,15},{9,8},{10,9... | collective-permute-start | bytes 1277960 | tf_op jit(solution)/shard_map/ppermute | solution.py:199
  70.7 11.2 %collective-permute-start.8 = (bf16[2,832,128]{2,1,0:T(8,128)(2,1)}, bf16[2,832,128]{2,1,0:T(8,128)(2,1)S(1)}, u32[]{:S(2)}, u32[]{:S(2)}) collective-permute-start(bf16[2,832,128]{2,1,0:T(8,128)(2,1)} %collective-permute-done.3.refs_3_), channel_id=1, source_target_pairs={{0,1},{1,2},{2,3},{3,4},{4,5},{5,6},{6,7},{7,0},{8,9},{9,10},{10,1... | collective-permute-start | bytes 1277960 | tf_op jit(solution)/shard_map/ppermute | solution.py:200
  83.6 19.8 %collective-permute-start.9 = (f32[2,8,3,2,56,128]{5,4,3,2,1,0:T(8,128)S(1)}, f32[2,8,3,2,56,128]{5,4,3,2,1,0:T(8,128)}, u32[]{:S(2)}, u32[]{:S(2)}) collective-permute-start(f32[2,8,3,2,56,128]{5,4,3,2,1,0:T(8,128)S(1)} %get-tuple-element.6.keep_ref), channel_id=1, source_target_pairs={{0,16},{16,0},{1,17},{17,1},{2,18},{18,2},{3,19},{19,3},{4,20},{20... | collective-permute-start | bytes 8257544 | tf_op jit(solution)/shard_map/ppermute | solution.py:241
  85.6 17.9 %all-to-all-start.1 = ((f32[32,1,128]{2,1,0:T(1,128)}), f32[32,1,128]{2,1,0:T(1,128)S(1)}, u32[]{:S(2)}, u32[]{:S(2)}) async-start(f32[32,1,128]{2,1,0:T(1,128)} %bitcast.12), calls=%async_computation.1 | async-start | bytes 32768 | tf_op jit(solution)/shard_map/all_to_all | solution.py:240
  103.5 54.5 %copy-start = (f32[104,104]{1,0:T(8,128)S(1)}, f32[104,104]{1,0:T(8,128)}, u32[]{:S(2)}) copy-start(f32[104,104]{1,0:T(8,128)} %noise_ref.1) | copy-start | bytes 129796
  103.5 54.5 %copy-start.1 = (f32[104,104]{1,0:T(8,128)S(1)}, f32[104,104]{1,0:T(8,128)}, u32[]{:S(2)}) copy-start(f32[104,104]{1,0:T(8,128)} %first_ref.1) | copy-start | bytes 129796
  103.5 54.5 %copy-start.2 = (f32[104,104]{1,0:T(8,128)S(1)}, f32[104,104]{1,0:T(8,128)}, u32[]{:S(2)}) copy-start(f32[104,104]{1,0:T(8,128)} %second_ref.1) | copy-start | bytes 129796

commit v9 on v8

--- a/solution.py
+++ b/solution.py
@@ -58,40 +58,40 @@
             out_ref[j, window] = jnp.dot(x, y, preferred_element_type=jnp.float32)
 
 
-def multiply_kernel(place, partial_ref, x_ref, own_ref, other_ref, out_ref, sum_ref, *, far):
+def multiply_kernel(place, partial_ref, x_ref, own_ref, other_ref, keep_ref, send_ref, sum_ref, *, far):
     part, core, count = place[0], place[1], place[2]
-    blocks = out_ref.shape[1] // 2
+    blocks = keep_ref.shape[0] // 2
     tokens = x_ref.shape[2]
     scale = 1.0 / count.astype(jnp.float32)
-    big_slot = (part != core).astype(jnp.int32)
     squares = jnp.zeros((8, LANES), jnp.float32)
     which = slice(far * tokens, (far + 2) * tokens)
+    keeps_big = jnp.broadcast_to(part == core, (BIG, LANES))
+    missing = jnp.zeros((BIG - SMALL, LANES), jnp.float32)
+    tiles = tiles_of(blocks)
     for j in range(3):
         y = jnp.concatenate([own_ref[j, which], other_ref[j, which]], axis=1)
-        for row, span, first in tiles_of(blocks):
-            rows = blocks * span
-            window = slice(row, row + rows)
-            x = jnp.concatenate([x_ref[0, window], x_ref[1, window]], axis=1)
-            slot = big_slot if span == BIG else 1 - big_slot
-            acc = (partial_ref[j, window] + jnp.dot(x, y, preferred_element_type=jnp.float32)) * scale
-            square = jnp.sum((acc * acc).reshape(rows // 8, 8, 2 * LANES), axis=0)
-            squares += square[:, :LANES] + square[:, LANES:]
+        for big, small in zip(tiles[:2], tiles[2:]):
+            accs = []
+            for row, span, first in (big, small):
+                rows = blocks * span
+                window = slice(row, row + rows)
+                x = jnp.concatenate([x_ref[0, window], x_ref[1, window]], axis=1)
+                acc = (partial_ref[j, window] + jnp.dot(x, y, preferred_element_type=jnp.float32)) * scale
+                square = jnp.sum((acc * acc).reshape(rows // 8, 8, 2 * LANES), axis=0)
+                squares += square[:, :LANES] + square[:, LANES:]
+                accs.append(acc)
             for b in range(blocks):
                 for h in range(2):
-                    out_ref[slot, first + b, j, h, :span] = acc[b * span : (b + 1) * span, h * LANES : (h + 1) * LANES]
-                    if span < BIG:
-                        out_ref[slot, first + b, j, h, span:] = jnp.zeros((BIG - span, LANES), jnp.float32)
+                    lanes = slice(h * LANES, (h + 1) * LANES)
+                    more = accs[0][b * BIG : (b + 1) * BIG, lanes]
+                    less = jnp.concatenate([accs[1][b * SMALL : (b + 1) * SMALL, lanes], missing], axis=0)
+                    keep_ref[first + b, j, h] = jnp.where(keeps_big, more, less)
+                    send_ref[first + b, j, h] = jnp.where(keeps_big, less, more)
     sum_ref[...] = jnp.broadcast_to(jnp.sum(squares, keepdims=True), sum_ref.shape)
 
 
-def clip_kernel(place, norms_ref, keep_ref, got_hbm, out_ref, got_ref, sems, *, clip, size):
+def clip_kernel(place, norms_ref, keep_ref, got_ref, out_ref, *, clip, size):
     part, core = place[0], place[1]
-    step = got_ref.shape[0] // 4
-    copies = []
-    for q in range(4):
-        some = pl.ds(q * step, step)
-        copies.append(pltpu.make_async_copy(got_hbm.at[1, some], got_ref.at[some], sems.at[q]))
-        copies[q].start()
     half = norms_ref.shape[0] // 2
     factors = []
     for c in range(2):
@@ -101,29 +101,31 @@
     theirs = jnp.where(core == 0, factors[1], factors[0])
     lane = lax.broadcasted_iota(jnp.int32, (8, LANES), 1)
 
-    def block(k, carry):
-        for j in range(3):
-            for h in range(2):
-                value = keep_ref[0, k, j, h] * mine + got_ref[k, j, h] * theirs
-                top = jnp.maximum(jnp.max(jnp.abs(value), axis=1, keepdims=True), 1e-30)
-                code = jnp.ceil(jnp.log2(top) * 8.0 + 0.05)
-                value = jnp.round(value * (jnp.exp2(code * -0.125) * TOP))
-                pieces = []
-                for g in range(SMALL // 8):
-                    if g < 5:
-                        spare = pltpu.roll(value[SMALL:], (size - SPARE * g) % LANES, 1)
-                    else:
-                        spare = jnp.zeros((8, LANES), jnp.float32)
-                        for q in range(BIG // 8):
-                            spare = jnp.where(lane == size + q, code[8 * q : 8 * q + 8], spare)
-                    pieces.append(jnp.where(lane < size, value[8 * g : 8 * g + 8], spare))
-                piece = jnp.concatenate(pieces, axis=0)
-                out_ref[j, k, jnp.bitwise_xor(part, h)] = piece.astype(jnp.int32).astype(jnp.int16)
-        return carry
-
-    for q in range(4):
-        copies[q].wait()
-        lax.fori_loop(q * step, (q + 1) * step, block, 0)
+    def run(flip):
+        def block(k, carry):
+            for j in range(3):
+                for h in range(2):
+                    value = keep_ref[k, j, h] * mine + got_ref[k, j, h] * theirs
+                    top = jnp.maximum(jnp.max(jnp.abs(value), axis=1, keepdims=True), 1e-30)
+                    code = jnp.ceil(jnp.log2(top) * 8.0 + 0.05)
+                    value = jnp.round(value * (jnp.exp2(code * -0.125) * TOP))
+                    pieces = []
+                    for g in range(SMALL // 8):
+                        if g < 5:
+                            spare = pltpu.roll(value[SMALL:], (size - SPARE * g) % LANES, 1)
+                        else:
+                            spare = jnp.zeros((8, LANES), jnp.float32)
+                            for q in range(BIG // 8):
+                                spare = jnp.where(lane == size + q, code[8 * q : 8 * q + 8], spare)
+                        pieces.append(jnp.where(lane < size, value[8 * g : 8 * g + 8], spare))
+                    piece = jnp.concatenate(pieces, axis=0)
+                    out_ref[j, k, h ^ flip] = piece.astype(jnp.int32).astype(jnp.int16)
+            return carry
+
+        lax.fori_loop(0, keep_ref.shape[0], block, 0)
+
+    for flip in range(2):
+        pl.when(part == flip)(functools.partial(run, flip))
 
 
 def update_kernel(place, got_ref, noise_ref, first_ref, second_ref, grad_ref, new_first_ref, new_second_ref, *, weight, images):
@@ -225,36 +227,25 @@
         name="sum",
     )(*x, *y)
     group = 2 * augs
-    share, square = call(
+    half = jax.ShapeDtypeStruct((pairs, 3, 2, BIG, LANES), jnp.float32)
+    keep, send, square = call(
         functools.partial(multiply_kernel, far=far),
-        [
-            jax.ShapeDtypeStruct((2, pairs, 3, 2, BIG, LANES), jnp.float32),
-            jax.ShapeDtypeStruct((group, LANES), jnp.float32),
-        ],
+        [half, half, jax.ShapeDtypeStruct((group, LANES), jnp.float32)],
         [smem] + [vmem] * 4,
-        out_specs=[vmem, vmem],
+        out_specs=[vmem] * 3,
         limit=LESS_VMEM,
         name="multiply",
     )(jnp.stack([part, core, aug_count[0]]), partial, back[-1], *y)
 
     norms = lax.all_to_all(square, ("core", "xl", "y"), 0, 0, tiled=True)
-    got = lax.ppermute(share, "core", swap)
-    half = (1, pairs, 3, 2, BIG, LANES)
+    got = lax.ppermute(send, "core", swap)
     pieces = call(
         functools.partial(clip_kernel, clip=clip, size=size),
         jax.ShapeDtypeStruct((3, pairs, 2, SMALL, LANES), jnp.int16),
-        [
-            smem,
-            pl.BlockSpec((group, LANES), lambda i: (0, 0)),
-            pl.BlockSpec(half, lambda i: (0, 0, 0, 0, 0, 0)),
-            pl.BlockSpec(memory_space=pltpu.HBM),
-        ],
-        grid=(1,),
-        out_specs=pl.BlockSpec((3, pairs, 2, SMALL, LANES), lambda i: (0, 0, 0, 0, 0)),
-        scratch_shapes=[pltpu.VMEM(half[1:], jnp.float32), pltpu.SemaphoreType.DMA((4,))],
+        [smem] + [vmem] * 3,
         limit=LESS_VMEM,
         name="clip",
-    )(jnp.stack([part, core]), norms, share, got)
+    )(jnp.stack([part, core]), norms, keep, got)
 
     pieces = pieces.reshape(2 * chips, SMALL, LANES)
     pieces = lax.all_to_all(pieces, ("z", "xh", "xl"), 0, 0, tiled=True)

time: 160 us -> 160 us (level)
  waiting for transfers between devices: 39.4 us -> 45.4 us
  starting transfers between devices: 53.9 us -> 49.6 us
  blocking collectives: 50.8 us -> 48.4 us
    ppermute x3, waiting for transfers between devices: 0.01 us -> 14.9 us  [body(): ahead.append(lax.ppermute(ahead[-1], 'y', down))]
    ppermute x4, waiting for transfers between devices: 13.3 us -> 2.31 us  [body(): back.append(lax.ppermute(back[-1], 'y', up))]
    all_to_all x1, starting transfers between devices: 10.8 us -> 5.18 us  [body(): norms = lax.all_to_all(square, ('core', 'xl', 'y'), 0, 0, tiled=True)]
    ppermute x3, starting transfers between devices: 9.31 us -> 13.8 us  [body(): ahead.append(lax.ppermute(ahead[-1], 'y', down))]
    ppermute x4, starting transfers between devices: 12.6 us -> 9.54 us  [body(): back.append(lax.ppermute(back[-1], 'y', up))]
    all_to_all x1, blocking collectives: 50.8 us -> 48.4 us  [body(): pieces = lax.all_to_all(pieces, ('z', 'xh', 'xl'), 0, 0, tiled=True)]
    all_to_all x1, waiting for transfers between devices: 10.5 us -> 12.7 us  [body(): own = lax.all_to_all(grads, ('xl', 'y'), 0, 0, tiled=True)]
where the time goes in v9:
time: 160 us; the launch traced here: 159 us
  starting transfers between devices  49.6 us (31%)
  blocking collectives  48.4 us (30%)
  waiting for transfers between devices  45.4 us (28%)
  Pallas kernels  12.8 us (8%)
    all_to_all x1, blocking collectives, body(): pieces = lax.all_to_all(pieces, ('z', 'xh', 'xl'), 0, 0, tiled=True)  48.4 us
    ppermute x3, waiting for transfers between devices, body(): ahead.append(lax.ppermute(ahead[-1], 'y', down))  14.9 us
    ppermute x3, starting transfers between devices, body(): ahead.append(lax.ppermute(ahead[-1], 'y', down))  13.8 us
    all_to_all x1, starting transfers between devices, body(): own = lax.all_to_all(grads, ('xl', 'y'), 0, 0, tiled=True)  13.1 us
    all_to_all x1, waiting for transfers between devices, body(): own = lax.all_to_all(grads, ('xl', 'y'), 0, 0, tiled=True)  12.7 us
    ppermute x4, starting transfers between devices, body(): back.append(lax.ppermute(back[-1], 'y', up))  9.54 us
    ppermute x1, waiting for transfers between devices, body(): passed = lax.ppermute(half_of(1 - part), 'xl', swap)  8.54 us
    all_to_all x1, waiting for transfers between devices, body(): norms = lax.all_to_all(square, ('core', 'xl', 'y'), 0, 0, tiled=True)  6.97 us
  transfers between devices with their start and end apart: 12, of which 7 were waited for; matrix products, arithmetic and copies ran while one was open for 0% of the time, Pallas kernels for 4%

profile of v9, /device:TPU:8, one launch (start us, length us, event | category | flops | bytes accessed | tf_op | source)
XLA Modules:
  0.0 158.9 jit_solution(1869211870074264537)
XLA Ops:
  0.6 13.1 %all-to-all-start = ((bf16[16,3,104,128]{3,2,1,0:T(8,128)(2,1)}), bf16[16,3,104,128]{3,2,1,0:T(8,128)(2,1)S(1)}, u32[]{:S(2)}, u32[]{:S(2)}) async-start(bf16[16,3,104,128]{3,2,1,0:T(8,128)(2,1)} %bitcast.29), calls=%async_computation | async-start | bytes 2555904 | tf_op jit(solution)/shard_map/all_to_all | solution.py:206
  13.8 3.4 %collective-permute-start = (bf16[832,128]{1,0:T(8,128)(2,1)S(1)}, bf16[832,128]{1,0:T(8,128)(2,1)S(1)}, u32[]{:S(2)}, u32[]{:S(2)}) collective-permute-start(bf16[832,128]{1,0:T(8,128)(2,1)S(1)} %pad_maximum_fusion.1), channel_id=1, source_target_pairs={{0,8},{8,0},{1,9},{9,1},{2,10},{10,2},{3,11},{11,3},{4,12},{12,4},... | collective-permute-start | bytes 638984 | tf_op jit(solution)/shard_map/ppermute | solution.py:192
  17.3 8.5 %collective-permute-done = bf16[832,128]{1,0:T(8,128)(2,1)S(1)} collective-permute-done((bf16[832,128]{1,0:T(8,128)(2,1)S(1)}, bf16[832,128]{1,0:T(8,128)(2,1)S(1)}, u32[]{:S(2)}, u32[]{:S(2)}) %collective-permute-start) | collective-permute-done | bytes 213024 | tf_op jit(solution)/shard_map/ppermute | solution.py:192
  25.9 3.6 %collective-permute-start.1 = (bf16[2,832,128]{2,1,0:T(8,128)(2,1)S(1)}, bf16[2,832,128]{2,1,0:T(8,128)(2,1)S(1)}, u32[]{:S(2)}, u32[]{:S(2)}) collective-permute-start(bf16[2,832,128]{2,1,0:T(8,128)(2,1)S(1)} %pad_maximum_fusion.refs_0_), channel_id=1, source_target_pairs={{0,1},{1,2},{2,3},{3,4},{4,5},{5,6},{6,7},{7,0},{8,9},{9,10},{10,1... | collective-permute-start | bytes 1277960 | tf_op jit(solution)/shard_map/ppermute | solution.py:200
  29.5 12.7 %all-to-all-done.grads_ref = bf16[16,3,104,128]{3,2,1,0:T(8,128)(2,1)S(1)} async-done(((bf16[16,3,104,128]{3,2,1,0:T(8,128)(2,1)}), bf16[16,3,104,128]{3,2,1,0:T(8,128)(2,1)S(1)}, u32[]{:S(2)}, u32[]{:S(2)}) %all-to-all-start) | async-done | bytes 1277984 | tf_op jit(solution)/shard_map/all_to_all | solution.py:206
  42.3 2.7 %collective-permute-start.7 = (bf16[16,3,104,128]{3,2,1,0:T(8,128)(2,1)S(1)}, bf16[16,3,104,128]{3,2,1,0:T(8,128)(2,1)S(1)}, u32[]{:S(2)}, u32[]{:S(2)}) collective-permute-start(bf16[16,3,104,128]{3,2,1,0:T(8,128)(2,1)S(1)} %all-to-all-done.grads_ref), channel_id=1, source_target_pairs={{0,8},{8,0},{1,9},{9,1},{2,10},{10,2},{3,11},{11,3},{4,12},{12,4},... | collective-permute-start | bytes 3833864 | tf_op jit(solution)/shard_map/ppermute | solution.py:207
  44.9 5.0 %collective-permute-start.4 = (bf16[2,832,128]{2,1,0:T(8,128)(2,1)S(1)}, bf16[2,832,128]{2,1,0:T(8,128)(2,1)S(1)}, u32[]{:S(2)}, u32[]{:S(2)}) collective-permute-start(bf16[2,832,128]{2,1,0:T(8,128)(2,1)S(1)} %pad_maximum_fusion.refs_0_), channel_id=1, source_target_pairs={{0,7},{1,0},{2,1},{3,2},{4,3},{5,4},{6,5},{7,6},{8,15},{9,8},{10,9... | collective-permute-start | bytes 1277960 | tf_op jit(solution)/shard_map/ppermute | solution.py:201
  50.0 1.9 %collective-permute-start.2 = (bf16[2,832,128]{2,1,0:T(8,128)(2,1)S(1)}, bf16[2,832,128]{2,1,0:T(8,128)(2,1)}, u32[]{:S(2)}, u32[]{:S(2)}) collective-permute-start(bf16[2,832,128]{2,1,0:T(8,128)(2,1)S(1)} %collective-permute-done.1.refs_1_), channel_id=1, source_target_pairs={{0,1},{1,2},{2,3},{3,4},{4,5},{5,6},{6,7},{7,0},{8,9},{9,10},{10,1... | collective-permute-start | bytes 1277960 | tf_op jit(solution)/shard_map/ppermute | solution.py:200
  51.9 8.1 %collective-permute-done.4.refs_6_ = bf16[2,832,128]{2,1,0:T(8,128)(2,1)S(1)} collective-permute-done((bf16[2,832,128]{2,1,0:T(8,128)(2,1)S(1)}, bf16[2,832,128]{2,1,0:T(8,128)(2,1)S(1)}, u32[]{:S(2)}, u32[]{:S(2)}) %collective-permute-start.4) | collective-permute-done | bytes 426016 | tf_op jit(solution)/shard_map/ppermute | solution.py:201
  60.0 4.4 %collective-permute-start.5 = (bf16[2,832,128]{2,1,0:T(8,128)(2,1)S(1)}, bf16[2,832,128]{2,1,0:T(8,128)(2,1)}, u32[]{:S(2)}, u32[]{:S(2)}) collective-permute-start(bf16[2,832,128]{2,1,0:T(8,128)(2,1)S(1)} %collective-permute-done.4.refs_6_), channel_id=1, source_target_pairs={{0,7},{1,0},{2,1},{3,2},{4,3},{5,4},{6,5},{7,6},{8,15},{9,8},{10,9... | collective-permute-start | bytes 1277960 | tf_op jit(solution)/shard_map/ppermute | solution.py:201
  65.2 1.9 %collective-permute-start.3 = (bf16[2,832,128]{2,1,0:T(8,128)(2,1)}, bf16[2,832,128]{2,1,0:T(8,128)(2,1)}, u32[]{:S(2)}, u32[]{:S(2)}) collective-permute-start(bf16[2,832,128]{2,1,0:T(8,128)(2,1)} %collective-permute-done.2.refs_2_), channel_id=1, source_target_pairs={{0,1},{1,2},{2,3},{3,4},{4,5},{5,6},{6,7},{7,0},{8,9},{9,10},{10,1... | collective-permute-start | bytes 1277960 | tf_op jit(solution)/shard_map/ppermute | solution.py:200
  67.1 6.8 %collective-permute-done.5.refs_5_ = bf16[2,832,128]{2,1,0:T(8,128)(2,1)} collective-permute-done((bf16[2,832,128]{2,1,0:T(8,128)(2,1)S(1)}, bf16[2,832,128]{2,1,0:T(8,128)(2,1)}, u32[]{:S(2)}, u32[]{:S(2)}) %collective-permute-start.5) | collective-permute-done | bytes 426016 | tf_op jit(solution)/shard_map/ppermute | solution.py:201
  73.9 4.4 %collective-permute-start.6 = (bf16[2,832,128]{2,1,0:T(8,128)(2,1)}, bf16[2,832,128]{2,1,0:T(8,128)(2,1)}, u32[]{:S(2)}, u32[]{:S(2)}) collective-permute-start(bf16[2,832,128]{2,1,0:T(8,128)(2,1)} %collective-permute-done.5.refs_5_), channel_id=1, source_target_pairs={{0,7},{1,0},{2,1},{3,2},{4,3},{5,4},{6,5},{7,6},{8,15},{9,8},{10,9... | collective-permute-start | bytes 1277960 | tf_op jit(solution)/shard_map/ppermute | solution.py:201
  79.7 2.1 %collective-permute-start.8 = (bf16[2,832,128]{2,1,0:T(8,128)(2,1)}, bf16[2,832,128]{2,1,0:T(8,128)(2,1)S(1)}, u32[]{:S(2)}, u32[]{:S(2)}) collective-permute-start(bf16[2,832,128]{2,1,0:T(8,128)(2,1)} %collective-permute-done.3.refs_3_), channel_id=1, source_target_pairs={{0,1},{1,2},{2,3},{3,4},{4,5},{5,6},{6,7},{7,0},{8,9},{9,10},{10,1... | collective-permute-start | bytes 1277960 | tf_op jit(solution)/shard_map/ppermute | solution.py:202
  81.9 1.3 prepare.2.refs_7_.own_ref
  84.5 3.9 %sum.1.partial_ref = f32[3,832,256]{2,1,0:T(8,128)S(1)} custom-call(bf16[2,832,128]{2,1,0:T(8,128)(2,1)S(1)} %pad_maximum_fusion.refs_0_, bf16[2,832,128]{2,1,0:T(8,128)(2,1)S(1)} %collective-permute-done.1.refs_1_, bf16[2,832,128]{2,1,0:T(8,128)(2,1)} %collective-permute-done.2.refs_2_, bf16[2,832,128]{2,1,0:T(8,128)(2,1)} %collective-permute-done.3.refs_3_, ...), custom_call_target="tpu_custom_call" | custom-call | flops 2290089984 | bytes 8388608 | tf_op jit(solution)/shard_map/sum/pallas_call | solution.py:221
  88.4 1.5 collective-permute-done.8.x_ref
  89.9 2.3 %multiply.1 = (f32[8,3,2,56,128]{4,3,2,1,0:T(8,128)S(1)}, f32[8,3,2,56,128]{4,3,2,1,0:T(8,128)}, f32[32,128]{1,0:T(8,128)}) custom-call(s32[3]{0:T(128)S(1)} %add_add_fusion.place, f32[3,832,256]{2,1,0:T(8,128)S(1)} %sum.1.partial_ref, bf16[2,832,128]{2,1,0:T(8,128)(2,1)S(1)} %collective-permute-done.8.x_ref, ...), custom_call_target="tpu_custom_call" | custom-call | tf_op jit(solution)/shard_map/multiply/pallas_call | solution.py:231
  92.2 1.9 %collective-permute-start.9 = (f32[8,3,2,56,128]{4,3,2,1,0:T(8,128)}, f32[8,3,2,56,128]{4,3,2,1,0:T(8,128)S(1)}, u32[]{:S(2)}, u32[]{:S(2)}) collective-permute-start(f32[8,3,2,56,128]{4,3,2,1,0:T(8,128)} %get-tuple-element.8), channel_id=1, source_target_pairs={{0,16},{16,0},{1,17},{17,1},{2,18},{18,2},{3,19},{19,3},{4,20},{20... | collective-permute-start | bytes 4128776 | tf_op jit(solution)/shard_map/ppermute | solution.py:241
  94.1 5.2 %all-to-all-start.1 = ((f32[32,1,128]{2,1,0:T(1,128)}), f32[32,1,128]{2,1,0:T(1,128)S(1)}, u32[]{:S(2)}, u32[]{:S(2)}) async-start(f32[32,1,128]{2,1,0:T(1,128)} %bitcast.12), calls=%async_computation.1 | async-start | bytes 32768 | tf_op jit(solution)/shard_map/all_to_all | solution.py:240
  99.4 7.0 %all-to-all-done.1 = f32[32,1,128]{2,1,0:T(1,128)S(1)} async-done(((f32[32,1,128]{2,1,0:T(1,128)}), f32[32,1,128]{2,1,0:T(1,128)S(1)}, u32[]{:S(2)}, u32[]{:S(2)}) %all-to-all-start.1) | async-done | bytes 16416 | tf_op jit(solution)/shard_map/all_to_all | solution.py:240
  106.4 2.7 %clip.1 = s16[3,8,2,48,128]{4,3,2,1,0:T(8,128)(2,1)S(1)} custom-call(s32[2]{0:T(128)S(1)} %pad_add_fusion.place, f32[32,128]{1,0:T(8,128)S(1)} %bitcast.28, f32[8,3,2,56,128]{4,3,2,1,0:T(8,128)S(1)} %get-tuple-element.7.keep_ref, f32[8,3,2,56,128]{4,3,2,1,0:T(8,128)S(1)} %collective-permute-done.9.got_ref), custom_call_target="tpu_custom_call" | custom-call | tf_op jit(solution)/shard_map/clip/pallas_call | solution.py:242
  109.1 48.4 %all_to_all.21 = s16[48,48,128]{2,1,0:T(8,128)(2,1)S(1)} all-to-all(s16[48,48,128]{2,1,0:T(8,128)(2,1)S(1)} %bitcast.27), channel_id=1, replica_groups=mesh['z'=12,'xh'=2,'core'=2,'xl'=2,'y'=8] {'z','xh','xl'}, dimensions={0} | all-to-all | bytes 1179648 | tf_op jit(solution)/shard_map/all_to_all | solution.py:251
  157.5 1.4 update.1
  (27 shorter events, 3.2 us)
Async XLA Ops:
  0.6 13.1 %copy-start.5 = (bf16[1,1,1664,128]{3,2,1,0:T(8,128)(2,1)S(1)}, bf16[1,1,1664,128]{3,2,1,0:T(8,128)(2,1)}, u32[]{:S(2)}) copy-start(bf16[1,1,1664,128]{3,2,1,0:T(8,128)(2,1)} %param.6) | copy-start | bytes 1277956
  0.6 41.6 %all-to-all-start = ((bf16[16,3,104,128]{3,2,1,0:T(8,128)(2,1)}), bf16[16,3,104,128]{3,2,1,0:T(8,128)(2,1)S(1)}, u32[]{:S(2)}, u32[]{:S(2)}) async-start(bf16[16,3,104,128]{3,2,1,0:T(8,128)(2,1)} %bitcast.29), calls=%async_computation | async-start | bytes 2555904 | tf_op jit(solution)/shard_map/all_to_all | solution.py:206
  13.8 12.0 %collective-permute-start = (bf16[832,128]{1,0:T(8,128)(2,1)S(1)}, bf16[832,128]{1,0:T(8,128)(2,1)S(1)}, u32[]{:S(2)}, u32[]{:S(2)}) collective-permute-start(bf16[832,128]{1,0:T(8,128)(2,1)S(1)} %pad_maximum_fusion.1), channel_id=1, source_target_pairs={{0,8},{8,0},{1,9},{9,1},{2,10},{10,2},{3,11},{11,3},{4,12},{12,4},... | collective-permute-start | bytes 638984 | tf_op jit(solution)/shard_map/ppermute | solution.py:192
  25.9 24.1 %collective-permute-start.1 = (bf16[2,832,128]{2,1,0:T(8,128)(2,1)S(1)}, bf16[2,832,128]{2,1,0:T(8,128)(2,1)S(1)}, u32[]{:S(2)}, u32[]{:S(2)}) collective-permute-start(bf16[2,832,128]{2,1,0:T(8,128)(2,1)S(1)} %pad_maximum_fusion.refs_0_), channel_id=1, source_target_pairs={{0,1},{1,2},{2,3},{3,4},{4,5},{5,6},{6,7},{7,0},{8,9},{9,10},{10,1... | collective-permute-start | bytes 1277960 | tf_op jit(solution)/shard_map/ppermute | solution.py:200
  42.3 40.9 %collective-permute-start.7 = (bf16[16,3,104,128]{3,2,1,0:T(8,128)(2,1)S(1)}, bf16[16,3,104,128]{3,2,1,0:T(8,128)(2,1)S(1)}, u32[]{:S(2)}, u32[]{:S(2)}) collective-permute-start(bf16[16,3,104,128]{3,2,1,0:T(8,128)(2,1)S(1)} %all-to-all-done.grads_ref), channel_id=1, source_target_pairs={{0,8},{8,0},{1,9},{9,1},{2,10},{10,2},{3,11},{11,3},{4,12},{12,4},... | collective-permute-start | bytes 3833864 | tf_op jit(solution)/shard_map/ppermute | solution.py:207
  44.9 15.0 %collective-permute-start.4 = (bf16[2,832,128]{2,1,0:T(8,128)(2,1)S(1)}, bf16[2,832,128]{2,1,0:T(8,128)(2,1)S(1)}, u32[]{:S(2)}, u32[]{:S(2)}) collective-permute-start(bf16[2,832,128]{2,1,0:T(8,128)(2,1)S(1)} %pad_maximum_fusion.refs_0_), channel_id=1, source_target_pairs={{0,7},{1,0},{2,1},{3,2},{4,3},{5,4},{6,5},{7,6},{8,15},{9,8},{10,9... | collective-permute-start | bytes 1277960 | tf_op jit(solution)/shard_map/ppermute | solution.py:201
  50.0 15.2 %collective-permute-start.2 = (bf16[2,832,128]{2,1,0:T(8,128)(2,1)S(1)}, bf16[2,832,128]{2,1,0:T(8,128)(2,1)}, u32[]{:S(2)}, u32[]{:S(2)}) collective-permute-start(bf16[2,832,128]{2,1,0:T(8,128)(2,1)S(1)} %collective-permute-done.1.refs_1_), channel_id=1, source_target_pairs={{0,1},{1,2},{2,3},{3,4},{4,5},{5,6},{6,7},{7,0},{8,9},{9,10},{10,1... | collective-permute-start | bytes 1277960 | tf_op jit(solution)/shard_map/ppermute | solution.py:200
  60.0 13.9 %collective-permute-start.5 = (bf16[2,832,128]{2,1,0:T(8,128)(2,1)S(1)}, bf16[2,832,128]{2,1,0:T(8,128)(2,1)}, u32[]{:S(2)}, u32[]{:S(2)}) collective-permute-start(bf16[2,832,128]{2,1,0:T(8,128)(2,1)S(1)} %collective-permute-done.4.refs_6_), channel_id=1, source_target_pairs={{0,7},{1,0},{2,1},{3,2},{4,3},{5,4},{6,5},{7,6},{8,15},{9,8},{10,9... | collective-permute-start | bytes 1277960 | tf_op jit(solution)/shard_map/ppermute | solution.py:201
  64.4 0.8 copy-start
  65.2 14.5 %collective-permute-start.3 = (bf16[2,832,128]{2,1,0:T(8,128)(2,1)}, bf16[2,832,128]{2,1,0:T(8,128)(2,1)}, u32[]{:S(2)}, u32[]{:S(2)}) collective-permute-start(bf16[2,832,128]{2,1,0:T(8,128)(2,1)} %collective-permute-done.2.refs_2_), channel_id=1, source_target_pairs={{0,1},{1,2},{2,3},{3,4},{4,5},{5,6},{6,7},{7,0},{8,9},{9,10},{10,1... | collective-permute-start | bytes 1277960 | tf_op jit(solution)/shard_map/ppermute | solution.py:200
  73.9 10.6 %collective-permute-start.6 = (bf16[2,832,128]{2,1,0:T(8,128)(2,1)}, bf16[2,832,128]{2,1,0:T(8,128)(2,1)}, u32[]{:S(2)}, u32[]{:S(2)}) collective-permute-start(bf16[2,832,128]{2,1,0:T(8,128)(2,1)} %collective-permute-done.5.refs_5_), channel_id=1, source_target_pairs={{0,7},{1,0},{2,1},{3,2},{4,3},{5,4},{6,5},{7,6},{8,15},{9,8},{10,9... | collective-permute-start | bytes 1277960 | tf_op jit(solution)/shard_map/ppermute | solution.py:201
  79.7 10.2 %collective-permute-start.8 = (bf16[2,832,128]{2,1,0:T(8,128)(2,1)}, bf16[2,832,128]{2,1,0:T(8,128)(2,1)S(1)}, u32[]{:S(2)}, u32[]{:S(2)}) collective-permute-start(bf16[2,832,128]{2,1,0:T(8,128)(2,1)} %collective-permute-done.3.refs_3_), channel_id=1, source_target_pairs={{0,1},{1,2},{2,3},{3,4},{4,5},{5,6},{6,7},{7,0},{8,9},{9,10},{10,1... | collective-permute-start | bytes 1277960 | tf_op jit(solution)/shard_map/ppermute | solution.py:202
  83.2 1.3 copy-start.1
  92.2 14.2 %collective-permute-start.9 = (f32[8,3,2,56,128]{4,3,2,1,0:T(8,128)}, f32[8,3,2,56,128]{4,3,2,1,0:T(8,128)S(1)}, u32[]{:S(2)}, u32[]{:S(2)}) collective-permute-start(f32[8,3,2,56,128]{4,3,2,1,0:T(8,128)} %get-tuple-element.8), channel_id=1, source_target_pairs={{0,16},{16,0},{1,17},{17,1},{2,18},{18,2},{3,19},{19,3},{4,20},{20... | collective-permute-start | bytes 4128776 | tf_op jit(solution)/shard_map/ppermute | solution.py:241
  94.1 12.2 %all-to-all-start.1 = ((f32[32,1,128]{2,1,0:T(1,128)}), f32[32,1,128]{2,1,0:T(1,128)S(1)}, u32[]{:S(2)}, u32[]{:S(2)}) async-start(f32[32,1,128]{2,1,0:T(1,128)} %bitcast.12), calls=%async_computation.1 | async-start | bytes 32768 | tf_op jit(solution)/shard_map/all_to_all | solution.py:240
  106.4 51.1 %copy-start.2 = (f32[104,104]{1,0:T(8,128)S(1)}, f32[104,104]{1,0:T(8,128)}, u32[]{:S(2)}) copy-start(f32[104,104]{1,0:T(8,128)} %noise_ref.1) | copy-start | bytes 129796
  106.4 51.1 %copy-start.3 = (f32[104,104]{1,0:T(8,128)S(1)}, f32[104,104]{1,0:T(8,128)}, u32[]{:S(2)}) copy-start(f32[104,104]{1,0:T(8,128)} %first_ref.1) | copy-start | bytes 129796
  106.4 51.1 %copy-start.4 = (f32[104,104]{1,0:T(8,128)S(1)}, f32[104,104]{1,0:T(8,128)}, u32[]{:S(2)}) copy-start(f32[104,104]{1,0:T(8,128)} %second_ref.1) | copy-start | bytes 129796

commit v10 on v9

--- a/solution.py
+++ b/solution.py
@@ -223,7 +223,6 @@
         jax.ShapeDtypeStruct((3, rows, 2 * LANES), jnp.float32),
         [vmem] * (len(x) + 2),
         limit=LESS_VMEM,
-        cost_estimate=pl.CostEstimate(flops=12 * rows * LANES * (augs - 2) * tokens, bytes_accessed=1 << 23, transcendentals=0),
         name="sum",
     )(*x, *y)
     group = 2 * augs

time: 160 us -> 159 us (level)
  waiting for transfers between devices: 45.4 us -> 37.7 us
  starting transfers between devices: 49.6 us -> 53.8 us
  blocking collectives: 48.4 us -> 50.8 us
    ppermute x3, waiting for transfers between devices: 14.9 us -> 0.06 us  [body(): ahead.append(lax.ppermute(ahead[-1], 'y', down))]
    ppermute x4, waiting for transfers between devices: 2.31 us -> 11.6 us  [body(): back.append(lax.ppermute(back[-1], 'y', up))]
    all_to_all x1, starting transfers between devices: 5.18 us -> 10.8 us  [body(): norms = lax.all_to_all(square, ('core', 'xl', 'y'), 0, 0, tiled=True)]
    ppermute x3, starting transfers between devices: 13.8 us -> 9.24 us  [body(): ahead.append(lax.ppermute(ahead[-1], 'y', down))]
    ppermute x4, starting transfers between devices: 9.54 us -> 12.6 us  [body(): back.append(lax.ppermute(back[-1], 'y', up))]
    all_to_all x1, blocking collectives: 48.4 us -> 50.8 us  [body(): pieces = lax.all_to_all(pieces, ('z', 'xh', 'xl'), 0, 0, tiled=True)]
    all_to_all x1, waiting for transfers between devices: 12.7 us -> 10.5 us  [body(): own = lax.all_to_all(grads, ('xl', 'y'), 0, 0, tiled=True)]
  transfers between devices with their start and end apart: 12 -> 12, of which waited for: 7 -> 8; matrix products, arithmetic and copies ran while one was open for 0% -> 0% of each run, Pallas kernels for 4% -> 4%
where the time goes in v10:
time: 159 us
  starting transfers between devices  53.8 us (34%)
  blocking collectives  50.8 us (32%)
  waiting for transfers between devices  37.7 us (24%)
  Pallas kernels  12.8 us (8%)
  local copies, waits for them, and re-layouts  1.59 us (1%)
    all_to_all x1, blocking collectives, body(): pieces = lax.all_to_all(pieces, ('z', 'xh', 'xl'), 0, 0, tiled=True)  50.8 us
    all_to_all x1, starting transfers between devices, body(): own = lax.all_to_all(grads, ('xl', 'y'), 0, 0, tiled=True)  13.1 us
    ppermute x4, starting transfers between devices, body(): back.append(lax.ppermute(back[-1], 'y', up))  12.6 us
    ppermute x4, waiting for transfers between devices, body(): back.append(lax.ppermute(back[-1], 'y', up))  11.6 us
    all_to_all x1, starting transfers between devices, body(): norms = lax.all_to_all(square, ('core', 'xl', 'y'), 0, 0, tiled=True)  10.8 us
    all_to_all x1, waiting for transfers between devices, body(): own = lax.all_to_all(grads, ('xl', 'y'), 0, 0, tiled=True)  10.5 us
    ppermute x3, starting transfers between devices, body(): ahead.append(lax.ppermute(ahead[-1], 'y', down))  9.24 us
    ppermute x1, waiting for transfers between devices, body(): passed = lax.ppermute(half_of(1 - part), 'xl', swap)  8.54 us
  transfers between devices with their start and end apart: 12, of which 8 were waited for; matrix products, arithmetic and copies ran while one was open for 0% of the time, Pallas kernels for 4%

profile of v10, /device:TPU:8, one launch (start us, length us, event | category | flops | bytes accessed | tf_op | source)
XLA Modules:
  0.0 158.6 jit_solution(11011192164992547664)
XLA Ops:
  0.6 13.1 %all-to-all-start = ((bf16[16,3,104,128]{3,2,1,0:T(8,128)(2,1)}), bf16[16,3,104,128]{3,2,1,0:T(8,128)(2,1)S(1)}, u32[]{:S(2)}, u32[]{:S(2)}) async-start(bf16[16,3,104,128]{3,2,1,0:T(8,128)(2,1)} %bitcast.29), calls=%async_computation | async-start | bytes 2555904 | tf_op jit(solution)/shard_map/all_to_all | solution.py:206
  13.8 3.4 %collective-permute-start = (bf16[832,128]{1,0:T(8,128)(2,1)S(1)}, bf16[832,128]{1,0:T(8,128)(2,1)S(1)}, u32[]{:S(2)}, u32[]{:S(2)}) collective-permute-start(bf16[832,128]{1,0:T(8,128)(2,1)S(1)} %pad_maximum_fusion.1), channel_id=1, source_target_pairs={{0,8},{8,0},{1,9},{9,1},{2,10},{10,2},{3,11},{11,3},{4,12},{12,4},... | collective-permute-start | bytes 638984 | tf_op jit(solution)/shard_map/ppermute | solution.py:192
  17.3 8.5 %collective-permute-done = bf16[832,128]{1,0:T(8,128)(2,1)S(1)} collective-permute-done((bf16[832,128]{1,0:T(8,128)(2,1)S(1)}, bf16[832,128]{1,0:T(8,128)(2,1)S(1)}, u32[]{:S(2)}, u32[]{:S(2)}) %collective-permute-start) | collective-permute-done | bytes 213024 | tf_op jit(solution)/shard_map/ppermute | solution.py:192
  25.9 3.6 %collective-permute-start.1 = (bf16[2,832,128]{2,1,0:T(8,128)(2,1)S(1)}, bf16[2,832,128]{2,1,0:T(8,128)(2,1)S(1)}, u32[]{:S(2)}, u32[]{:S(2)}) collective-permute-start(bf16[2,832,128]{2,1,0:T(8,128)(2,1)S(1)} %pad_maximum_fusion.refs_0_), channel_id=1, source_target_pairs={{0,1},{1,2},{2,3},{3,4},{4,5},{5,6},{6,7},{7,0},{8,9},{9,10},{10,1... | collective-permute-start | bytes 1277960 | tf_op jit(solution)/shard_map/ppermute | solution.py:200
  29.5 2.2 %collective-permute-start.4 = (bf16[2,832,128]{2,1,0:T(8,128)(2,1)S(1)}, bf16[2,832,128]{2,1,0:T(8,128)(2,1)}, u32[]{:S(2)}, u32[]{:S(2)}) collective-permute-start(bf16[2,832,128]{2,1,0:T(8,128)(2,1)S(1)} %pad_maximum_fusion.refs_0_), channel_id=1, source_target_pairs={{0,7},{1,0},{2,1},{3,2},{4,3},{5,4},{6,5},{7,6},{8,15},{9,8},{10,9... | collective-permute-start | bytes 1277960 | tf_op jit(solution)/shard_map/ppermute | solution.py:201
  31.7 10.5 %all-to-all-done.grads_ref = bf16[16,3,104,128]{3,2,1,0:T(8,128)(2,1)S(1)} async-done(((bf16[16,3,104,128]{3,2,1,0:T(8,128)(2,1)}), bf16[16,3,104,128]{3,2,1,0:T(8,128)(2,1)S(1)}, u32[]{:S(2)}, u32[]{:S(2)}) %all-to-all-start) | async-done | bytes 1277984 | tf_op jit(solution)/shard_map/all_to_all | solution.py:206
  42.3 2.7 %collective-permute-start.7 = (bf16[16,3,104,128]{3,2,1,0:T(8,128)(2,1)S(1)}, bf16[16,3,104,128]{3,2,1,0:T(8,128)(2,1)S(1)}, u32[]{:S(2)}, u32[]{:S(2)}) collective-permute-start(bf16[16,3,104,128]{3,2,1,0:T(8,128)(2,1)S(1)} %all-to-all-done.grads_ref), channel_id=1, source_target_pairs={{0,8},{8,0},{1,9},{9,1},{2,10},{10,2},{3,11},{11,3},{4,12},{12,4},... | collective-permute-start | bytes 3833864 | tf_op jit(solution)/shard_map/ppermute | solution.py:207
  44.9 1.5 collective-permute-done.1.refs_1_
  46.5 3.3 %collective-permute-start.2 = (bf16[2,832,128]{2,1,0:T(8,128)(2,1)S(1)}, bf16[2,832,128]{2,1,0:T(8,128)(2,1)S(1)}, u32[]{:S(2)}, u32[]{:S(2)}) collective-permute-start(bf16[2,832,128]{2,1,0:T(8,128)(2,1)S(1)} %collective-permute-done.1.refs_1_), channel_id=1, source_target_pairs={{0,1},{1,2},{2,3},{3,4},{4,5},{5,6},{6,7},{7,0},{8,9},{9,10},{10,1... | collective-permute-start | bytes 1277960 | tf_op jit(solution)/shard_map/ppermute | solution.py:200
  50.6 3.3 %collective-permute-start.5 = (bf16[2,832,128]{2,1,0:T(8,128)(2,1)}, bf16[2,832,128]{2,1,0:T(8,128)(2,1)}, u32[]{:S(2)}, u32[]{:S(2)}) collective-permute-start(bf16[2,832,128]{2,1,0:T(8,128)(2,1)} %collective-permute-done.4.refs_6_), channel_id=1, source_target_pairs={{0,7},{1,0},{2,1},{3,2},{4,3},{5,4},{6,5},{7,6},{8,15},{9,8},{10,9... | collective-permute-start | bytes 1277960 | tf_op jit(solution)/shard_map/ppermute | solution.py:201
  53.9 4.8 %collective-permute-done.2.refs_2_ = bf16[2,832,128]{2,1,0:T(8,128)(2,1)S(1)} collective-permute-done((bf16[2,832,128]{2,1,0:T(8,128)(2,1)S(1)}, bf16[2,832,128]{2,1,0:T(8,128)(2,1)S(1)}, u32[]{:S(2)}, u32[]{:S(2)}) %collective-permute-start.2) | collective-permute-done | bytes 426016 | tf_op jit(solution)/shard_map/ppermute | solution.py:200
  58.8 3.0 %collective-permute-start.3 = (bf16[2,832,128]{2,1,0:T(8,128)(2,1)S(1)}, bf16[2,832,128]{2,1,0:T(8,128)(2,1)}, u32[]{:S(2)}, u32[]{:S(2)}) collective-permute-start(bf16[2,832,128]{2,1,0:T(8,128)(2,1)S(1)} %collective-permute-done.2.refs_2_), channel_id=1, source_target_pairs={{0,1},{1,2},{2,3},{3,4},{4,5},{5,6},{6,7},{7,0},{8,9},{9,10},{10,1... | collective-permute-start | bytes 1277960 | tf_op jit(solution)/shard_map/ppermute | solution.py:200
  62.6 3.7 %collective-permute-start.6 = (bf16[2,832,128]{2,1,0:T(8,128)(2,1)}, bf16[2,832,128]{2,1,0:T(8,128)(2,1)}, u32[]{:S(2)}, u32[]{:S(2)}) collective-permute-start(bf16[2,832,128]{2,1,0:T(8,128)(2,1)} %collective-permute-done.5.refs_5_), channel_id=1, source_target_pairs={{0,7},{1,0},{2,1},{3,2},{4,3},{5,4},{6,5},{7,6},{8,15},{9,8},{10,9... | collective-permute-start | bytes 1277960 | tf_op jit(solution)/shard_map/ppermute | solution.py:201
  66.3 4.0 %collective-permute-done.3.refs_3_ = bf16[2,832,128]{2,1,0:T(8,128)(2,1)} collective-permute-done((bf16[2,832,128]{2,1,0:T(8,128)(2,1)S(1)}, bf16[2,832,128]{2,1,0:T(8,128)(2,1)}, u32[]{:S(2)}, u32[]{:S(2)}) %collective-permute-start.3) | collective-permute-done | bytes 426016 | tf_op jit(solution)/shard_map/ppermute | solution.py:200
  70.4 2.7 %collective-permute-start.8 = (bf16[2,832,128]{2,1,0:T(8,128)(2,1)}, bf16[2,832,128]{2,1,0:T(8,128)(2,1)S(1)}, u32[]{:S(2)}, u32[]{:S(2)}) collective-permute-start(bf16[2,832,128]{2,1,0:T(8,128)(2,1)} %collective-permute-done.3.refs_3_), channel_id=1, source_target_pairs={{0,1},{1,2},{2,3},{3,4},{4,5},{5,6},{6,7},{7,0},{8,9},{9,10},{10,1... | collective-permute-start | bytes 1277960 | tf_op jit(solution)/shard_map/ppermute | solution.py:202
  73.8 1.3 prepare.2.refs_7_.own_ref
  76.4 3.9 %sum.1.partial_ref = f32[3,832,256]{2,1,0:T(8,128)S(1)} custom-call(bf16[2,832,128]{2,1,0:T(8,128)(2,1)S(1)} %pad_maximum_fusion.refs_0_, bf16[2,832,128]{2,1,0:T(8,128)(2,1)S(1)} %copy-done.1, bf16[2,832,128]{2,1,0:T(8,128)(2,1)S(1)} %copy-done.3, bf16[2,832,128]{2,1,0:T(8,128)(2,1)} %collective-permute-done.3.refs_3_, ...), custom_call_target="tpu_custom_call" | custom-call | tf_op jit(solution)/shard_map/sum/pallas_call | solution.py:221
  81.5 2.3 %multiply.1 = (f32[8,3,2,56,128]{4,3,2,1,0:T(8,128)S(1)}, f32[8,3,2,56,128]{4,3,2,1,0:T(8,128)}, f32[32,128]{1,0:T(8,128)}) custom-call(s32[3]{0:T(128)S(1)} %add_add_fusion.place, f32[3,832,256]{2,1,0:T(8,128)S(1)} %sum.1.partial_ref, bf16[2,832,128]{2,1,0:T(8,128)(2,1)S(1)} %collective-permute-done.8.x_ref, ...), custom_call_target="tpu_custom_call" | custom-call | tf_op jit(solution)/shard_map/multiply/pallas_call | solution.py:230
  83.8 1.9 %collective-permute-start.9 = (f32[8,3,2,56,128]{4,3,2,1,0:T(8,128)}, f32[8,3,2,56,128]{4,3,2,1,0:T(8,128)S(1)}, u32[]{:S(2)}, u32[]{:S(2)}) collective-permute-start(f32[8,3,2,56,128]{4,3,2,1,0:T(8,128)} %get-tuple-element.8), channel_id=1, source_target_pairs={{0,16},{16,0},{1,17},{17,1},{2,18},{18,2},{3,19},{19,3},{4,20},{20... | collective-permute-start | bytes 4128776 | tf_op jit(solution)/shard_map/ppermute | solution.py:240
  85.7 10.8 %all-to-all-start.1 = ((f32[32,1,128]{2,1,0:T(1,128)}), f32[32,1,128]{2,1,0:T(1,128)S(1)}, u32[]{:S(2)}, u32[]{:S(2)}) async-start(f32[32,1,128]{2,1,0:T(1,128)} %bitcast.12), calls=%async_computation.1 | async-start | bytes 32768 | tf_op jit(solution)/shard_map/all_to_all | solution.py:239
  96.6 7.0 %all-to-all-done.1 = f32[32,1,128]{2,1,0:T(1,128)S(1)} async-done(((f32[32,1,128]{2,1,0:T(1,128)}), f32[32,1,128]{2,1,0:T(1,128)S(1)}, u32[]{:S(2)}, u32[]{:S(2)}) %all-to-all-start.1) | async-done | bytes 16416 | tf_op jit(solution)/shard_map/all_to_all | solution.py:239
  103.6 2.7 %clip.1 = s16[3,8,2,48,128]{4,3,2,1,0:T(8,128)(2,1)S(1)} custom-call(s32[2]{0:T(128)S(1)} %pad_add_fusion.place, f32[32,128]{1,0:T(8,128)S(1)} %bitcast.28, f32[8,3,2,56,128]{4,3,2,1,0:T(8,128)S(1)} %get-tuple-element.7.keep_ref, f32[8,3,2,56,128]{4,3,2,1,0:T(8,128)S(1)} %collective-permute-done.9.got_ref), custom_call_target="tpu_custom_call" | custom-call | tf_op jit(solution)/shard_map/clip/pallas_call | solution.py:241
  106.3 50.8 %all_to_all.21 = s16[48,48,128]{2,1,0:T(8,128)(2,1)S(1)} all-to-all(s16[48,48,128]{2,1,0:T(8,128)(2,1)S(1)} %bitcast.27), channel_id=1, replica_groups=mesh['z'=12,'xh'=2,'core'=2,'xl'=2,'y'=8] {'z','xh','xl'}, dimensions={0} | all-to-all | bytes 1179648 | tf_op jit(solution)/shard_map/all_to_all | solution.py:250
  157.2 1.4 update.1
  (31 shorter events, 4.4 us)
Async XLA Ops:
  0.6 13.1 %copy-start.7 = (bf16[1,1,1664,128]{3,2,1,0:T(8,128)(2,1)S(1)}, bf16[1,1,1664,128]{3,2,1,0:T(8,128)(2,1)}, u32[]{:S(2)}) copy-start(bf16[1,1,1664,128]{3,2,1,0:T(8,128)(2,1)} %param.6) | copy-start | bytes 1277956
  0.6 41.6 %all-to-all-start = ((bf16[16,3,104,128]{3,2,1,0:T(8,128)(2,1)}), bf16[16,3,104,128]{3,2,1,0:T(8,128)(2,1)S(1)}, u32[]{:S(2)}, u32[]{:S(2)}) async-start(bf16[16,3,104,128]{3,2,1,0:T(8,128)(2,1)} %bitcast.29), calls=%async_computation | async-start | bytes 2555904 | tf_op jit(solution)/shard_map/all_to_all | solution.py:206
  13.8 12.0 %collective-permute-start = (bf16[832,128]{1,0:T(8,128)(2,1)S(1)}, bf16[832,128]{1,0:T(8,128)(2,1)S(1)}, u32[]{:S(2)}, u32[]{:S(2)}) collective-permute-start(bf16[832,128]{1,0:T(8,128)(2,1)S(1)} %pad_maximum_fusion.1), channel_id=1, source_target_pairs={{0,8},{8,0},{1,9},{9,1},{2,10},{10,2},{3,11},{11,3},{4,12},{12,4},... | collective-permute-start | bytes 638984 | tf_op jit(solution)/shard_map/ppermute | solution.py:192
  25.9 20.6 %collective-permute-start.1 = (bf16[2,832,128]{2,1,0:T(8,128)(2,1)S(1)}, bf16[2,832,128]{2,1,0:T(8,128)(2,1)S(1)}, u32[]{:S(2)}, u32[]{:S(2)}) collective-permute-start(bf16[2,832,128]{2,1,0:T(8,128)(2,1)S(1)} %pad_maximum_fusion.refs_0_), channel_id=1, source_target_pairs={{0,1},{1,2},{2,3},{3,4},{4,5},{5,6},{6,7},{7,0},{8,9},{9,10},{10,1... | collective-permute-start | bytes 1277960 | tf_op jit(solution)/shard_map/ppermute | solution.py:200
  29.5 21.1 %collective-permute-start.4 = (bf16[2,832,128]{2,1,0:T(8,128)(2,1)S(1)}, bf16[2,832,128]{2,1,0:T(8,128)(2,1)}, u32[]{:S(2)}, u32[]{:S(2)}) collective-permute-start(bf16[2,832,128]{2,1,0:T(8,128)(2,1)S(1)} %pad_maximum_fusion.refs_0_), channel_id=1, source_target_pairs={{0,7},{1,0},{2,1},{3,2},{4,3},{5,4},{6,5},{7,6},{8,15},{9,8},{10,9... | collective-permute-start | bytes 1277960 | tf_op jit(solution)/shard_map/ppermute | solution.py:201
  42.3 32.8 %collective-permute-start.7 = (bf16[16,3,104,128]{3,2,1,0:T(8,128)(2,1)S(1)}, bf16[16,3,104,128]{3,2,1,0:T(8,128)(2,1)S(1)}, u32[]{:S(2)}, u32[]{:S(2)}) collective-permute-start(bf16[16,3,104,128]{3,2,1,0:T(8,128)(2,1)S(1)} %all-to-all-done.grads_ref), channel_id=1, source_target_pairs={{0,8},{8,0},{1,9},{9,1},{2,10},{10,2},{3,11},{11,3},{4,12},{12,4},... | collective-permute-start | bytes 3833864 | tf_op jit(solution)/shard_map/ppermute | solution.py:207
  46.5 12.3 %collective-permute-start.2 = (bf16[2,832,128]{2,1,0:T(8,128)(2,1)S(1)}, bf16[2,832,128]{2,1,0:T(8,128)(2,1)S(1)}, u32[]{:S(2)}, u32[]{:S(2)}) collective-permute-start(bf16[2,832,128]{2,1,0:T(8,128)(2,1)S(1)} %collective-permute-done.1.refs_1_), channel_id=1, source_target_pairs={{0,1},{1,2},{2,3},{3,4},{4,5},{5,6},{6,7},{7,0},{8,9},{9,10},{10,1... | collective-permute-start | bytes 1277960 | tf_op jit(solution)/shard_map/ppermute | solution.py:200
  49.8 0.8 copy-start
  50.6 12.0 %collective-permute-start.5 = (bf16[2,832,128]{2,1,0:T(8,128)(2,1)}, bf16[2,832,128]{2,1,0:T(8,128)(2,1)}, u32[]{:S(2)}, u32[]{:S(2)}) collective-permute-start(bf16[2,832,128]{2,1,0:T(8,128)(2,1)} %collective-permute-done.4.refs_6_), channel_id=1, source_target_pairs={{0,7},{1,0},{2,1},{3,2},{4,3},{5,4},{6,5},{7,6},{8,15},{9,8},{10,9... | collective-permute-start | bytes 1277960 | tf_op jit(solution)/shard_map/ppermute | solution.py:201
  58.8 11.6 %collective-permute-start.3 = (bf16[2,832,128]{2,1,0:T(8,128)(2,1)S(1)}, bf16[2,832,128]{2,1,0:T(8,128)(2,1)}, u32[]{:S(2)}, u32[]{:S(2)}) collective-permute-start(bf16[2,832,128]{2,1,0:T(8,128)(2,1)S(1)} %collective-permute-done.2.refs_2_), channel_id=1, source_target_pairs={{0,1},{1,2},{2,3},{3,4},{4,5},{5,6},{6,7},{7,0},{8,9},{9,10},{10,1... | collective-permute-start | bytes 1277960 | tf_op jit(solution)/shard_map/ppermute | solution.py:200
  61.8 0.8 copy-start.2
  62.6 13.7 %collective-permute-start.6 = (bf16[2,832,128]{2,1,0:T(8,128)(2,1)}, bf16[2,832,128]{2,1,0:T(8,128)(2,1)}, u32[]{:S(2)}, u32[]{:S(2)}) collective-permute-start(bf16[2,832,128]{2,1,0:T(8,128)(2,1)} %collective-permute-done.5.refs_5_), channel_id=1, source_target_pairs={{0,7},{1,0},{2,1},{3,2},{4,3},{5,4},{6,5},{7,6},{8,15},{9,8},{10,9... | collective-permute-start | bytes 1277960 | tf_op jit(solution)/shard_map/ppermute | solution.py:201
  70.4 11.2 %collective-permute-start.8 = (bf16[2,832,128]{2,1,0:T(8,128)(2,1)}, bf16[2,832,128]{2,1,0:T(8,128)(2,1)S(1)}, u32[]{:S(2)}, u32[]{:S(2)}) collective-permute-start(bf16[2,832,128]{2,1,0:T(8,128)(2,1)} %collective-permute-done.3.refs_3_), channel_id=1, source_target_pairs={{0,1},{1,2},{2,3},{3,4},{4,5},{5,6},{6,7},{7,0},{8,9},{9,10},{10,1... | collective-permute-start | bytes 1277960 | tf_op jit(solution)/shard_map/ppermute | solution.py:202
  75.1 1.3 copy-start.1
  75.1 1.3 copy-start.3
  83.8 19.8 %collective-permute-start.9 = (f32[8,3,2,56,128]{4,3,2,1,0:T(8,128)}, f32[8,3,2,56,128]{4,3,2,1,0:T(8,128)S(1)}, u32[]{:S(2)}, u32[]{:S(2)}) collective-permute-start(f32[8,3,2,56,128]{4,3,2,1,0:T(8,128)} %get-tuple-element.8), channel_id=1, source_target_pairs={{0,16},{16,0},{1,17},{17,1},{2,18},{18,2},{3,19},{19,3},{4,20},{20... | collective-permute-start | bytes 4128776 | tf_op jit(solution)/shard_map/ppermute | solution.py:240
  85.7 17.9 %all-to-all-start.1 = ((f32[32,1,128]{2,1,0:T(1,128)}), f32[32,1,128]{2,1,0:T(1,128)S(1)}, u32[]{:S(2)}, u32[]{:S(2)}) async-start(f32[32,1,128]{2,1,0:T(1,128)} %bitcast.12), calls=%async_computation.1 | async-start | bytes 32768 | tf_op jit(solution)/shard_map/all_to_all | solution.py:239
  103.6 53.6 %copy-start.4 = (f32[104,104]{1,0:T(8,128)S(1)}, f32[104,104]{1,0:T(8,128)}, u32[]{:S(2)}) copy-start(f32[104,104]{1,0:T(8,128)} %noise_ref.1) | copy-start | bytes 129796
  103.6 53.6 %copy-start.5 = (f32[104,104]{1,0:T(8,128)S(1)}, f32[104,104]{1,0:T(8,128)}, u32[]{:S(2)}) copy-start(f32[104,104]{1,0:T(8,128)} %first_ref.1) | copy-start | bytes 129796
  103.6 53.6 %copy-start.6 = (f32[104,104]{1,0:T(8,128)S(1)}, f32[104,104]{1,0:T(8,128)}, u32[]{:S(2)}) copy-start(f32[104,104]{1,0:T(8,128)} %second_ref.1) | copy-start | bytes 129796
